TPU v7x, 32 devices: a whole 2x2x4 slice. The times are simulated.
32 devices in a mesh: day: 2 (over x), chan: 16 (over z, y, core).
Axes of the slice: x: 2, y: 2, z: 4, core: 2. Of those that a mesh axis runs over, the one named last changes fastest.
Arguments:
- records: bfloat16 [1024, 8, 3000], P(('day', 'chan')), parts along dimension 0, may hold values from -6 to 6
- live_mask: int32 [1024], P(('day', 'chan')), parts along dimension 0, may hold values 0 or 1
- offsets: int32 [16], replicated, may hold values from 1 to 511, as said below
Outputs:
- correlations: bfloat16 [1024, 16, 2048], P(('day', 'chan')), parts along dimension 0
There are 2 independent parts, one for each index of `day`. A program takes and returns all parts, laid end to end along the dimension named above; an argument that names none is the same for every part. Nothing has to cross between parts.
Inputs may be any that keep to these rules, and one draw needn't show every extreme that they name: offsets[k] lies between k * 32 + 1 and (k + 1) * 32, and the last one equals 511.
All inputs are finite; a program needn't handle non-finite values. No bound on the sum of `live_mask` on one device may be relied on, other than what follows from the above.
Results may differ from a plain program's by a relative error of at most 0.0076.
Values may be sent and summed in bfloat16 or wider, within the bound.
No kernel may reach another device: no remote copies, remote signals or barrier semaphores. Data moves between devices by JAX's collectives and lax.ppermute only.
A program may use at most 128 MiB of HBM per device.

v0:
```python
import math

import jax
import jax.numpy as jnp
from jax import lax
from jax.sharding import PartitionSpec as P

F = 512
F0 = 6
LAGS = 2048
BAND = 512


def passed_along(value, axis, by):
    length = lax.axis_size(axis)
    pairs = [(i, i + by) for i in range(length) if 0 <= i + by < length]
    return lax.ppermute(value, axis, pairs)


def forward_table(length):
    samples = jnp.arange(length, dtype=jnp.int32)
    freqs = F0 + jnp.arange(F, dtype=jnp.int32)
    phase = jnp.mod(samples[:, None] * freqs[None, :], length).astype(jnp.float32)
    angle = 2.0 * math.pi / length * phase
    return jnp.concatenate([jnp.cos(angle), -jnp.sin(angle)], axis=1).astype(jnp.bfloat16)


def inverse_table(length):
    freqs = F0 + jnp.arange(F, dtype=jnp.int32)
    shifts = jnp.arange(LAGS, dtype=jnp.int32) - LAGS // 2
    phase = jnp.mod(freqs[:, None] * shifts[None, :], length).astype(jnp.float32)
    angle = 2.0 * math.pi / length * phase
    return jnp.concatenate([jnp.cos(angle), -jnp.sin(angle)], axis=0).astype(jnp.bfloat16)


def whiten(records, live_mask):
    count, windows, length = records.shape
    table = forward_table(length)
    spectrum = jnp.dot(
        records.reshape(count * windows, length), table, preferred_element_type=jnp.float32
    )
    power = jnp.mean(spectrum * spectrum, axis=1, keepdims=True)
    gain = jnp.repeat(live_mask.astype(jnp.float32), windows)[:, None]
    white = spectrum * (gain * lax.rsqrt(power + 1e-06))
    return white.astype(jnp.bfloat16).reshape(count, windows, 2, spectrum.shape[1] // 2)


def stacked_cross(local_spec, extended, offsets):
    row_count, windows, paired, bin_count = local_spec.shape
    first = local_spec.astype(jnp.float32)

    def single(offset_value):
        partner = lax.dynamic_slice_in_dim(extended, offset_value, row_count, 0).astype(jnp.float32)
        real_part = jnp.sum(
            first[:, :, 0] * partner[:, :, 0] + first[:, :, 1] * partner[:, :, 1], axis=1
        )
        imag_part = jnp.sum(
            first[:, :, 1] * partner[:, :, 0] - first[:, :, 0] * partner[:, :, 1], axis=1
        )
        return jnp.stack([real_part, imag_part], axis=1) / float(windows)

    def grouped(group):
        return jax.vmap(single)(group)

    result = lax.map(grouped, offsets.reshape(-1, 8))
    result = result.reshape(offsets.shape[0], row_count, 2, bin_count)
    return jnp.transpose(result, (1, 0, 2, 3)).astype(jnp.bfloat16)


def lag_transform(cross, length):
    count, pairs, paired, bin_count = cross.shape
    table = inverse_table(length)
    result = jnp.dot(
        cross.reshape(count * pairs, 2 * bin_count), table, preferred_element_type=jnp.float32
    )
    result = result * (1.0 / math.sqrt(bin_count))
    return result.reshape(count, pairs, table.shape[1]).astype(jnp.bfloat16)


def shards(records, live_mask, offsets):
    count = records.shape[0]
    spectra = whiten(records, live_mask)
    reach = (BAND + count - 2) // count
    extended = jnp.zeros(((reach + 1) * count,) + spectra.shape[1:], jnp.bfloat16)
    extended = lax.dynamic_update_slice_in_dim(extended, spectra, 0, 0)

    def advance(step_index, carry):
        buffer, travelling = carry
        travelling = passed_along(travelling, "chan", -1)
        buffer = lax.dynamic_update_slice_in_dim(buffer, travelling, step_index * count, 0)
        return (buffer, travelling)

    extended, last_piece = lax.fori_loop(1, reach + 1, advance, (extended, spectra))
    cross = stacked_cross(spectra, extended, offsets)
    return lag_transform(cross, records.shape[2])


def solution(mesh):
    in_specs = (P(("day", "chan"), None, None), P(("day", "chan")), P())
    out_specs = P(("day", "chan"), None, None)
    return jax.shard_map(shards, mesh=mesh, in_specs=in_specs, out_specs=out_specs, check_vma=False)
```

profile of v0, /device:TPU:7, one launch (start us, length us, event | category | flops | bytes accessed | tf_op | source)
XLA Modules:
  0.0 317.9 jit_solution(9821043525393969551)
XLA Ops:
  0.0 26.1 %cosine_convert_fusion = (bf16[3000,512]{1,0:T(8,128)(2,1)S(1)}, bf16[3000,512]{1,0:T(8,128)(2,1)S(1)}) fusion(s32[512]{0:T(512)S(1)} %iota_add_fusion.1), kind=kLoop, calls=%fused_computation.23 | loop fusion | flops 18432000 | bytes 6146048 | tf_op jit(solution)/shard_map/convert.2
  29.0 13.7 %dynamic_update_slice.14 = bf16[544,8,2,512]{3,2,1,0:T(2,128)(2,1)} pad(bf16[32,8,2,512]{3,2,1,0:T(2,128)(2,1)S(1)} %reshape.105, bf16[]{:T(256)} %constant.84.clone.1), padding=0_512x0_0x0_0x0_0 | pad | bytes 9437186 | tf_op jit(solution)/shard_map/dynamic_update_slice | solution.py:85
  43.1 209.4 %while.25 = (s32[]{:T(128)}, bf16[544,8,2,512]{3,2,1,0:T(2,128)(2,1)}, bf16[32,8,2,512]{3,2,1,0:T(2,128)(2,1)S(1)}, s32[]{:T(128)}, s32[]{:T(128)}, /*index=5*/s32[]{:T(128)}, s32[]{:T(128)}) while((s32[]{:T(128)}, bf16[544,8,2,512]{3,2,1,0:T(2,128)(2,1)}, bf16[32,8,2,512]{3,2,1,0:T(2,128)(2,1)S(1)}, s32[]{:T(128)}, s32[]{:T(128)}, ...), condition=%wide.region_2.3_spmd, body=%wide.region_1.2_spmd.sunk | while | flops 6 | bytes 4194471 | solution.py:93
  45.7 8.8 %collective-permute-done = bf16[32,8,2,512]{3,2,1,0:T(2,128)(2,1)S(1)} collective-permute-done((bf16[32,8,2,512]{3,2,1,0:T(2,128)(2,1)S(1)}, bf16[32,8,2,512]{3,2,1,0:T(2,128)(2,1)S(1)}, u32[]{:S(2)}, u32[]{:S(2)}) %collective-permute-start) | collective-permute-done | bytes 524320 | tf_op jit(solution)/shard_map/while/body/eval_jaxpr/ppermute | solution.py:17
  58.1 9.5 %collective-permute-done = bf16[32,8,2,512]{3,2,1,0:T(2,128)(2,1)S(1)} collective-permute-done((bf16[32,8,2,512]{3,2,1,0:T(2,128)(2,1)S(1)}, bf16[32,8,2,512]{3,2,1,0:T(2,128)(2,1)S(1)}, u32[]{:S(2)}, u32[]{:S(2)}) %collective-permute-start) | collective-permute-done | bytes 524320 | tf_op jit(solution)/shard_map/while/body/eval_jaxpr/ppermute | solution.py:17
  71.2 9.5 %collective-permute-done = bf16[32,8,2,512]{3,2,1,0:T(2,128)(2,1)S(1)} collective-permute-done((bf16[32,8,2,512]{3,2,1,0:T(2,128)(2,1)S(1)}, bf16[32,8,2,512]{3,2,1,0:T(2,128)(2,1)S(1)}, u32[]{:S(2)}, u32[]{:S(2)}) %collective-permute-start) | collective-permute-done | bytes 524320 | tf_op jit(solution)/shard_map/while/body/eval_jaxpr/ppermute | solution.py:17
  84.3 9.5 %collective-permute-done = bf16[32,8,2,512]{3,2,1,0:T(2,128)(2,1)S(1)} collective-permute-done((bf16[32,8,2,512]{3,2,1,0:T(2,128)(2,1)S(1)}, bf16[32,8,2,512]{3,2,1,0:T(2,128)(2,1)S(1)}, u32[]{:S(2)}, u32[]{:S(2)}) %collective-permute-start) | collective-permute-done | bytes 524320 | tf_op jit(solution)/shard_map/while/body/eval_jaxpr/ppermute | solution.py:17
  97.4 9.5 %collective-permute-done = bf16[32,8,2,512]{3,2,1,0:T(2,128)(2,1)S(1)} collective-permute-done((bf16[32,8,2,512]{3,2,1,0:T(2,128)(2,1)S(1)}, bf16[32,8,2,512]{3,2,1,0:T(2,128)(2,1)S(1)}, u32[]{:S(2)}, u32[]{:S(2)}) %collective-permute-start) | collective-permute-done | bytes 524320 | tf_op jit(solution)/shard_map/while/body/eval_jaxpr/ppermute | solution.py:17
  110.5 9.5 %collective-permute-done = bf16[32,8,2,512]{3,2,1,0:T(2,128)(2,1)S(1)} collective-permute-done((bf16[32,8,2,512]{3,2,1,0:T(2,128)(2,1)S(1)}, bf16[32,8,2,512]{3,2,1,0:T(2,128)(2,1)S(1)}, u32[]{:S(2)}, u32[]{:S(2)}) %collective-permute-start) | collective-permute-done | bytes 524320 | tf_op jit(solution)/shard_map/while/body/eval_jaxpr/ppermute | solution.py:17
  123.6 9.5 %collective-permute-done = bf16[32,8,2,512]{3,2,1,0:T(2,128)(2,1)S(1)} collective-permute-done((bf16[32,8,2,512]{3,2,1,0:T(2,128)(2,1)S(1)}, bf16[32,8,2,512]{3,2,1,0:T(2,128)(2,1)S(1)}, u32[]{:S(2)}, u32[]{:S(2)}) %collective-permute-start) | collective-permute-done | bytes 524320 | tf_op jit(solution)/shard_map/while/body/eval_jaxpr/ppermute | solution.py:17
  136.7 9.5 %collective-permute-done = bf16[32,8,2,512]{3,2,1,0:T(2,128)(2,1)S(1)} collective-permute-done((bf16[32,8,2,512]{3,2,1,0:T(2,128)(2,1)S(1)}, bf16[32,8,2,512]{3,2,1,0:T(2,128)(2,1)S(1)}, u32[]{:S(2)}, u32[]{:S(2)}) %collective-permute-start) | collective-permute-done | bytes 524320 | tf_op jit(solution)/shard_map/while/body/eval_jaxpr/ppermute | solution.py:17
  149.8 9.5 %collective-permute-done = bf16[32,8,2,512]{3,2,1,0:T(2,128)(2,1)S(1)} collective-permute-done((bf16[32,8,2,512]{3,2,1,0:T(2,128)(2,1)S(1)}, bf16[32,8,2,512]{3,2,1,0:T(2,128)(2,1)S(1)}, u32[]{:S(2)}, u32[]{:S(2)}) %collective-permute-start) | collective-permute-done | bytes 524320 | tf_op jit(solution)/shard_map/while/body/eval_jaxpr/ppermute | solution.py:17
  162.8 9.5 %collective-permute-done = bf16[32,8,2,512]{3,2,1,0:T(2,128)(2,1)S(1)} collective-permute-done((bf16[32,8,2,512]{3,2,1,0:T(2,128)(2,1)S(1)}, bf16[32,8,2,512]{3,2,1,0:T(2,128)(2,1)S(1)}, u32[]{:S(2)}, u32[]{:S(2)}) %collective-permute-start) | collective-permute-done | bytes 524320 | tf_op jit(solution)/shard_map/while/body/eval_jaxpr/ppermute | solution.py:17
  175.9 9.5 %collective-permute-done = bf16[32,8,2,512]{3,2,1,0:T(2,128)(2,1)S(1)} collective-permute-done((bf16[32,8,2,512]{3,2,1,0:T(2,128)(2,1)S(1)}, bf16[32,8,2,512]{3,2,1,0:T(2,128)(2,1)S(1)}, u32[]{:S(2)}, u32[]{:S(2)}) %collective-permute-start) | collective-permute-done | bytes 524320 | tf_op jit(solution)/shard_map/while/body/eval_jaxpr/ppermute | solution.py:17
  189.0 9.5 %collective-permute-done = bf16[32,8,2,512]{3,2,1,0:T(2,128)(2,1)S(1)} collective-permute-done((bf16[32,8,2,512]{3,2,1,0:T(2,128)(2,1)S(1)}, bf16[32,8,2,512]{3,2,1,0:T(2,128)(2,1)S(1)}, u32[]{:S(2)}, u32[]{:S(2)}) %collective-permute-start) | collective-permute-done | bytes 524320 | tf_op jit(solution)/shard_map/while/body/eval_jaxpr/ppermute | solution.py:17
  202.1 9.5 %collective-permute-done = bf16[32,8,2,512]{3,2,1,0:T(2,128)(2,1)S(1)} collective-permute-done((bf16[32,8,2,512]{3,2,1,0:T(2,128)(2,1)S(1)}, bf16[32,8,2,512]{3,2,1,0:T(2,128)(2,1)S(1)}, u32[]{:S(2)}, u32[]{:S(2)}) %collective-permute-start) | collective-permute-done | bytes 524320 | tf_op jit(solution)/shard_map/while/body/eval_jaxpr/ppermute | solution.py:17
  215.2 9.5 %collective-permute-done = bf16[32,8,2,512]{3,2,1,0:T(2,128)(2,1)S(1)} collective-permute-done((bf16[32,8,2,512]{3,2,1,0:T(2,128)(2,1)S(1)}, bf16[32,8,2,512]{3,2,1,0:T(2,128)(2,1)S(1)}, u32[]{:S(2)}, u32[]{:S(2)}) %collective-permute-start) | collective-permute-done | bytes 524320 | tf_op jit(solution)/shard_map/while/body/eval_jaxpr/ppermute | solution.py:17
  228.3 9.5 %collective-permute-done = bf16[32,8,2,512]{3,2,1,0:T(2,128)(2,1)S(1)} collective-permute-done((bf16[32,8,2,512]{3,2,1,0:T(2,128)(2,1)S(1)}, bf16[32,8,2,512]{3,2,1,0:T(2,128)(2,1)S(1)}, u32[]{:S(2)}, u32[]{:S(2)}) %collective-permute-start) | collective-permute-done | bytes 524320 | tf_op jit(solution)/shard_map/while/body/eval_jaxpr/ppermute | solution.py:17
  241.4 9.5 %collective-permute-done = bf16[32,8,2,512]{3,2,1,0:T(2,128)(2,1)S(1)} collective-permute-done((bf16[32,8,2,512]{3,2,1,0:T(2,128)(2,1)S(1)}, bf16[32,8,2,512]{3,2,1,0:T(2,128)(2,1)S(1)}, u32[]{:S(2)}, u32[]{:S(2)}) %collective-permute-start) | collective-permute-done | bytes 524320 | tf_op jit(solution)/shard_map/while/body/eval_jaxpr/ppermute | solution.py:17
  252.6 9.8 %copy.12 = bf16[544,8,2,512]{3,1,2,0:T(8,128)(2,1)} copy(bf16[544,8,2,512]{3,2,1,0:T(2,128)(2,1)} %get-tuple-element.110) | data formatting | bytes 17825792 | tf_op jit(solution)/shard_map/while | solution.py:65
  262.6 31.2 %while.26 = (s32[]{:T(128)}, bf16[2,8,32,2,512]{4,3,2,1,0:T(2,128)(2,1)}, f32[32,8,2,512]{3,1,0,2:T(8,128)S(1)}, s32[2,8]{1,0:T(2,128)S(1)}, bf16[544,8,2,512]{3,1,2,0:T(8,128)(2,1)}, /*index=5*/s32[]{:T(128)}) while((s32[]{:T(128)}, bf16[2,8,32,2,512]{4,3,2,1,0:T(2,128)(2,1)}, f32[32,8,2,512]{3,1,0,2:T(8,128)S(1)}, s32[2,8]{1,0:T(2,128)S(1)}, ...), condition=%wide.region_6.7_spmd, body=%wide.region_3.6_spmd.sunk | while | flops 10747946 | bytes 37749512 | solution.py:65
  262.8 6.3 %gather_fusion = bf16[8,32,8,2,512]{4,2,3,1,0:T(8,128)(2,1)} fusion(bf16[544,8,2,512]{3,1,2,0:T(8,128)(2,1)} %get-tuple-element.232, s32[8]{0:T(128)S(1)} %fusion.31), kind=kCustom, calls=%fused_computation.clone.1 | custom fusion | bytes 8388736 | tf_op jit(solution)/shard_map/while/body/eval_jaxpr/vmap()/gather | solution.py:53
  278.3 6.3 %gather_fusion = bf16[8,32,8,2,512]{4,2,3,1,0:T(8,128)(2,1)} fusion(bf16[544,8,2,512]{3,1,2,0:T(8,128)(2,1)} %get-tuple-element.232, s32[8]{0:T(128)S(1)} %fusion.31), kind=kCustom, calls=%fused_computation.clone.1 | custom fusion | bytes 8388736 | tf_op jit(solution)/shard_map/while/body/eval_jaxpr/vmap()/gather | solution.py:53
  296.4 17.8 %cosine_convert_fusion.1 = (bf16[512,2048]{1,0:T(8,128)(2,1)S(1)}, bf16[512,2048]{1,0:T(8,128)(2,1)S(1)}) fusion(s32[2048]{0:T(1024)S(1)} %iota_add_fusion, s32[512]{0:T(512)S(1)} %iota_add_fusion.1), kind=kLoop, calls=%fused_computation.36 | loop fusion | flops 12582912 | bytes 4204544 | tf_op jit(solution)/shard_map/convert
  (85 shorter events, 86.4 us)
Async XLA Ops:
  0.0 26.1 %copy-start = (bf16[32,8,3000]{2,1,0:T(8,128)(2,1)S(1)}, bf16[32,8,3000]{2,1,0:T(8,128)(2,1)}, u32[]{:S(2)}) copy-start(bf16[32,8,3000]{2,1,0:T(8,128)(2,1)} %param.7) | copy-start | bytes 4608004
  26.1 2.0 copy-start.1
  43.1 11.4 %collective-permute-start = (bf16[32,8,2,512]{3,2,1,0:T(2,128)(2,1)S(1)}, bf16[32,8,2,512]{3,2,1,0:T(2,128)(2,1)S(1)}, u32[]{:S(2)}, u32[]{:S(2)}) collective-permute-start(bf16[32,8,2,512]{3,2,1,0:T(2,128)(2,1)S(1)} %get-tuple-element.204), channel_id=1, source_target_pairs={{1,0},{2,1},{3,2},{4,3},{5,4},{6,5},{7,6},{8,7},{9,8},{10,9},{11,1... | collective-permute-start | bytes 1572872 | tf_op jit(solution)/shard_map/while/body/eval_jaxpr/ppermute | solution.py:17
  56.2 11.4 %collective-permute-start = (bf16[32,8,2,512]{3,2,1,0:T(2,128)(2,1)S(1)}, bf16[32,8,2,512]{3,2,1,0:T(2,128)(2,1)S(1)}, u32[]{:S(2)}, u32[]{:S(2)}) collective-permute-start(bf16[32,8,2,512]{3,2,1,0:T(2,128)(2,1)S(1)} %get-tuple-element.204), channel_id=1, source_target_pairs={{1,0},{2,1},{3,2},{4,3},{5,4},{6,5},{7,6},{8,7},{9,8},{10,9},{11,1... | collective-permute-start | bytes 1572872 | tf_op jit(solution)/shard_map/while/body/eval_jaxpr/ppermute | solution.py:17
  69.3 11.4 %collective-permute-start = (bf16[32,8,2,512]{3,2,1,0:T(2,128)(2,1)S(1)}, bf16[32,8,2,512]{3,2,1,0:T(2,128)(2,1)S(1)}, u32[]{:S(2)}, u32[]{:S(2)}) collective-permute-start(bf16[32,8,2,512]{3,2,1,0:T(2,128)(2,1)S(1)} %get-tuple-element.204), channel_id=1, source_target_pairs={{1,0},{2,1},{3,2},{4,3},{5,4},{6,5},{7,6},{8,7},{9,8},{10,9},{11,1... | collective-permute-start | bytes 1572872 | tf_op jit(solution)/shard_map/while/body/eval_jaxpr/ppermute | solution.py:17
  82.4 11.4 %collective-permute-start = (bf16[32,8,2,512]{3,2,1,0:T(2,128)(2,1)S(1)}, bf16[32,8,2,512]{3,2,1,0:T(2,128)(2,1)S(1)}, u32[]{:S(2)}, u32[]{:S(2)}) collective-permute-start(bf16[32,8,2,512]{3,2,1,0:T(2,128)(2,1)S(1)} %get-tuple-element.204), channel_id=1, source_target_pairs={{1,0},{2,1},{3,2},{4,3},{5,4},{6,5},{7,6},{8,7},{9,8},{10,9},{11,1... | collective-permute-start | bytes 1572872 | tf_op jit(solution)/shard_map/while/body/eval_jaxpr/ppermute | solution.py:17
  95.5 11.4 %collective-permute-start = (bf16[32,8,2,512]{3,2,1,0:T(2,128)(2,1)S(1)}, bf16[32,8,2,512]{3,2,1,0:T(2,128)(2,1)S(1)}, u32[]{:S(2)}, u32[]{:S(2)}) collective-permute-start(bf16[32,8,2,512]{3,2,1,0:T(2,128)(2,1)S(1)} %get-tuple-element.204), channel_id=1, source_target_pairs={{1,0},{2,1},{3,2},{4,3},{5,4},{6,5},{7,6},{8,7},{9,8},{10,9},{11,1... | collective-permute-start | bytes 1572872 | tf_op jit(solution)/shard_map/while/body/eval_jaxpr/ppermute | solution.py:17
  108.5 11.4 %collective-permute-start = (bf16[32,8,2,512]{3,2,1,0:T(2,128)(2,1)S(1)}, bf16[32,8,2,512]{3,2,1,0:T(2,128)(2,1)S(1)}, u32[]{:S(2)}, u32[]{:S(2)}) collective-permute-start(bf16[32,8,2,512]{3,2,1,0:T(2,128)(2,1)S(1)} %get-tuple-element.204), channel_id=1, source_target_pairs={{1,0},{2,1},{3,2},{4,3},{5,4},{6,5},{7,6},{8,7},{9,8},{10,9},{11,1... | collective-permute-start | bytes 1572872 | tf_op jit(solution)/shard_map/while/body/eval_jaxpr/ppermute | solution.py:17
  121.6 11.4 %collective-permute-start = (bf16[32,8,2,512]{3,2,1,0:T(2,128)(2,1)S(1)}, bf16[32,8,2,512]{3,2,1,0:T(2,128)(2,1)S(1)}, u32[]{:S(2)}, u32[]{:S(2)}) collective-permute-start(bf16[32,8,2,512]{3,2,1,0:T(2,128)(2,1)S(1)} %get-tuple-element.204), channel_id=1, source_target_pairs={{1,0},{2,1},{3,2},{4,3},{5,4},{6,5},{7,6},{8,7},{9,8},{10,9},{11,1... | collective-permute-start | bytes 1572872 | tf_op jit(solution)/shard_map/while/body/eval_jaxpr/ppermute | solution.py:17
  134.7 11.4 %collective-permute-start = (bf16[32,8,2,512]{3,2,1,0:T(2,128)(2,1)S(1)}, bf16[32,8,2,512]{3,2,1,0:T(2,128)(2,1)S(1)}, u32[]{:S(2)}, u32[]{:S(2)}) collective-permute-start(bf16[32,8,2,512]{3,2,1,0:T(2,128)(2,1)S(1)} %get-tuple-element.204), channel_id=1, source_target_pairs={{1,0},{2,1},{3,2},{4,3},{5,4},{6,5},{7,6},{8,7},{9,8},{10,9},{11,1... | collective-permute-start | bytes 1572872 | tf_op jit(solution)/shard_map/while/body/eval_jaxpr/ppermute | solution.py:17
  147.9 11.4 %collective-permute-start = (bf16[32,8,2,512]{3,2,1,0:T(2,128)(2,1)S(1)}, bf16[32,8,2,512]{3,2,1,0:T(2,128)(2,1)S(1)}, u32[]{:S(2)}, u32[]{:S(2)}) collective-permute-start(bf16[32,8,2,512]{3,2,1,0:T(2,128)(2,1)S(1)} %get-tuple-element.204), channel_id=1, source_target_pairs={{1,0},{2,1},{3,2},{4,3},{5,4},{6,5},{7,6},{8,7},{9,8},{10,9},{11,1... | collective-permute-start | bytes 1572872 | tf_op jit(solution)/shard_map/while/body/eval_jaxpr/ppermute | solution.py:17
  160.9 11.4 %collective-permute-start = (bf16[32,8,2,512]{3,2,1,0:T(2,128)(2,1)S(1)}, bf16[32,8,2,512]{3,2,1,0:T(2,128)(2,1)S(1)}, u32[]{:S(2)}, u32[]{:S(2)}) collective-permute-start(bf16[32,8,2,512]{3,2,1,0:T(2,128)(2,1)S(1)} %get-tuple-element.204), channel_id=1, source_target_pairs={{1,0},{2,1},{3,2},{4,3},{5,4},{6,5},{7,6},{8,7},{9,8},{10,9},{11,1... | collective-permute-start | bytes 1572872 | tf_op jit(solution)/shard_map/while/body/eval_jaxpr/ppermute | solution.py:17
  174.0 11.4 %collective-permute-start = (bf16[32,8,2,512]{3,2,1,0:T(2,128)(2,1)S(1)}, bf16[32,8,2,512]{3,2,1,0:T(2,128)(2,1)S(1)}, u32[]{:S(2)}, u32[]{:S(2)}) collective-permute-start(bf16[32,8,2,512]{3,2,1,0:T(2,128)(2,1)S(1)} %get-tuple-element.204), channel_id=1, source_target_pairs={{1,0},{2,1},{3,2},{4,3},{5,4},{6,5},{7,6},{8,7},{9,8},{10,9},{11,1... | collective-permute-start | bytes 1572872 | tf_op jit(solution)/shard_map/while/body/eval_jaxpr/ppermute | solution.py:17
  187.1 11.4 %collective-permute-start = (bf16[32,8,2,512]{3,2,1,0:T(2,128)(2,1)S(1)}, bf16[32,8,2,512]{3,2,1,0:T(2,128)(2,1)S(1)}, u32[]{:S(2)}, u32[]{:S(2)}) collective-permute-start(bf16[32,8,2,512]{3,2,1,0:T(2,128)(2,1)S(1)} %get-tuple-element.204), channel_id=1, source_target_pairs={{1,0},{2,1},{3,2},{4,3},{5,4},{6,5},{7,6},{8,7},{9,8},{10,9},{11,1... | collective-permute-start | bytes 1572872 | tf_op jit(solution)/shard_map/while/body/eval_jaxpr/ppermute | solution.py:17
  200.2 11.4 %collective-permute-start = (bf16[32,8,2,512]{3,2,1,0:T(2,128)(2,1)S(1)}, bf16[32,8,2,512]{3,2,1,0:T(2,128)(2,1)S(1)}, u32[]{:S(2)}, u32[]{:S(2)}) collective-permute-start(bf16[32,8,2,512]{3,2,1,0:T(2,128)(2,1)S(1)} %get-tuple-element.204), channel_id=1, source_target_pairs={{1,0},{2,1},{3,2},{4,3},{5,4},{6,5},{7,6},{8,7},{9,8},{10,9},{11,1... | collective-permute-start | bytes 1572872 | tf_op jit(solution)/shard_map/while/body/eval_jaxpr/ppermute | solution.py:17
  213.3 11.4 %collective-permute-start = (bf16[32,8,2,512]{3,2,1,0:T(2,128)(2,1)S(1)}, bf16[32,8,2,512]{3,2,1,0:T(2,128)(2,1)S(1)}, u32[]{:S(2)}, u32[]{:S(2)}) collective-permute-start(bf16[32,8,2,512]{3,2,1,0:T(2,128)(2,1)S(1)} %get-tuple-element.204), channel_id=1, source_target_pairs={{1,0},{2,1},{3,2},{4,3},{5,4},{6,5},{7,6},{8,7},{9,8},{10,9},{11,1... | collective-permute-start | bytes 1572872 | tf_op jit(solution)/shard_map/while/body/eval_jaxpr/ppermute | solution.py:17
  226.4 11.4 %collective-permute-start = (bf16[32,8,2,512]{3,2,1,0:T(2,128)(2,1)S(1)}, bf16[32,8,2,512]{3,2,1,0:T(2,128)(2,1)S(1)}, u32[]{:S(2)}, u32[]{:S(2)}) collective-permute-start(bf16[32,8,2,512]{3,2,1,0:T(2,128)(2,1)S(1)} %get-tuple-element.204), channel_id=1, source_target_pairs={{1,0},{2,1},{3,2},{4,3},{5,4},{6,5},{7,6},{8,7},{9,8},{10,9},{11,1... | collective-permute-start | bytes 1572872 | tf_op jit(solution)/shard_map/while/body/eval_jaxpr/ppermute | solution.py:17
  239.5 11.4 %collective-permute-start = (bf16[32,8,2,512]{3,2,1,0:T(2,128)(2,1)S(1)}, bf16[32,8,2,512]{3,2,1,0:T(2,128)(2,1)S(1)}, u32[]{:S(2)}, u32[]{:S(2)}) collective-permute-start(bf16[32,8,2,512]{3,2,1,0:T(2,128)(2,1)S(1)} %get-tuple-element.204), channel_id=1, source_target_pairs={{1,0},{2,1},{3,2},{4,3},{5,4},{6,5},{7,6},{8,7},{9,8},{10,9},{11,1... | collective-permute-start | bytes 1572872 | tf_op jit(solution)/shard_map/while/body/eval_jaxpr/ppermute | solution.py:17
  252.5 10.0 %copy-start.2 = (s32[16]{0:T(128)S(1)}, s32[16]{0:T(128)}, u32[]{:S(2)}) copy-start(s32[16]{0:T(128)} %param.9) | copy-start | bytes 196
where the time goes:
time: 319 us; the launch traced here: 318 us
  waiting for transfers between devices  151 us (47%)
  local copies, waits for them, and re-layouts  68.8 us (22%)
  other arithmetic  60.8 us (19%)
  starting transfers between devices  31.2 us (10%)
  matrix products  5.65 us (2%)
    ppermute x16, waiting for transfers between devices, passed_along(): return lax.ppermute(value, axis, pairs)  151 us
    another operation x2, other arithmetic  43.9 us
    ppermute x16, starting transfers between devices, passed_along(): return lax.ppermute(value, axis, pairs)  31.2 us
    dynamic_update_slice x16, local copies, waits for them, and re-layouts, advance(): lax.dynamic_update_slice_in_dim(buffer, travelling, step_index * count, 0)  20.2 us
    dynamic_update_slice x1, local copies, waits for them, and re-layouts, shards(): extended = lax.dynamic_update_slice_in_dim(extended, spectra, 0, 0)  13.7 us
    gather x2, local copies, waits for them, and re-layouts, single(): lax.dynamic_slice_in_dim(extended, offset_value, row_count, 0)  12.7 us
    while x2, local copies, waits for them, and re-layouts, stacked_cross(): result = lax.map(grouped, offsets.reshape(-1, 8))  9.96 us
    while x16, local copies, waits for them, and re-layouts  6.93 us
  transfers between devices with their start and end apart: 16, of which 16 were waited for; matrix products, arithmetic and copies ran while one was open for 0% of the time, Pallas kernels for 0%

commit v1 on v0

v1 whole, which is shorter than its diff:
```python
import functools
import math

import jax
import jax.numpy as jnp
import ml_dtypes
import numpy as np
from jax import lax
from jax.experimental import pallas as pl
from jax.experimental.pallas import tpu as pltpu
from jax.sharding import PartitionSpec as P

F = 512
F0 = 6
LAGS = 2048
BAND = 512
TEAM = 4
HALVES = 2
LANES = 128
BINS = F // (TEAM * HALVES)
VMEM = 56 * 1024 * 1024


def column_order():
    bins = np.arange(F).reshape(TEAM, HALVES, 1, BINS)
    parts = np.arange(2).reshape(1, 1, 2, 1) * F
    return (bins + parts).reshape(-1)


def tables(length):
    freqs = F0 + np.arange(F, dtype=np.int64)
    unit = np.float32(2.0 * math.pi / length)

    def cut(phase):
        angle = unit * np.mod(phase, length).astype(np.float32)
        return np.cos(angle), -np.sin(angle)

    order = column_order()
    forward = np.concatenate(cut(np.arange(length)[:, None] * freqs[None, :]), axis=1)[:, order]
    forward = forward.reshape(length, TEAM, 2 * F // TEAM).transpose(1, 0, 2)
    shifts = np.arange(LAGS, dtype=np.int64) - LAGS // 2
    inverse = np.concatenate(cut(freqs[:, None] * shifts[None, :]), axis=0)[order]
    inverse = inverse.reshape(TEAM, 2 * F // TEAM, LAGS)
    return forward.astype(ml_dtypes.bfloat16), inverse.astype(ml_dtypes.bfloat16)


def spectra_kernel(windows, records, table, live, own0, own1, far0, far1, spec, power):
    step = pl.program_id(0)
    rows = records.shape[0]
    count = rows // windows
    block = jnp.dot(records[...], table[0], preferred_element_type=jnp.float32)
    for half in range(HALVES):
        spec[step * HALVES + half] = block[:, half * LANES : (half + 1) * LANES]
    squares = jnp.sum(block * block, axis=1, keepdims=True)
    total = jnp.where(step == 0, 0.0, power[...]) + squares
    power[...] = total

    @pl.when(step == TEAM - 1)
    def _():
        me = lax.rem(lax.axis_index("chan"), TEAM)
        channel = lax.broadcasted_iota(jnp.int32, (rows, count), 0) // windows
        lane = lax.broadcasted_iota(jnp.int32, (rows, count), 1)
        mask = jnp.where(channel == lane, live[...].astype(jnp.float32), 0.0)
        gain = jnp.sum(mask, axis=1, keepdims=True)
        scale = gain * lax.rsqrt(total * (1.0 / (2 * F)) + 1e-06)
        for part in range(TEAM * HALVES):
            spec[part] = spec[part] * scale
        for d in range(TEAM):
            quarter = jnp.bitwise_xor(me, d)
            for half, out in enumerate((own0, own1) if d < 2 else (far0, far1)):
                for w in range(windows):
                    piece = spec[quarter * HALVES + half, pl.ds(w, count, stride=windows), :]
                    out[d % 2, w * count : (w + 1) * count, :] = piece.astype(jnp.bfloat16)


def spectra(records, live_mask, table):
    count, windows, length = records.shape
    rows = count * windows
    width = 2 * F // TEAM
    piece = jax.ShapeDtypeStruct((2, rows, LANES), jnp.bfloat16)
    whole = pl.BlockSpec((2, rows, LANES), lambda i: (0, 0, 0))
    return pl.pallas_call(
        functools.partial(spectra_kernel, windows),
        grid=(TEAM,),
        in_specs=[
            pl.BlockSpec((rows, length), lambda i: (0, 0)),
            pl.BlockSpec((1, length, width), lambda i: (i, 0, 0)),
            pl.BlockSpec((1, count), lambda i: (0, 0)),
        ],
        out_specs=[whole] * 4,
        out_shape=[piece] * 4,
        scratch_shapes=[
            pltpu.VMEM((TEAM * HALVES, rows, LANES), jnp.float32),
            pltpu.VMEM((rows, 1), jnp.float32),
        ],
        compiler_params=pltpu.CompilerParams(vmem_limit_bytes=VMEM),
        name="spectra",
    )(records.reshape(rows, length), table, live_mask.reshape(1, count))


def cross_kernel(windows, count, first, last, low, planes, offsets, *refs):
    given, (near, far, side, extended, paired) = refs[: 4 * (planes + 1)], refs[4 * (planes + 1) :]
    me = lax.rem(lax.axis_index("chan"), TEAM)
    span = TEAM * count
    number = last - first
    blocks = [jnp.bitwise_xor(me, d) for d in range(TEAM)]

    def pieces(plane):
        own, own_swapped, across, across_swapped = given[4 * plane : 4 * plane + 4]
        return (own, own_swapped, across, across_swapped)

    for d, ref in enumerate(pieces(0)):
        for w in range(windows):
            side[w, d * count : (d + 1) * count, :] = ref[0, w * count : (w + 1) * count, :].astype(jnp.float32)
    for plane in range(planes):
        for d, ref in enumerate(pieces(plane + 1)):
            start = pl.multiple_of(plane * span + blocks[d] * count, count)
            for w in range(windows):
                extended[w, pl.ds(start, count), :] = ref[0, w * count : (w + 1) * count, :].astype(jnp.float32)
    tail = extended.shape[1] - planes * span
    if tail:
        extended[:, planes * span :, :] = jnp.zeros((windows, tail, LANES), jnp.float32)

    lane = lax.broadcasted_iota(jnp.int32, (8, LANES), 1)
    real_lane = lane < BINS
    sign = jnp.where(real_lane, 1.0 / windows, -1.0 / windows)

    def group(step, carry):
        at = pl.multiple_of(step * 8, 8)
        d = step // (count // 8)
        within = lax.rem(step, count // 8) * 8
        channel = jnp.bitwise_xor(me, d) * count + within
        straight, turned = [], []
        for w in range(windows):
            value = side[w, pl.ds(at, 8), :]
            straight.append(value * (1.0 / windows))
            turned.append(pltpu.roll(value, BINS, 1) * sign)
        for j in range(number):
            place = channel + offsets[first + j] - low * span
            real_part, imag_part = None, None
            for w in range(windows):
                partner = extended[w, pl.ds(place, 8), :]
                r, i = straight[w] * partner, turned[w] * partner
                real_part = r if w == 0 else real_part + r
                imag_part = i if w == 0 else imag_part + i
            real_part = real_part + pltpu.roll(real_part, BINS, 1)
            imag_part = imag_part + pltpu.roll(imag_part, BINS, 1)
            both = jnp.where(real_lane, real_part, imag_part)
            paired[d, pl.ds(within * number + j, 8, stride=number), :] = both
        return carry

    lax.fori_loop(0, span // 8, group, 0)
    for d in range(TEAM):
        (near if d < 2 else far)[d % 2] = paired[d].astype(jnp.bfloat16)


def cross(windows, count, first, last, offsets, team_planes):
    span = TEAM * count
    stride = BAND // offsets.shape[0]
    low = (first * stride + 1) // span
    high = (span - 1 + last * stride) // span
    partners = [team_planes[p] for p in range(low, min(high, len(team_planes) - 1) + 1)]
    rows = windows * count
    halves = [0, 1, 0, 1] * (len(partners) + 1)
    number = last - first
    out = jax.ShapeDtypeStruct((2, count * number, LANES), jnp.bfloat16)
    return pl.pallas_call(
        functools.partial(cross_kernel, windows, count, first, last, low, len(partners)),
        grid=(1,),
        in_specs=[pl.BlockSpec(memory_space=pltpu.SMEM)]
        + [pl.BlockSpec((1, rows, LANES), lambda i, h=h: (h, 0, 0)) for h in halves],
        out_specs=[pl.BlockSpec((2, count * number, LANES), lambda i: (0, 0, 0))] * 2,
        out_shape=[out] * 2,
        scratch_shapes=[
            pltpu.VMEM((windows, span, LANES), jnp.float32),
            pltpu.VMEM((windows, (high - low + 1) * span, LANES), jnp.float32),
            pltpu.VMEM((TEAM, count * number, LANES), jnp.float32),
        ],
        compiler_params=pltpu.CompilerParams(vmem_limit_bytes=VMEM),
        name="cross",
    )(offsets, *[piece for plane in [team_planes[0]] + partners for piece in plane])


def lag_kernel(count, groups, *refs):
    given, table, out = refs[:-2], refs[-2], refs[-1]
    me = lax.rem(lax.axis_index("chan"), TEAM)
    columns = []
    for g in range(groups):
        total = None
        for d in range(TEAM):
            quarter = jnp.bitwise_xor(me, d)
            left = jnp.concatenate([given[(g * HALVES + h) * TEAM + d][0] for h in range(HALVES)], axis=1)
            term = jnp.dot(left, table[quarter], preferred_element_type=jnp.float32)
            total = term if d == 0 else total + term
        columns.append(total.reshape(count, total.shape[0] // count, total.shape[1]))
    result = jnp.concatenate(columns, axis=1) * (1.0 / math.sqrt(F))
    out[...] = result.astype(jnp.bfloat16)


def lags(count, number, parts, table):
    tile = 512
    arrays = [piece for group in parts for half in group for piece in half]
    halves = [0, 1, 0, 1] * (len(arrays) // 4)
    return pl.pallas_call(
        functools.partial(lag_kernel, count, len(parts)),
        grid=(LAGS // tile,),
        in_specs=[
            pl.BlockSpec((1,) + a.shape[1:], lambda i, h=h: (h, 0, 0)) for a, h in zip(arrays, halves)
        ]
        + [pl.BlockSpec((TEAM, table.shape[1], tile), lambda i: (0, 0, i))],
        out_specs=pl.BlockSpec((count, number, tile), lambda i: (0, 0, i)),
        out_shape=jax.ShapeDtypeStruct((count, number, LAGS), jnp.bfloat16),
        compiler_params=pltpu.CompilerParams(vmem_limit_bytes=VMEM),
        name="lags",
    )(*arrays, table)


def solution(mesh):
    ring = mesh.shape["chan"]
    if ring % TEAM:
        raise ValueError("chan")

    def swapped(value, by):
        return lax.ppermute(value, "chan", [(i, i ^ by) for i in range(ring)])

    def down(value, hops):
        pairs = [(i, i - TEAM) for i in range(TEAM, ring) if i // TEAM + hops - 1 < ring // TEAM]
        return lax.ppermute(value, "chan", pairs)

    def shards(records, live_mask, offsets):
        count, windows, length = records.shape
        span = TEAM * count
        number = offsets.shape[0]
        forward, inverse = tables(length)
        own0, own1, far0, far1 = spectra(records, live_mask, jnp.asarray(forward))
        across0, across1 = swapped(far0, 2), swapped(far1, 2)
        reach = min((span + BAND - 2) // span, ring // TEAM - 1)
        chunks = [[[own0, across0], [own1, across1]]]
        for hops in range(1, reach + 1):
            previous = chunks[-1]
            chunks.append([[down(c, hops) for c in half] for half in previous])
        planes = [
            [[piece for c in half for piece in (c, swapped(c, 1))] for half in chunk] for chunk in chunks
        ]
        parts = []
        for first, last in ((0, number // 2), (number // 2, number)):
            group = []
            for half in range(HALVES):
                near, far = cross(windows, count, first, last, offsets, [p[half] for p in planes])
                back = swapped(far, 2)
                group.append([near, swapped(near, 1), back, swapped(back, 1)])
            parts.append(group)
        return lags(count, number, parts, jnp.asarray(inverse))

    in_specs = (P(("day", "chan"), None, None), P(("day", "chan")), P())
    out_specs = P(("day", "chan"), None, None)
    return jax.shard_map(shards, mesh=mesh, in_specs=in_specs, out_specs=out_specs, check_vma=False)
```

time: 319 us -> 87.1 us (0.27)
  the two profiles are of different devices: /device:TPU:7 before, /device:TPU:0 now
where the time goes in v1:
time: 87.1 us; the launch traced here: 86.3 us
  Pallas kernels  31.4 us (36%)
  waiting for transfers between devices  27.4 us (31%)
  starting transfers between devices  25.9 us (30%)
  local copies, waits for them, and re-layouts  1.02 us (1%)
    pallas_call x4, Pallas kernels, cross(): pl.pallas_call(functools.partial(cross_kernel, windows, count, first, las...  18.8 us
    ppermute x12, waiting for transfers between devices, down(): return lax.ppermute(value, 'chan', pairs)  18.2 us
    ppermute x12, starting transfers between devices, down(): return lax.ppermute(value, 'chan', pairs)  15.5 us
    ppermute x30, starting transfers between devices, swapped(): return lax.ppermute(value, 'chan', [(i, i ^ by) for i in range(ring)])  10.4 us
    ppermute x30, waiting for transfers between devices, swapped(): return lax.ppermute(value, 'chan', [(i, i ^ by) for i in range(ring)])  9.15 us
    pallas_call x1, Pallas kernels, spectra(): pl.pallas_call(functools.partial(spectra_kernel, windows), grid=(TEAM,),...  6.57 us
    pallas_call x1, Pallas kernels, lags(): pl.pallas_call(functools.partial(lag_kernel, count, len(parts)), grid=(LA...  6.03 us
  transfers between devices with their start and end apart: 42, of which 15 were waited for; matrix products, arithmetic and copies ran while one was open for 0% of the time, Pallas kernels for 22%

profile of v1, /device:TPU:0, one launch (start us, length us, event | category | flops | bytes accessed | tf_op | source)
XLA Modules:
  0.0 86.3 jit_solution(8877893874373192092)
XLA Ops:
  0.0 6.6 %spectra.1 = (bf16[2,256,128]{2,1,0:T(8,128)(2,1)}, bf16[2,256,128]{2,1,0:T(8,128)(2,1)}, bf16[2,256,128]{2,1,0:T(8,128)(2,1)}, bf16[2,256,128]{2,1,0:T(8,128)(2,1)}) custom-call(bf16[256,3000]{1,0:T(8,128)(2,1)} %bitcast.2, bf16[4,3000,256]{2,1,0:T(8,128)(2,1)} %constant.4.clone.table, s32[1,32]{1,0:T(1,128)} %bitcast.3), custom_call_target="tpu_custom_call" | custom-call | tf_op jit(solution)/shard_map/spectra/pallas_call | solution.py:82
  6.6 3.0 %collective-permute-start.1 = (bf16[2,256,128]{2,1,0:T(8,128)(2,1)}, bf16[2,256,128]{2,1,0:T(8,128)(2,1)S(1)}, u32[]{:S(2)}, u32[]{:S(2)}) collective-permute-start(bf16[2,256,128]{2,1,0:T(8,128)(2,1)} %get-tuple-element.18), channel_id=1, source_target_pairs={{0,2},{1,3},{2,0},{3,1},{4,6},{5,7},{6,4},{7,5},{8,10},{9,11},{10,... | collective-permute-start | bytes 393224 | tf_op jit(solution)/shard_map/ppermute | solution.py:224
  10.9 1.3 %collective-permute-start.17 = (bf16[2,256,128]{2,1,0:T(8,128)(2,1)}, bf16[2,256,128]{2,1,0:T(8,128)(2,1)S(1)}, u32[]{:S(2)}, u32[]{:S(2)}) collective-permute-start(bf16[2,256,128]{2,1,0:T(8,128)(2,1)} %get-tuple-element.21.refs_0_.refs_4_), channel_id=1, source_target_pairs={{4,0},{5,1},{6,2},{7,3},{8,4},{9,5},{10,6},{11,7},{12,8},{13,9},{1... | collective-permute-start | bytes 393224 | tf_op jit(solution)/shard_map/ppermute | solution.py:228
  12.2 1.8 %collective-permute-done.1.refs_2_.refs_6_ = bf16[2,256,128]{2,1,0:T(8,128)(2,1)S(1)} collective-permute-done((bf16[2,256,128]{2,1,0:T(8,128)(2,1)}, bf16[2,256,128]{2,1,0:T(8,128)(2,1)S(1)}, u32[]{:S(2)}, u32[]{:S(2)}) %collective-permute-start.1) | collective-permute-done | bytes 131104 | tf_op jit(solution)/shard_map/ppermute | solution.py:224
  14.1 2.0 %collective-permute-done.15.refs_2_.refs_6_ = bf16[2,256,128]{2,1,0:T(8,128)(2,1)S(1)} collective-permute-done((bf16[2,256,128]{2,1,0:T(8,128)(2,1)}, bf16[2,256,128]{2,1,0:T(8,128)(2,1)S(1)}, u32[]{:S(2)}, u32[]{:S(2)}) %collective-permute-start.15) | collective-permute-done | bytes 131104 | tf_op jit(solution)/shard_map/ppermute | solution.py:224
  17.5 1.3 %collective-permute-start.19 = (bf16[2,256,128]{2,1,0:T(8,128)(2,1)S(1)}, bf16[2,256,128]{2,1,0:T(8,128)(2,1)S(1)}, u32[]{:S(2)}, u32[]{:S(2)}) collective-permute-start(bf16[2,256,128]{2,1,0:T(8,128)(2,1)S(1)} %collective-permute-done.15.refs_2_.refs_6_), channel_id=1, source_target_pairs={{4,0},{5,1},{6,2},{7,3},{8,4},{9,5},{10,6},{11,7},{12,8},{13,9},{1... | collective-permute-start | bytes 393224 | tf_op jit(solution)/shard_map/ppermute | solution.py:228
  21.2 1.7 %collective-permute-done.5.refs_10_ = bf16[2,256,128]{2,1,0:T(8,128)(2,1)S(1)} collective-permute-done((bf16[2,256,128]{2,1,0:T(8,128)(2,1)S(1)}, bf16[2,256,128]{2,1,0:T(8,128)(2,1)S(1)}, u32[]{:S(2)}, u32[]{:S(2)}) %collective-permute-start.5) | collective-permute-done | bytes 131104 | tf_op jit(solution)/shard_map/ppermute | solution.py:228
  24.2 2.1 %collective-permute-done.19.refs_10_ = bf16[2,256,128]{2,1,0:T(8,128)(2,1)S(1)} collective-permute-done((bf16[2,256,128]{2,1,0:T(8,128)(2,1)S(1)}, bf16[2,256,128]{2,1,0:T(8,128)(2,1)S(1)}, u32[]{:S(2)}, u32[]{:S(2)}) %collective-permute-start.19) | collective-permute-done | bytes 131104 | tf_op jit(solution)/shard_map/ppermute | solution.py:228
  27.7 1.5 %collective-permute-done.7.refs_12_.refs_4_ = bf16[2,256,128]{2,1,0:T(8,128)(2,1)S(1)} collective-permute-done((bf16[2,256,128]{2,1,0:T(8,128)(2,1)S(1)}, bf16[2,256,128]{2,1,0:T(8,128)(2,1)S(1)}, u32[]{:S(2)}, u32[]{:S(2)}) %collective-permute-start.7) | collective-permute-done | bytes 131104 | tf_op jit(solution)/shard_map/ppermute | solution.py:228
  30.5 1.4 %collective-permute-done.21.refs_12_.refs_4_ = bf16[2,256,128]{2,1,0:T(8,128)(2,1)S(1)} collective-permute-done((bf16[2,256,128]{2,1,0:T(8,128)(2,1)S(1)}, bf16[2,256,128]{2,1,0:T(8,128)(2,1)S(1)}, u32[]{:S(2)}, u32[]{:S(2)}) %collective-permute-start.21) | collective-permute-done | bytes 131104 | tf_op jit(solution)/shard_map/ppermute | solution.py:228
  33.2 1.5 %collective-permute-done.9.refs_14_.refs_6_ = bf16[2,256,128]{2,1,0:T(8,128)(2,1)S(1)} collective-permute-done((bf16[2,256,128]{2,1,0:T(8,128)(2,1)S(1)}, bf16[2,256,128]{2,1,0:T(8,128)(2,1)S(1)}, u32[]{:S(2)}, u32[]{:S(2)}) %collective-permute-start.9) | collective-permute-done | bytes 131104 | tf_op jit(solution)/shard_map/ppermute | solution.py:228
  36.0 1.5 %collective-permute-done.23.refs_14_.refs_6_ = bf16[2,256,128]{2,1,0:T(8,128)(2,1)S(1)} collective-permute-done((bf16[2,256,128]{2,1,0:T(8,128)(2,1)S(1)}, bf16[2,256,128]{2,1,0:T(8,128)(2,1)S(1)}, u32[]{:S(2)}, u32[]{:S(2)}) %collective-permute-start.23) | collective-permute-done | bytes 131104 | tf_op jit(solution)/shard_map/ppermute | solution.py:228
  38.8 1.5 %collective-permute-done.28.refs_8_ = bf16[2,256,128]{2,1,0:T(8,128)(2,1)S(1)} collective-permute-done((bf16[2,256,128]{2,1,0:T(8,128)(2,1)S(1)}, bf16[2,256,128]{2,1,0:T(8,128)(2,1)S(1)}, u32[]{:S(2)}, u32[]{:S(2)}) %collective-permute-start.28) | collective-permute-done | bytes 131104 | tf_op jit(solution)/shard_map/ppermute | solution.py:228
  40.3 1.3 %collective-permute-start.37 = (bf16[2,256,128]{2,1,0:T(8,128)(2,1)S(1)}, bf16[2,256,128]{2,1,0:T(8,128)(2,1)S(1)}, u32[]{:S(2)}, u32[]{:S(2)}) collective-permute-start(bf16[2,256,128]{2,1,0:T(8,128)(2,1)S(1)} %collective-permute-done.23.refs_14_.refs_6_), channel_id=1, source_target_pairs={{4,0},{5,1},{6,2},{7,3},{20,16},{21,17},{22,18},{23,19}} | collective-permute-start | bytes 393224 | tf_op jit(solution)/shard_map/ppermute | solution.py:228
  41.6 1.5 %collective-permute-done.35.refs_8_ = bf16[2,256,128]{2,1,0:T(8,128)(2,1)S(1)} collective-permute-done((bf16[2,256,128]{2,1,0:T(8,128)(2,1)S(1)}, bf16[2,256,128]{2,1,0:T(8,128)(2,1)S(1)}, u32[]{:S(2)}, u32[]{:S(2)}) %collective-permute-start.35) | collective-permute-done | bytes 131104 | tf_op jit(solution)/shard_map/ppermute | solution.py:228
  43.6 2.3 %collective-permute-done.30.refs_10_ = bf16[2,256,128]{2,1,0:T(8,128)(2,1)S(1)} collective-permute-done((bf16[2,256,128]{2,1,0:T(8,128)(2,1)S(1)}, bf16[2,256,128]{2,1,0:T(8,128)(2,1)S(1)}, u32[]{:S(2)}, u32[]{:S(2)}) %collective-permute-start.30) | collective-permute-done | bytes 131104 | tf_op jit(solution)/shard_map/ppermute | solution.py:228
  46.5 2.2 %collective-permute-done.37.refs_10_ = bf16[2,256,128]{2,1,0:T(8,128)(2,1)S(1)} collective-permute-done((bf16[2,256,128]{2,1,0:T(8,128)(2,1)S(1)}, bf16[2,256,128]{2,1,0:T(8,128)(2,1)S(1)}, u32[]{:S(2)}, u32[]{:S(2)}) %collective-permute-start.37) | collective-permute-done | bytes 131104 | tf_op jit(solution)/shard_map/ppermute | solution.py:228
  48.7 4.7 %cross.4 = (bf16[2,256,128]{2,1,0:T(8,128)(2,1)}, bf16[2,256,128]{2,1,0:T(8,128)(2,1)}) custom-call(s32[16]{0:T(128)} %offsets.7, bf16[2,256,128]{2,1,0:T(8,128)(2,1)} %get-tuple-element.17.refs_0_.refs_4_, bf16[2,256,128]{2,1,0:T(8,128)(2,1)} %copy-done.3, bf16[2,256,128]{2,1,0:T(8,128)(2,1)} %copy-done.2, bf16[2,256,128]{2,1,0:T(8,128)(2,1)} %copy-done.5, ...), custom_call_target="tpu_custom_call" | custom-call | tf_op jit(solution)/shard_map/cross/pallas_call | solution.py:167
  53.5 1.8 %collective-permute-start.12 = (bf16[2,256,128]{2,1,0:T(8,128)(2,1)}, bf16[2,256,128]{2,1,0:T(8,128)(2,1)S(1)}, u32[]{:S(2)}, u32[]{:S(2)}) collective-permute-start(bf16[2,256,128]{2,1,0:T(8,128)(2,1)} %get-tuple-element.20), channel_id=1, source_target_pairs={{0,2},{1,3},{2,0},{3,1},{4,6},{5,7},{6,4},{7,5},{8,10},{9,11},{10,... | collective-permute-start | bytes 393224 | tf_op jit(solution)/shard_map/ppermute | solution.py:224
  55.6 4.8 %cross.5 = (bf16[2,256,128]{2,1,0:T(8,128)(2,1)}, bf16[2,256,128]{2,1,0:T(8,128)(2,1)}) custom-call(s32[16]{0:T(128)} %offsets.7, bf16[2,256,128]{2,1,0:T(8,128)(2,1)} %get-tuple-element.21.refs_0_.refs_4_, bf16[2,256,128]{2,1,0:T(8,128)(2,1)} %copy-done.1, bf16[2,256,128]{2,1,0:T(8,128)(2,1)} %copy-done, bf16[2,256,128]{2,1,0:T(8,128)(2,1)} %copy-done.4, ...), custom_call_target="tpu_custom_call" | custom-call | tf_op jit(solution)/shard_map/cross/pallas_call | solution.py:167
  61.0 4.7 %cross.6 = (bf16[2,256,128]{2,1,0:T(8,128)(2,1)}, bf16[2,256,128]{2,1,0:T(8,128)(2,1)}) custom-call(s32[16]{0:T(128)} %offsets.7, bf16[2,256,128]{2,1,0:T(8,128)(2,1)} %get-tuple-element.17.refs_0_.refs_4_, bf16[2,256,128]{2,1,0:T(8,128)(2,1)} %copy-done.3, bf16[2,256,128]{2,1,0:T(8,128)(2,1)} %copy-done.2, bf16[2,256,128]{2,1,0:T(8,128)(2,1)} %copy-done.5, ...), custom_call_target="tpu_custom_call" | custom-call | tf_op jit(solution)/shard_map/cross/pallas_call | solution.py:167
  67.3 4.7 %cross.7 = (bf16[2,256,128]{2,1,0:T(8,128)(2,1)}, bf16[2,256,128]{2,1,0:T(8,128)(2,1)}) custom-call(s32[16]{0:T(128)} %offsets.7, bf16[2,256,128]{2,1,0:T(8,128)(2,1)} %get-tuple-element.21.refs_0_.refs_4_, bf16[2,256,128]{2,1,0:T(8,128)(2,1)} %copy-done.1, bf16[2,256,128]{2,1,0:T(8,128)(2,1)} %copy-done, bf16[2,256,128]{2,1,0:T(8,128)(2,1)} %copy-done.4, ...), custom_call_target="tpu_custom_call" | custom-call | tf_op jit(solution)/shard_map/cross/pallas_call | solution.py:167
  74.2 4.0 %collective-permute-done.40.refs_14_ = bf16[2,256,128]{2,1,0:T(8,128)(2,1)S(1)} collective-permute-done((bf16[2,256,128]{2,1,0:T(8,128)(2,1)}, bf16[2,256,128]{2,1,0:T(8,128)(2,1)S(1)}, u32[]{:S(2)}, u32[]{:S(2)}) %collective-permute-start.40) | collective-permute-done | bytes 131104 | tf_op jit(solution)/shard_map/ppermute | solution.py:224
  80.3 6.0 %lags.1 = bf16[32,16,2048]{2,1,0:T(8,128)(2,1)} custom-call(bf16[2,256,128]{2,1,0:T(8,128)(2,1)} %get-tuple-element.19.refs_0_, bf16[2,256,128]{2,1,0:T(8,128)(2,1)} %copy-done.15, bf16[2,256,128]{2,1,0:T(8,128)(2,1)} %copy-done.14, bf16[2,256,128]{2,1,0:T(8,128)(2,1)} %copy-done.22, bf16[2,256,128]{2,1,0:T(8,128)(2,1)} %get-tuple-element.23.refs_4_, ...), custom_call_target="tpu_custom_call" | custom-call | tf_op jit(solution)/shard_map/lags/pallas_call | solution.py:204
  (150 shorter events, 20.7 us)
Async XLA Ops:
  6.6 7.5 %collective-permute-start.1 = (bf16[2,256,128]{2,1,0:T(8,128)(2,1)}, bf16[2,256,128]{2,1,0:T(8,128)(2,1)S(1)}, u32[]{:S(2)}, u32[]{:S(2)}) collective-permute-start(bf16[2,256,128]{2,1,0:T(8,128)(2,1)} %get-tuple-element.18), channel_id=1, source_target_pairs={{0,2},{1,3},{2,0},{3,1},{4,6},{5,7},{6,4},{7,5},{8,10},{9,11},{10,... | collective-permute-start | bytes 393224 | tf_op jit(solution)/shard_map/ppermute | solution.py:224
  9.6 7.8 %collective-permute-start.3 = (bf16[2,256,128]{2,1,0:T(8,128)(2,1)}, bf16[2,256,128]{2,1,0:T(8,128)(2,1)S(1)}, u32[]{:S(2)}, u32[]{:S(2)}) collective-permute-start(bf16[2,256,128]{2,1,0:T(8,128)(2,1)} %get-tuple-element.17.refs_0_.refs_4_), channel_id=1, source_target_pairs={{4,0},{5,1},{6,2},{7,3},{8,4},{9,5},{10,6},{11,7},{12,8},{13,9},{1... | collective-permute-start | bytes 393224 | tf_op jit(solution)/shard_map/ppermute | solution.py:228
  10.9 6.6 %collective-permute-start = (bf16[2,256,128]{2,1,0:T(8,128)(2,1)}, bf16[2,256,128]{2,1,0:T(8,128)(2,1)S(1)}, u32[]{:S(2)}, u32[]{:S(2)}) collective-permute-start(bf16[2,256,128]{2,1,0:T(8,128)(2,1)} %get-tuple-element.17.refs_0_.refs_4_), channel_id=1, source_target_pairs={{0,1},{1,0},{2,3},{3,2},{4,5},{5,4},{6,7},{7,6},{8,9},{9,8},{10,11... | collective-permute-start | bytes 393224 | tf_op jit(solution)/shard_map/ppermute | solution.py:224
  10.9 8.9 %collective-permute-start.17 = (bf16[2,256,128]{2,1,0:T(8,128)(2,1)}, bf16[2,256,128]{2,1,0:T(8,128)(2,1)S(1)}, u32[]{:S(2)}, u32[]{:S(2)}) collective-permute-start(bf16[2,256,128]{2,1,0:T(8,128)(2,1)} %get-tuple-element.21.refs_0_.refs_4_), channel_id=1, source_target_pairs={{4,0},{5,1},{6,2},{7,3},{8,4},{9,5},{10,6},{11,7},{12,8},{13,9},{1... | collective-permute-start | bytes 393224 | tf_op jit(solution)/shard_map/ppermute | solution.py:228
  16.0 6.8 %collective-permute-start.5 = (bf16[2,256,128]{2,1,0:T(8,128)(2,1)S(1)}, bf16[2,256,128]{2,1,0:T(8,128)(2,1)S(1)}, u32[]{:S(2)}, u32[]{:S(2)}) collective-permute-start(bf16[2,256,128]{2,1,0:T(8,128)(2,1)S(1)} %collective-permute-done.1.refs_2_.refs_6_), channel_id=1, source_target_pairs={{4,0},{5,1},{6,2},{7,3},{8,4},{9,5},{10,6},{11,7},{12,8},{13,9},{1... | collective-permute-start | bytes 393224 | tf_op jit(solution)/shard_map/ppermute | solution.py:228
  17.5 8.9 %collective-permute-start.19 = (bf16[2,256,128]{2,1,0:T(8,128)(2,1)S(1)}, bf16[2,256,128]{2,1,0:T(8,128)(2,1)S(1)}, u32[]{:S(2)}, u32[]{:S(2)}) collective-permute-start(bf16[2,256,128]{2,1,0:T(8,128)(2,1)S(1)} %collective-permute-done.15.refs_2_.refs_6_), channel_id=1, source_target_pairs={{4,0},{5,1},{6,2},{7,3},{8,4},{9,5},{10,6},{11,7},{12,8},{13,9},{1... | collective-permute-start | bytes 393224 | tf_op jit(solution)/shard_map/ppermute | solution.py:228
  19.9 9.3 %collective-permute-start.7 = (bf16[2,256,128]{2,1,0:T(8,128)(2,1)S(1)}, bf16[2,256,128]{2,1,0:T(8,128)(2,1)S(1)}, u32[]{:S(2)}, u32[]{:S(2)}) collective-permute-start(bf16[2,256,128]{2,1,0:T(8,128)(2,1)S(1)} %collective-permute-done.3.refs_8_), channel_id=1, source_target_pairs={{4,0},{5,1},{6,2},{7,3},{8,4},{9,5},{10,6},{11,7},{20,16},{21,17},... | collective-permute-start | bytes 393224 | tf_op jit(solution)/shard_map/ppermute | solution.py:228
  22.9 9.0 %collective-permute-start.21 = (bf16[2,256,128]{2,1,0:T(8,128)(2,1)S(1)}, bf16[2,256,128]{2,1,0:T(8,128)(2,1)S(1)}, u32[]{:S(2)}, u32[]{:S(2)}) collective-permute-start(bf16[2,256,128]{2,1,0:T(8,128)(2,1)S(1)} %collective-permute-done.17.refs_8_), channel_id=1, source_target_pairs={{4,0},{5,1},{6,2},{7,3},{8,4},{9,5},{10,6},{11,7},{20,16},{21,17},... | collective-permute-start | bytes 393224 | tf_op jit(solution)/shard_map/ppermute | solution.py:228
  26.4 8.3 %collective-permute-start.9 = (bf16[2,256,128]{2,1,0:T(8,128)(2,1)S(1)}, bf16[2,256,128]{2,1,0:T(8,128)(2,1)S(1)}, u32[]{:S(2)}, u32[]{:S(2)}) collective-permute-start(bf16[2,256,128]{2,1,0:T(8,128)(2,1)S(1)} %collective-permute-done.5.refs_10_), channel_id=1, source_target_pairs={{4,0},{5,1},{6,2},{7,3},{8,4},{9,5},{10,6},{11,7},{20,16},{21,17},... | collective-permute-start | bytes 393224 | tf_op jit(solution)/shard_map/ppermute | solution.py:228
  29.2 8.3 %collective-permute-start.23 = (bf16[2,256,128]{2,1,0:T(8,128)(2,1)S(1)}, bf16[2,256,128]{2,1,0:T(8,128)(2,1)S(1)}, u32[]{:S(2)}, u32[]{:S(2)}) collective-permute-start(bf16[2,256,128]{2,1,0:T(8,128)(2,1)S(1)} %collective-permute-done.19.refs_10_), channel_id=1, source_target_pairs={{4,0},{5,1},{6,2},{7,3},{8,4},{9,5},{10,6},{11,7},{20,16},{21,17},... | collective-permute-start | bytes 393224 | tf_op jit(solution)/shard_map/ppermute | solution.py:228
  31.9 8.4 %collective-permute-start.28 = (bf16[2,256,128]{2,1,0:T(8,128)(2,1)S(1)}, bf16[2,256,128]{2,1,0:T(8,128)(2,1)S(1)}, u32[]{:S(2)}, u32[]{:S(2)}) collective-permute-start(bf16[2,256,128]{2,1,0:T(8,128)(2,1)S(1)} %collective-permute-done.7.refs_12_.refs_4_), channel_id=1, source_target_pairs={{4,0},{5,1},{6,2},{7,3},{20,16},{21,17},{22,18},{23,19}} | collective-permute-start | bytes 393224 | tf_op jit(solution)/shard_map/ppermute | solution.py:228
  34.7 8.4 %collective-permute-start.35 = (bf16[2,256,128]{2,1,0:T(8,128)(2,1)S(1)}, bf16[2,256,128]{2,1,0:T(8,128)(2,1)S(1)}, u32[]{:S(2)}, u32[]{:S(2)}) collective-permute-start(bf16[2,256,128]{2,1,0:T(8,128)(2,1)S(1)} %collective-permute-done.21.refs_12_.refs_4_), channel_id=1, source_target_pairs={{4,0},{5,1},{6,2},{7,3},{20,16},{21,17},{22,18},{23,19}} | collective-permute-start | bytes 393224 | tf_op jit(solution)/shard_map/ppermute | solution.py:228
  37.5 8.4 %collective-permute-start.30 = (bf16[2,256,128]{2,1,0:T(8,128)(2,1)S(1)}, bf16[2,256,128]{2,1,0:T(8,128)(2,1)S(1)}, u32[]{:S(2)}, u32[]{:S(2)}) collective-permute-start(bf16[2,256,128]{2,1,0:T(8,128)(2,1)S(1)} %collective-permute-done.9.refs_14_.refs_6_), channel_id=1, source_target_pairs={{4,0},{5,1},{6,2},{7,3},{20,16},{21,17},{22,18},{23,19}} | collective-permute-start | bytes 393224 | tf_op jit(solution)/shard_map/ppermute | solution.py:228
  40.3 8.3 %collective-permute-start.37 = (bf16[2,256,128]{2,1,0:T(8,128)(2,1)S(1)}, bf16[2,256,128]{2,1,0:T(8,128)(2,1)S(1)}, u32[]{:S(2)}, u32[]{:S(2)}) collective-permute-start(bf16[2,256,128]{2,1,0:T(8,128)(2,1)S(1)} %collective-permute-done.23.refs_14_.refs_6_), channel_id=1, source_target_pairs={{4,0},{5,1},{6,2},{7,3},{20,16},{21,17},{22,18},{23,19}} | collective-permute-start | bytes 393224 | tf_op jit(solution)/shard_map/ppermute | solution.py:228
  43.1 10.3 %collective-permute-start.24 = (bf16[2,256,128]{2,1,0:T(8,128)(2,1)S(1)}, bf16[2,256,128]{2,1,0:T(8,128)(2,1)S(1)}, u32[]{:S(2)}, u32[]{:S(2)}) collective-permute-start(bf16[2,256,128]{2,1,0:T(8,128)(2,1)S(1)} %collective-permute-done.23.refs_14_.refs_6_), channel_id=1, source_target_pairs={{0,1},{1,0},{2,3},{3,2},{4,5},{5,4},{6,7},{7,6},{8,9},{9,8},{10,11... | collective-permute-start | bytes 393224 | tf_op jit(solution)/shard_map/ppermute | solution.py:224
  43.1 12.1 %collective-permute-start.29 = (bf16[2,256,128]{2,1,0:T(8,128)(2,1)S(1)}, bf16[2,256,128]{2,1,0:T(8,128)(2,1)S(1)}, u32[]{:S(2)}, u32[]{:S(2)}) collective-permute-start(bf16[2,256,128]{2,1,0:T(8,128)(2,1)S(1)} %collective-permute-done.28.refs_8_), channel_id=1, source_target_pairs={{0,1},{1,0},{2,3},{3,2},{4,5},{5,4},{6,7},{7,6},{8,9},{9,8},{10,11... | collective-permute-start | bytes 393224 | tf_op jit(solution)/shard_map/ppermute | solution.py:224
  45.9 14.4 %collective-permute-start.31 = (bf16[2,256,128]{2,1,0:T(8,128)(2,1)S(1)}, bf16[2,256,128]{2,1,0:T(8,128)(2,1)S(1)}, u32[]{:S(2)}, u32[]{:S(2)}) collective-permute-start(bf16[2,256,128]{2,1,0:T(8,128)(2,1)S(1)} %collective-permute-done.30.refs_10_), channel_id=1, source_target_pairs={{0,1},{1,0},{2,3},{3,2},{4,5},{5,4},{6,7},{7,6},{8,9},{9,8},{10,11... | collective-permute-start | bytes 393224 | tf_op jit(solution)/shard_map/ppermute | solution.py:224
  46.0 19.7 %collective-permute-start.36 = (bf16[2,256,128]{2,1,0:T(8,128)(2,1)S(1)}, bf16[2,256,128]{2,1,0:T(8,128)(2,1)S(1)}, u32[]{:S(2)}, u32[]{:S(2)}) collective-permute-start(bf16[2,256,128]{2,1,0:T(8,128)(2,1)S(1)} %collective-permute-done.35.refs_8_), channel_id=1, source_target_pairs={{0,1},{1,0},{2,3},{3,2},{4,5},{5,4},{6,7},{7,6},{8,9},{9,8},{10,11... | collective-permute-start | bytes 393224 | tf_op jit(solution)/shard_map/ppermute | solution.py:224
  48.6 17.5 %collective-permute-start.38 = (bf16[2,256,128]{2,1,0:T(8,128)(2,1)S(1)}, bf16[2,256,128]{2,1,0:T(8,128)(2,1)S(1)}, u32[]{:S(2)}, u32[]{:S(2)}) collective-permute-start(bf16[2,256,128]{2,1,0:T(8,128)(2,1)S(1)} %collective-permute-done.37.refs_10_), channel_id=1, source_target_pairs={{0,1},{1,0},{2,3},{3,2},{4,5},{5,4},{6,7},{7,6},{8,9},{9,8},{10,11... | collective-permute-start | bytes 393224 | tf_op jit(solution)/shard_map/ppermute | solution.py:224
  53.5 18.5 %collective-permute-start.12 = (bf16[2,256,128]{2,1,0:T(8,128)(2,1)}, bf16[2,256,128]{2,1,0:T(8,128)(2,1)S(1)}, u32[]{:S(2)}, u32[]{:S(2)}) collective-permute-start(bf16[2,256,128]{2,1,0:T(8,128)(2,1)} %get-tuple-element.20), channel_id=1, source_target_pairs={{0,2},{1,3},{2,0},{3,1},{4,6},{5,7},{6,4},{7,5},{8,10},{9,11},{10,... | collective-permute-start | bytes 393224 | tf_op jit(solution)/shard_map/ppermute | solution.py:224
  55.3 16.9 %collective-permute-start.11 = (bf16[2,256,128]{2,1,0:T(8,128)(2,1)}, bf16[2,256,128]{2,1,0:T(8,128)(2,1)S(1)}, u32[]{:S(2)}, u32[]{:S(2)}) collective-permute-start(bf16[2,256,128]{2,1,0:T(8,128)(2,1)} %get-tuple-element.19.refs_0_), channel_id=1, source_target_pairs={{0,1},{1,0},{2,3},{3,2},{4,5},{5,4},{6,7},{7,6},{8,9},{9,8},{10,11... | collective-permute-start | bytes 393224 | tf_op jit(solution)/shard_map/ppermute | solution.py:224
  60.4 12.8 %collective-permute-start.26 = (bf16[2,256,128]{2,1,0:T(8,128)(2,1)}, bf16[2,256,128]{2,1,0:T(8,128)(2,1)S(1)}, u32[]{:S(2)}, u32[]{:S(2)}) collective-permute-start(bf16[2,256,128]{2,1,0:T(8,128)(2,1)} %get-tuple-element.24), channel_id=1, source_target_pairs={{0,2},{1,3},{2,0},{3,1},{4,6},{5,7},{6,4},{7,5},{8,10},{9,11},{10,... | collective-permute-start | bytes 393224 | tf_op jit(solution)/shard_map/ppermute | solution.py:224
  65.7 7.4 %collective-permute-start.25 = (bf16[2,256,128]{2,1,0:T(8,128)(2,1)}, bf16[2,256,128]{2,1,0:T(8,128)(2,1)S(1)}, u32[]{:S(2)}, u32[]{:S(2)}) collective-permute-start(bf16[2,256,128]{2,1,0:T(8,128)(2,1)} %get-tuple-element.23.refs_4_), channel_id=1, source_target_pairs={{0,1},{1,0},{2,3},{3,2},{4,5},{5,4},{6,7},{7,6},{8,9},{9,8},{10,11... | collective-permute-start | bytes 393224 | tf_op jit(solution)/shard_map/ppermute | solution.py:224
  66.1 7.6 %collective-permute-start.33 = (bf16[2,256,128]{2,1,0:T(8,128)(2,1)}, bf16[2,256,128]{2,1,0:T(8,128)(2,1)S(1)}, u32[]{:S(2)}, u32[]{:S(2)}) collective-permute-start(bf16[2,256,128]{2,1,0:T(8,128)(2,1)} %get-tuple-element.26), channel_id=1, source_target_pairs={{0,2},{1,3},{2,0},{3,1},{4,6},{5,7},{6,4},{7,5},{8,10},{9,11},{10,... | collective-permute-start | bytes 393224 | tf_op jit(solution)/shard_map/ppermute | solution.py:224
  (60 other events, 720.3 us)

commit v2 on v1

v2 whole, which is shorter than its diff:
```python
import functools
import math

import jax
import jax.numpy as jnp
import ml_dtypes
import numpy as np
from jax import lax
from jax.experimental import pallas as pl
from jax.experimental.pallas import tpu as pltpu
from jax.sharding import PartitionSpec as P

F = 512
F0 = 6
LAGS = 2048
BAND = 512
TEAM = 4
HALVES = 2
LANES = 128
BINS = F // (TEAM * HALVES)
QUADRANTS = 4

MIB = 1024 * 1024


def busy(microseconds):
    return pl.CostEstimate(flops=int(microseconds * 1.1535e9), bytes_accessed=0, transcendentals=0)


def column_order():
    bins = np.arange(F)[np.argsort((F0 + np.arange(F)) % TEAM, kind="stable")].reshape(TEAM, HALVES, 1, BINS)
    parts = np.arange(2).reshape(1, 1, 2, 1) * F
    return (bins + parts).reshape(-1)


def tables(length):
    freqs = F0 + np.arange(F, dtype=np.int64)
    unit = np.float32(2.0 * math.pi / length)

    def cut(phase):
        angle = unit * np.mod(phase, length).astype(np.float32)
        return np.cos(angle), -np.sin(angle)

    order = column_order()
    part = length // QUADRANTS
    forward = np.concatenate(cut(np.arange(part)[:, None] * freqs[None, :]), axis=1)[:, order]
    forward = forward.reshape(part, TEAM, 2 * F // TEAM).transpose(1, 0, 2)
    shifts = np.arange(LAGS, dtype=np.int64) - LAGS // 2
    inverse = np.concatenate(cut(freqs[:, None] * shifts[None, :]), axis=0)[order]
    inverse = inverse.reshape(TEAM, 2 * F // TEAM, LAGS)
    return forward.astype(ml_dtypes.bfloat16), inverse.astype(ml_dtypes.bfloat16)


def spectra_kernel(windows, records_hbm, table_hbm, live, own0, own1, far0, far1, records, table, spec, sems):
    rows, length = records.shape
    count = rows // windows
    part = length // QUADRANTS
    copies = [pltpu.make_async_copy(records_hbm, records, sems.at[0])]
    copies += [pltpu.make_async_copy(table_hbm.at[c], table.at[c], sems.at[1 + c]) for c in range(TEAM)]
    for copy in copies:
        copy.start()
    me = lax.rem(lax.axis_index("chan"), TEAM)
    channel = lax.broadcasted_iota(jnp.int32, (rows, count), 0) // windows
    lane = lax.broadcasted_iota(jnp.int32, (rows, count), 1)
    mask = jnp.where(channel == lane, live[...].astype(jnp.float32), 0.0)
    gain = jnp.sum(mask, axis=1, keepdims=True)
    real_lane = lax.broadcasted_iota(jnp.int32, (rows, LANES), 1) < BINS
    copies[0].wait()
    quadrants = [records[:, q * part : (q + 1) * part] for q in range(QUADRANTS)]
    squares = jnp.zeros((rows, LANES), jnp.float32)
    for c in range(TEAM):
        copies[1 + c].wait()
        terms = [jnp.dot(x, table[c], preferred_element_type=jnp.float32) for x in quadrants]
        for half in range(HALVES):
            t0, t1, t2, t3 = (t[:, half * LANES : (half + 1) * LANES] for t in terms)
            if c == 0:
                value = (t0 + t2) + (t1 + t3)
            elif c == 2:
                value = (t0 + t2) - (t1 + t3)
            else:
                turned = pltpu.roll(t1 - t3, BINS, 1)
                value = (t0 - t2) + jnp.where(real_lane == (c == 1), turned, -turned)
            spec[c * HALVES + half] = value
            squares = squares + value * value
    power = jnp.sum(squares, axis=1, keepdims=True)
    scale = gain * lax.rsqrt(power * (1.0 / (2 * F)) + 1e-06)
    for k in range(TEAM * HALVES):
        spec[k] = spec[k] * scale
    for half, outs in enumerate(((own0, far0), (own1, far1))):
        for d in range(TEAM):
            c = jnp.bitwise_xor(me, d)
            for w in range(windows):
                piece = spec[c * HALVES + half, pl.ds(w, count, stride=windows), :]
                outs[d // 2][d % 2, w * count : (w + 1) * count, :] = piece.astype(jnp.bfloat16)


def spectra(records, live_mask, table):
    count, windows, length = records.shape
    rows = count * windows
    return pl.pallas_call(
        functools.partial(spectra_kernel, windows),
        in_specs=[
            pl.BlockSpec(memory_space=pl.ANY),
            pl.BlockSpec(memory_space=pl.ANY),
            pl.BlockSpec(memory_space=pltpu.VMEM),
        ],
        out_specs=[pl.BlockSpec(memory_space=pltpu.VMEM)] * 4,
        out_shape=[pltpu.VMEM((2, rows, LANES), jnp.bfloat16)] * 4,
        scratch_shapes=[
            pltpu.VMEM((rows, length), jnp.bfloat16),
            pltpu.VMEM(table.shape, jnp.bfloat16),
            pltpu.VMEM((TEAM * HALVES, rows, LANES), jnp.float32),
            pltpu.SemaphoreType.DMA((1 + TEAM,)),
        ],
        compiler_params=pltpu.CompilerParams(vmem_limit_bytes=20 * MIB),
        cost_estimate=busy(3.0),
        name="spectra",
    )(records.reshape(rows, length), table, live_mask.reshape(1, count))


def cross_kernel(windows, count, first, last, low, planes, offsets, *refs):
    given, (near, far, side, extended, paired) = refs[: 4 * (planes + 1)], refs[4 * (planes + 1) :]
    me = lax.rem(lax.axis_index("chan"), TEAM)
    span = TEAM * count
    number = last - first
    blocks = [jnp.bitwise_xor(me, d) for d in range(TEAM)]

    def pieces(plane):
        own, own_swapped, across, across_swapped = given[4 * plane : 4 * plane + 4]
        return (own, own_swapped, across, across_swapped)

    for d, ref in enumerate(pieces(0)):
        for w in range(windows):
            side[w, d * count : (d + 1) * count, :] = ref[d % 2, w * count : (w + 1) * count, :].astype(jnp.float32)
    for plane in range(planes):
        for d, ref in enumerate(pieces(plane + 1)):
            start = pl.multiple_of(plane * span + blocks[d] * count, count)
            for w in range(windows):
                extended[w, pl.ds(start, count), :] = ref[d % 2, w * count : (w + 1) * count, :].astype(jnp.float32)
    tail = extended.shape[1] - planes * span
    if tail:
        extended[:, planes * span :, :] = jnp.zeros((windows, tail, LANES), jnp.float32)

    lane = lax.broadcasted_iota(jnp.int32, (8, LANES), 1)
    real_lane = lane < BINS
    sign = jnp.where(real_lane, 1.0 / windows, -1.0 / windows)

    def group(step, carry):
        at = pl.multiple_of(step * 8, 8)
        d = step // (count // 8)
        within = lax.rem(step, count // 8) * 8
        channel = jnp.bitwise_xor(me, d) * count + within
        straight, turned = [], []
        for w in range(windows):
            value = side[w, pl.ds(at, 8), :]
            straight.append(value * (1.0 / windows))
            turned.append(pltpu.roll(value, BINS, 1) * sign)
        for j in range(number):
            place = channel + offsets[first + j] - low * span
            real_part, imag_part = None, None
            for w in range(windows):
                partner = extended[w, pl.ds(place, 8), :]
                r, i = straight[w] * partner, turned[w] * partner
                real_part = r if w == 0 else real_part + r
                imag_part = i if w == 0 else imag_part + i
            folded = pltpu.roll(jnp.where(real_lane, imag_part, real_part), BINS, 1)
            both = jnp.where(real_lane, real_part, imag_part) + folded
            paired[d, pl.ds(within * number + j, 8, stride=number), :] = both
        return carry

    lax.fori_loop(0, span // 8, group, 0, unroll=2)
    for d in range(TEAM):
        (near if d < 2 else far)[d % 2] = paired[d].astype(jnp.bfloat16)


def cross(windows, count, first, last, offsets, team_planes):
    span = TEAM * count
    stride = BAND // offsets.shape[0]
    low = (first * stride + 1) // span
    high = (span - 1 + last * stride) // span
    partners = [team_planes[p] for p in range(low, min(high, len(team_planes) - 1) + 1)]
    number = last - first
    vmem = pl.BlockSpec(memory_space=pltpu.VMEM)
    return pl.pallas_call(
        functools.partial(cross_kernel, windows, count, first, last, low, len(partners)),
        in_specs=[pl.BlockSpec(memory_space=pltpu.SMEM)] + [vmem] * (4 * len(partners) + 4),
        out_specs=[vmem] * 2,
        out_shape=[pltpu.VMEM((2, count * number, LANES), jnp.bfloat16)] * 2,
        scratch_shapes=[
            pltpu.VMEM((windows, span, LANES), jnp.float32),
            pltpu.VMEM((windows, (high - low + 1) * span, LANES), jnp.float32),
            pltpu.VMEM((TEAM, count * number, LANES), jnp.float32),
        ],
        compiler_params=pltpu.CompilerParams(vmem_limit_bytes=8 * MIB),
        cost_estimate=busy(2.5),
        name="cross",
    )(offsets, *[piece for plane in [team_planes[0]] + partners for piece in plane])


def lag_sum(given, table, columns):
    me = lax.rem(lax.axis_index("chan"), TEAM)
    total = None
    for d in range(TEAM):
        left = jnp.concatenate([given[h * TEAM + d][d % 2] for h in range(HALVES)], axis=1)
        term = jnp.dot(left, table[jnp.bitwise_xor(me, d), :, columns], preferred_element_type=jnp.float32)
        total = term if d == 0 else total + term
    return total * (1.0 / math.sqrt(F))


def early_kernel(tile, *refs):
    given, table, out = refs[:-2], refs[-2], refs[-1]
    for t in range(LAGS // tile):
        columns = pl.ds(t * tile, tile)
        out[:, columns] = lag_sum(given, table, columns)


def late_kernel(count, tile, *refs):
    given, table, early, out = refs[:-3], refs[-3], refs[-2], refs[-1]
    columns = pl.ds(pl.multiple_of(pl.program_id(0) * tile, tile), tile)
    both = [early[:, columns], lag_sum(given, table, columns)]
    both = [v.reshape(count, v.shape[0] // count, tile) for v in both]
    out[...] = jnp.concatenate(both, axis=1).astype(jnp.bfloat16)


def lags_early(group, table):
    arrays = [piece for half in group for piece in half]
    vmem = pl.BlockSpec(memory_space=pltpu.VMEM)
    return pl.pallas_call(
        functools.partial(early_kernel, 512),
        in_specs=[vmem] * (len(arrays) + 1),
        out_specs=vmem,
        out_shape=pltpu.VMEM((arrays[0].shape[1], LAGS), jnp.float32),
        compiler_params=pltpu.CompilerParams(vmem_limit_bytes=12 * MIB),
        cost_estimate=busy(1.5),
        name="lags_early",
    )(*arrays, table)


def lags_late(group, table, early, count, number):
    arrays = [piece for half in group for piece in half]
    vmem = pl.BlockSpec(memory_space=pltpu.VMEM)
    tile = 512
    return pl.pallas_call(
        functools.partial(late_kernel, count, tile),
        grid=(LAGS // tile,),
        in_specs=[vmem] * (len(arrays) + 2),
        out_specs=pl.BlockSpec((count, number, tile), lambda i: (0, 0, i)),
        out_shape=jax.ShapeDtypeStruct((count, number, LAGS), jnp.bfloat16),
        compiler_params=pltpu.CompilerParams(vmem_limit_bytes=16 * MIB),
        cost_estimate=busy(2.0),
        name="lags_late",
    )(*arrays, table, early)


def solution(mesh):
    ring = mesh.shape["chan"]
    if ring % TEAM:
        raise ValueError("chan")

    def swapped(value, by):
        return lax.ppermute(value, "chan", [(i, i ^ by) for i in range(ring)])

    def down(value, hops):
        pairs = [(i, i - TEAM) for i in range(TEAM, ring) if i // TEAM + hops - 1 < ring // TEAM]
        return lax.ppermute(value, "chan", pairs)

    def shards(records, live_mask, offsets):
        count, windows, length = records.shape
        span = TEAM * count
        number = offsets.shape[0]
        forward, inverse = tables(length)
        own0, own1, far0, far1 = spectra(records, live_mask, jnp.asarray(forward))
        across0, across1 = swapped(far0, 2), swapped(far1, 2)
        reach = min((span + BAND - 2) // span, ring // TEAM - 1)
        chunks = [[[own0, across0], [own1, across1]]]
        for hops in range(1, reach + 1):
            previous = chunks[-1]
            chunks.append([[down(c, hops) for c in half] for half in previous])
        planes = [
            [[piece for c in half for piece in (c, swapped(c, 1))] for half in chunk] for chunk in chunks
        ]
        parts = []
        for first, last in ((0, number // 2), (number // 2, number)):
            group = []
            for half in range(HALVES):
                near, far = cross(windows, count, first, last, offsets, [p[half] for p in planes])
                back = swapped(far, 2)
                group.append([near, swapped(near, 1), back, swapped(back, 1)])
            parts.append(group)
        inverse = jnp.asarray(inverse)
        return lags_late(parts[1], inverse, lags_early(parts[0], inverse), count, number)

    in_specs = (P(("day", "chan"), None, None), P(("day", "chan")), P())
    out_specs = P(("day", "chan"), None, None)
    return jax.shard_map(shards, mesh=mesh, in_specs=in_specs, out_specs=out_specs, check_vma=False)
```

time: 87.1 us -> 74.9 us (0.86)
  Pallas kernels: 31.4 us -> 18.5 us
  local copies, waits for them, and re-layouts: 1.02 us -> 3.47 us
  waiting for transfers between devices: 27.4 us -> 25.4 us
  starting transfers between devices: 25.9 us -> 26.8 us
    pallas_call x4, Pallas kernels: 18.8 us -> 9.68 us  [cross(): pl.pallas_call(functools.partial(cross_kernel, windows, count, first, las...]
    pallas_call x2 -> x3, Pallas kernels: 12.6 us -> 8.8 us  [the longest x1 4.59 us: spectra(): pl.pallas_call(functools.partial(spectra_kernel, windows), in_specs=[pl.B...]
    unnamed x84 -> x10, local copies, waits for them, and re-layouts: 1.02 us -> 3.47 us
    ppermute x12, waiting for transfers between devices: 18.2 us -> 16.9 us  [down(): return lax.ppermute(value, 'chan', pairs)]
    ppermute x30, starting transfers between devices: 10.4 us -> 11.4 us  [swapped(): return lax.ppermute(value, 'chan', [(i, i ^ by) for i in range(ring)])]
  transfers between devices with their start and end apart: 42 -> 42, of which waited for: 15 -> 13; matrix products, arithmetic and copies ran while one was open for 0% -> 0% of each run, Pallas kernels for 22% -> 15%
where the time goes in v2:
time: 74.9 us; the launch traced here: 74.4 us
  starting transfers between devices  26.8 us (36%)
  waiting for transfers between devices  25.4 us (34%)
  Pallas kernels  18.5 us (25%)
  local copies, waits for them, and re-layouts  3.47 us (5%)
    ppermute x12, waiting for transfers between devices, down(): return lax.ppermute(value, 'chan', pairs)  16.9 us
    ppermute x12, starting transfers between devices, down(): return lax.ppermute(value, 'chan', pairs)  15.4 us
    ppermute x30, starting transfers between devices, swapped(): return lax.ppermute(value, 'chan', [(i, i ^ by) for i in range(ring)])  11.4 us
    pallas_call x4, Pallas kernels, cross(): pl.pallas_call(functools.partial(cross_kernel, windows, count, first, las...  9.68 us
    ppermute x30, waiting for transfers between devices, swapped(): return lax.ppermute(value, 'chan', [(i, i ^ by) for i in range(ring)])  8.45 us
    pallas_call x1, Pallas kernels, spectra(): pl.pallas_call(functools.partial(spectra_kernel, windows), in_specs=[pl.B...  4.59 us
    unnamed x10, local copies, waits for them, and re-layouts  3.47 us
    pallas_call x1, Pallas kernels, lags_late(): pl.pallas_call(functools.partial(late_kernel, count, tile), grid=(LAGS //...  2.95 us
  transfers between devices with their start and end apart: 42, of which 13 were waited for; matrix products, arithmetic and copies ran while one was open for 0% of the time, Pallas kernels for 15%

profile of v2, /device:TPU:0, one launch (start us, length us, event | category | flops | bytes accessed | tf_op | source)
XLA Modules:
  0.0 74.4 jit_solution(2748397751147574937)
XLA Ops:
  0.0 1.4 %copy-done.1 = bf16[32,8,3000]{2,1,0:T(8,128)(2,1)S(1)} copy-done((bf16[32,8,3000]{2,1,0:T(8,128)(2,1)S(1)}, bf16[32,8,3000]{2,1,0:T(8,128)(2,1)}, u32[]{:S(2)}) %copy-start.1) | copy-done | bytes 1536024
  2.1 1.4 %copy-done.4 = bf16[4,750,256]{2,1,0:T(8,128)(2,1)S(1)} copy-done((bf16[4,750,256]{2,1,0:T(8,128)(2,1)S(1)}, bf16[4,750,256]{2,1,0:T(8,128)(2,1)}, u32[]{:S(2)}) %copy-start.4) | copy-done | bytes 1536024
  3.5 4.6 %spectra.1 = (bf16[2,256,128]{2,1,0:T(8,128)(2,1)S(1)}, bf16[2,256,128]{2,1,0:T(8,128)(2,1)S(1)}, bf16[2,256,128]{2,1,0:T(8,128)(2,1)S(1)}, bf16[2,256,128]{2,1,0:T(8,128)(2,1)S(1)}) custom-call(bf16[256,3000]{1,0:T(8,128)(2,1)S(1)} %bitcast.2, bf16[4,750,256]{2,1,0:T(8,128)(2,1)S(1)} %copy-done.4, s32[1,32]{1,0:T(1,128)S(1)} %bitcast.3), custom_call_target="tpu_custom_call" | custom-call | flops 3460499968 | tf_op jit(solution)/shard_map/spectra/pallas_call | solution.py:100
  8.1 3.0 %collective-permute-start.1 = (bf16[2,256,128]{2,1,0:T(8,128)(2,1)S(1)}, bf16[2,256,128]{2,1,0:T(8,128)(2,1)S(1)}, u32[]{:S(2)}, u32[]{:S(2)}) collective-permute-start(bf16[2,256,128]{2,1,0:T(8,128)(2,1)S(1)} %get-tuple-element.18), channel_id=1, source_target_pairs={{0,2},{1,3},{2,0},{3,1},{4,6},{5,7},{6,4},{7,5},{8,10},{9,11},{10,... | collective-permute-start | bytes 393224 | tf_op jit(solution)/shard_map/ppermute | solution.py:261
  12.5 1.3 %collective-permute-start.19 = (bf16[2,256,128]{2,1,0:T(8,128)(2,1)S(1)}, bf16[2,256,128]{2,1,0:T(8,128)(2,1)S(1)}, u32[]{:S(2)}, u32[]{:S(2)}) collective-permute-start(bf16[2,256,128]{2,1,0:T(8,128)(2,1)S(1)} %get-tuple-element.21.refs_0_.refs_4_), channel_id=1, source_target_pairs={{4,0},{5,1},{6,2},{7,3},{8,4},{9,5},{10,6},{11,7},{12,8},{13,9},{1... | collective-permute-start | bytes 393224 | tf_op jit(solution)/shard_map/ppermute | solution.py:265
  13.8 1.6 %collective-permute-done.1.refs_2_.refs_6_ = bf16[2,256,128]{2,1,0:T(8,128)(2,1)S(1)} collective-permute-done((bf16[2,256,128]{2,1,0:T(8,128)(2,1)S(1)}, bf16[2,256,128]{2,1,0:T(8,128)(2,1)S(1)}, u32[]{:S(2)}, u32[]{:S(2)}) %collective-permute-start.1) | collective-permute-done | bytes 131104 | tf_op jit(solution)/shard_map/ppermute | solution.py:261
  15.4 2.0 %collective-permute-done.17.refs_2_.refs_6_ = bf16[2,256,128]{2,1,0:T(8,128)(2,1)S(1)} collective-permute-done((bf16[2,256,128]{2,1,0:T(8,128)(2,1)S(1)}, bf16[2,256,128]{2,1,0:T(8,128)(2,1)S(1)}, u32[]{:S(2)}, u32[]{:S(2)}) %collective-permute-start.17) | collective-permute-done | bytes 131104 | tf_op jit(solution)/shard_map/ppermute | solution.py:261
  18.8 1.3 %collective-permute-start.22 = (bf16[2,256,128]{2,1,0:T(8,128)(2,1)S(1)}, bf16[2,256,128]{2,1,0:T(8,128)(2,1)S(1)}, u32[]{:S(2)}, u32[]{:S(2)}) collective-permute-start(bf16[2,256,128]{2,1,0:T(8,128)(2,1)S(1)} %collective-permute-done.17.refs_2_.refs_6_), channel_id=1, source_target_pairs={{4,0},{5,1},{6,2},{7,3},{8,4},{9,5},{10,6},{11,7},{12,8},{13,9},{1... | collective-permute-start | bytes 393224 | tf_op jit(solution)/shard_map/ppermute | solution.py:265
  21.7 2.5 %collective-permute-done.6.refs_10_ = bf16[2,256,128]{2,1,0:T(8,128)(2,1)S(1)} collective-permute-done((bf16[2,256,128]{2,1,0:T(8,128)(2,1)S(1)}, bf16[2,256,128]{2,1,0:T(8,128)(2,1)S(1)}, u32[]{:S(2)}, u32[]{:S(2)}) %collective-permute-start.6) | collective-permute-done | bytes 131104 | tf_op jit(solution)/shard_map/ppermute | solution.py:265
  25.6 2.1 %collective-permute-done.22.refs_10_ = bf16[2,256,128]{2,1,0:T(8,128)(2,1)S(1)} collective-permute-done((bf16[2,256,128]{2,1,0:T(8,128)(2,1)S(1)}, bf16[2,256,128]{2,1,0:T(8,128)(2,1)S(1)}, u32[]{:S(2)}, u32[]{:S(2)}) %collective-permute-start.22) | collective-permute-done | bytes 131104 | tf_op jit(solution)/shard_map/ppermute | solution.py:265
  29.0 1.3 %collective-permute-start.7 = (bf16[2,256,128]{2,1,0:T(8,128)(2,1)S(1)}, bf16[2,256,128]{2,1,0:T(8,128)(2,1)S(1)}, u32[]{:S(2)}, u32[]{:S(2)}) collective-permute-start(bf16[2,256,128]{2,1,0:T(8,128)(2,1)S(1)} %collective-permute-done.6.refs_10_), channel_id=1, source_target_pairs={{4,0},{5,1},{6,2},{7,3},{8,4},{9,5},{10,6},{11,7},{20,16},{21,17},... | collective-permute-start | bytes 393224 | tf_op jit(solution)/shard_map/ppermute | solution.py:265
  32.4 3.2 %collective-permute-done.20.refs_4_.refs_12_ = bf16[2,256,128]{2,1,0:T(8,128)(2,1)S(1)} collective-permute-done((bf16[2,256,128]{2,1,0:T(8,128)(2,1)S(1)}, bf16[2,256,128]{2,1,0:T(8,128)(2,1)S(1)}, u32[]{:S(2)}, u32[]{:S(2)}) %collective-permute-start.20) | collective-permute-done | bytes 131104 | tf_op jit(solution)/shard_map/ppermute | solution.py:265
  35.6 2.3 %collective-permute-done.7.refs_6_.refs_14_ = bf16[2,256,128]{2,1,0:T(8,128)(2,1)S(1)} collective-permute-done((bf16[2,256,128]{2,1,0:T(8,128)(2,1)S(1)}, bf16[2,256,128]{2,1,0:T(8,128)(2,1)S(1)}, u32[]{:S(2)}, u32[]{:S(2)}) %collective-permute-start.7) | collective-permute-done | bytes 131104 | tf_op jit(solution)/shard_map/ppermute | solution.py:265
  39.2 1.3 %collective-permute-start.25 = (bf16[2,256,128]{2,1,0:T(8,128)(2,1)S(1)}, bf16[2,256,128]{2,1,0:T(8,128)(2,1)S(1)}, u32[]{:S(2)}, u32[]{:S(2)}) collective-permute-start(bf16[2,256,128]{2,1,0:T(8,128)(2,1)S(1)} %collective-permute-done.20.refs_4_.refs_12_), channel_id=1, source_target_pairs={{4,0},{5,1},{6,2},{7,3},{20,16},{21,17},{22,18},{23,19}} | collective-permute-start | bytes 393224 | tf_op jit(solution)/shard_map/ppermute | solution.py:265
  42.5 2.4 %cross.6 = (bf16[2,256,128]{2,1,0:T(8,128)(2,1)S(1)}, bf16[2,256,128]{2,1,0:T(8,128)(2,1)S(1)}) custom-call(s32[16]{0:T(128)S(1)} %copy-done.3, bf16[2,256,128]{2,1,0:T(8,128)(2,1)S(1)} %get-tuple-element.17.refs_0_.refs_4_, bf16[2,256,128]{2,1,0:T(8,128)(2,1)S(1)} %collective-permute-done.refs_1_.refs_5_, ...), custom_call_target="tpu_custom_call" | custom-call | flops 2883749888 | tf_op jit(solution)/shard_map/cross/pallas_call | solution.py:184
  47.4 1.5 %collective-permute-done.25.refs_8_ = bf16[2,256,128]{2,1,0:T(8,128)(2,1)S(1)} collective-permute-done((bf16[2,256,128]{2,1,0:T(8,128)(2,1)S(1)}, bf16[2,256,128]{2,1,0:T(8,128)(2,1)S(1)}, u32[]{:S(2)}, u32[]{:S(2)}) %collective-permute-start.25) | collective-permute-done | bytes 131104 | tf_op jit(solution)/shard_map/ppermute | solution.py:265
  49.4 2.3 %collective-permute-done.11.refs_10_ = bf16[2,256,128]{2,1,0:T(8,128)(2,1)S(1)} collective-permute-done((bf16[2,256,128]{2,1,0:T(8,128)(2,1)S(1)}, bf16[2,256,128]{2,1,0:T(8,128)(2,1)S(1)}, u32[]{:S(2)}, u32[]{:S(2)}) %collective-permute-start.11) | collective-permute-done | bytes 131104 | tf_op jit(solution)/shard_map/ppermute | solution.py:265
  51.7 1.9 %collective-permute-start.35 = (bf16[2,256,128]{2,1,0:T(8,128)(2,1)S(1)}, bf16[2,256,128]{2,1,0:T(8,128)(2,1)S(1)}, u32[]{:S(2)}, u32[]{:S(2)}) collective-permute-start(bf16[2,256,128]{2,1,0:T(8,128)(2,1)S(1)} %get-tuple-element.26), channel_id=1, source_target_pairs={{0,2},{1,3},{2,0},{3,1},{4,6},{5,7},{6,4},{7,5},{8,10},{9,11},{10,... | collective-permute-start | bytes 393224 | tf_op jit(solution)/shard_map/ppermute | solution.py:261
  53.7 2.4 %cross.7 = (bf16[2,256,128]{2,1,0:T(8,128)(2,1)S(1)}, bf16[2,256,128]{2,1,0:T(8,128)(2,1)S(1)}) custom-call(s32[16]{0:T(128)S(1)} %copy-done.3, bf16[2,256,128]{2,1,0:T(8,128)(2,1)S(1)} %get-tuple-element.21.refs_0_.refs_4_, bf16[2,256,128]{2,1,0:T(8,128)(2,1)S(1)} %collective-permute-done.16.refs_1_.refs_5_, ...), custom_call_target="tpu_custom_call" | custom-call | flops 2883749888 | tf_op jit(solution)/shard_map/cross/pallas_call | solution.py:184
  56.8 2.4 %cross.4 = (bf16[2,256,128]{2,1,0:T(8,128)(2,1)S(1)}, bf16[2,256,128]{2,1,0:T(8,128)(2,1)S(1)}) custom-call(s32[16]{0:T(128)S(1)} %copy-done.3, bf16[2,256,128]{2,1,0:T(8,128)(2,1)S(1)} %get-tuple-element.17.refs_0_.refs_4_, bf16[2,256,128]{2,1,0:T(8,128)(2,1)S(1)} %collective-permute-done.refs_1_.refs_5_, ...), custom_call_target="tpu_custom_call" | custom-call | flops 2883749888 | tf_op jit(solution)/shard_map/cross/pallas_call | solution.py:184
  59.8 1.9 %collective-permute-start.14 = (bf16[2,256,128]{2,1,0:T(8,128)(2,1)S(1)}, bf16[2,256,128]{2,1,0:T(8,128)(2,1)S(1)}, u32[]{:S(2)}, u32[]{:S(2)}) collective-permute-start(bf16[2,256,128]{2,1,0:T(8,128)(2,1)S(1)} %get-tuple-element.20), channel_id=1, source_target_pairs={{0,2},{1,3},{2,0},{3,1},{4,6},{5,7},{6,4},{7,5},{8,10},{9,11},{10,... | collective-permute-start | bytes 393224 | tf_op jit(solution)/shard_map/ppermute | solution.py:261
  61.7 2.4 %cross.5 = (bf16[2,256,128]{2,1,0:T(8,128)(2,1)S(1)}, bf16[2,256,128]{2,1,0:T(8,128)(2,1)S(1)}) custom-call(s32[16]{0:T(128)S(1)} %copy-done.3, bf16[2,256,128]{2,1,0:T(8,128)(2,1)S(1)} %get-tuple-element.21.refs_0_.refs_4_, bf16[2,256,128]{2,1,0:T(8,128)(2,1)S(1)} %collective-permute-done.16.refs_1_.refs_5_, ...), custom_call_target="tpu_custom_call" | custom-call | flops 2883749888 | tf_op jit(solution)/shard_map/cross/pallas_call | solution.py:184
  65.5 4.7 %collective-permute-done.30.refs_6_ = bf16[2,256,128]{2,1,0:T(8,128)(2,1)S(1)} collective-permute-done((bf16[2,256,128]{2,1,0:T(8,128)(2,1)S(1)}, bf16[2,256,128]{2,1,0:T(8,128)(2,1)S(1)}, u32[]{:S(2)}, u32[]{:S(2)}) %collective-permute-start.30) | collective-permute-done | bytes 131104 | tf_op jit(solution)/shard_map/ppermute | solution.py:261
  71.5 2.9 %lags_late.1 = bf16[32,16,2048]{2,1,0:T(8,128)(2,1)} custom-call(bf16[2,256,128]{2,1,0:T(8,128)(2,1)S(1)} %get-tuple-element.19.refs_0_, bf16[2,256,128]{2,1,0:T(8,128)(2,1)S(1)} %collective-permute-done.13.refs_1_, bf16[2,256,128]{2,1,0:T(8,128)(2,1)S(1)} %collective-permute-done.14.refs_2_, bf16[2,256,128]{2,1,0:T(8,128)(2,1)S(1)} %collective-permute-done.15.refs_3_, ...), custom_call_target="tpu_custom_call" | custom-call | flops 2307000064 | tf_op jit(solution)/shard_map/lags_late/pallas_call | solution.py:243
  (77 shorter events, 19.9 us)
Async XLA Ops:
  8.1 7.4 %collective-permute-start.1 = (bf16[2,256,128]{2,1,0:T(8,128)(2,1)S(1)}, bf16[2,256,128]{2,1,0:T(8,128)(2,1)S(1)}, u32[]{:S(2)}, u32[]{:S(2)}) collective-permute-start(bf16[2,256,128]{2,1,0:T(8,128)(2,1)S(1)} %get-tuple-element.18), channel_id=1, source_target_pairs={{0,2},{1,3},{2,0},{3,1},{4,6},{5,7},{6,4},{7,5},{8,10},{9,11},{10,... | collective-permute-start | bytes 393224 | tf_op jit(solution)/shard_map/ppermute | solution.py:261
  11.2 7.5 %collective-permute-start.3 = (bf16[2,256,128]{2,1,0:T(8,128)(2,1)S(1)}, bf16[2,256,128]{2,1,0:T(8,128)(2,1)S(1)}, u32[]{:S(2)}, u32[]{:S(2)}) collective-permute-start(bf16[2,256,128]{2,1,0:T(8,128)(2,1)S(1)} %get-tuple-element.17.refs_0_.refs_4_), channel_id=1, source_target_pairs={{4,0},{5,1},{6,2},{7,3},{8,4},{9,5},{10,6},{11,7},{12,8},{13,9},{1... | collective-permute-start | bytes 393224 | tf_op jit(solution)/shard_map/ppermute | solution.py:265
  12.5 8.7 %collective-permute-start.19 = (bf16[2,256,128]{2,1,0:T(8,128)(2,1)S(1)}, bf16[2,256,128]{2,1,0:T(8,128)(2,1)S(1)}, u32[]{:S(2)}, u32[]{:S(2)}) collective-permute-start(bf16[2,256,128]{2,1,0:T(8,128)(2,1)S(1)} %get-tuple-element.21.refs_0_.refs_4_), channel_id=1, source_target_pairs={{4,0},{5,1},{6,2},{7,3},{8,4},{9,5},{10,6},{11,7},{12,8},{13,9},{1... | collective-permute-start | bytes 393224 | tf_op jit(solution)/shard_map/ppermute | solution.py:265
  17.4 6.8 %collective-permute-start.6 = (bf16[2,256,128]{2,1,0:T(8,128)(2,1)S(1)}, bf16[2,256,128]{2,1,0:T(8,128)(2,1)S(1)}, u32[]{:S(2)}, u32[]{:S(2)}) collective-permute-start(bf16[2,256,128]{2,1,0:T(8,128)(2,1)S(1)} %collective-permute-done.1.refs_2_.refs_6_), channel_id=1, source_target_pairs={{4,0},{5,1},{6,2},{7,3},{8,4},{9,5},{10,6},{11,7},{12,8},{13,9},{1... | collective-permute-start | bytes 393224 | tf_op jit(solution)/shard_map/ppermute | solution.py:265
  18.8 8.9 %collective-permute-start.22 = (bf16[2,256,128]{2,1,0:T(8,128)(2,1)S(1)}, bf16[2,256,128]{2,1,0:T(8,128)(2,1)S(1)}, u32[]{:S(2)}, u32[]{:S(2)}) collective-permute-start(bf16[2,256,128]{2,1,0:T(8,128)(2,1)S(1)} %collective-permute-done.17.refs_2_.refs_6_), channel_id=1, source_target_pairs={{4,0},{5,1},{6,2},{7,3},{8,4},{9,5},{10,6},{11,7},{12,8},{13,9},{1... | collective-permute-start | bytes 393224 | tf_op jit(solution)/shard_map/ppermute | solution.py:265
  21.2 7.7 %collective-permute-start.18 = (bf16[2,256,128]{2,1,0:T(8,128)(2,1)S(1)}, bf16[2,256,128]{2,1,0:T(8,128)(2,1)S(1)}, u32[]{:S(2)}, u32[]{:S(2)}) collective-permute-start(bf16[2,256,128]{2,1,0:T(8,128)(2,1)S(1)} %collective-permute-done.17.refs_2_.refs_6_), channel_id=1, source_target_pairs={{0,1},{1,0},{2,3},{3,2},{4,5},{5,4},{6,7},{7,6},{8,9},{9,8},{10,11... | collective-permute-start | bytes 393224 | tf_op jit(solution)/shard_map/ppermute | solution.py:261
  21.2 9.0 %collective-permute-start.32 = (bf16[2,256,128]{2,1,0:T(8,128)(2,1)S(1)}, bf16[2,256,128]{2,1,0:T(8,128)(2,1)S(1)}, u32[]{:S(2)}, u32[]{:S(2)}) collective-permute-start(bf16[2,256,128]{2,1,0:T(8,128)(2,1)S(1)} %collective-permute-done.3.refs_8_), channel_id=1, source_target_pairs={{0,1},{1,0},{2,3},{3,2},{4,5},{5,4},{6,7},{7,6},{8,9},{9,8},{10,11... | collective-permute-start | bytes 393224 | tf_op jit(solution)/shard_map/ppermute | solution.py:261
  24.3 6.8 %collective-permute-start.4 = (bf16[2,256,128]{2,1,0:T(8,128)(2,1)S(1)}, bf16[2,256,128]{2,1,0:T(8,128)(2,1)S(1)}, u32[]{:S(2)}, u32[]{:S(2)}) collective-permute-start(bf16[2,256,128]{2,1,0:T(8,128)(2,1)S(1)} %collective-permute-done.3.refs_8_), channel_id=1, source_target_pairs={{4,0},{5,1},{6,2},{7,3},{8,4},{9,5},{10,6},{11,7},{20,16},{21,17},... | collective-permute-start | bytes 393224 | tf_op jit(solution)/shard_map/ppermute | solution.py:265
  27.7 7.9 %collective-permute-start.20 = (bf16[2,256,128]{2,1,0:T(8,128)(2,1)S(1)}, bf16[2,256,128]{2,1,0:T(8,128)(2,1)S(1)}, u32[]{:S(2)}, u32[]{:S(2)}) collective-permute-start(bf16[2,256,128]{2,1,0:T(8,128)(2,1)S(1)} %collective-permute-done.19.refs_8_), channel_id=1, source_target_pairs={{4,0},{5,1},{6,2},{7,3},{8,4},{9,5},{10,6},{11,7},{20,16},{21,17},... | collective-permute-start | bytes 393224 | tf_op jit(solution)/shard_map/ppermute | solution.py:265
  29.0 8.9 %collective-permute-start.7 = (bf16[2,256,128]{2,1,0:T(8,128)(2,1)S(1)}, bf16[2,256,128]{2,1,0:T(8,128)(2,1)S(1)}, u32[]{:S(2)}, u32[]{:S(2)}) collective-permute-start(bf16[2,256,128]{2,1,0:T(8,128)(2,1)S(1)} %collective-permute-done.6.refs_10_), channel_id=1, source_target_pairs={{4,0},{5,1},{6,2},{7,3},{8,4},{9,5},{10,6},{11,7},{20,16},{21,17},... | collective-permute-start | bytes 393224 | tf_op jit(solution)/shard_map/ppermute | solution.py:265
  30.3 7.6 %collective-permute-start.33 = (bf16[2,256,128]{2,1,0:T(8,128)(2,1)S(1)}, bf16[2,256,128]{2,1,0:T(8,128)(2,1)S(1)}, u32[]{:S(2)}, u32[]{:S(2)}) collective-permute-start(bf16[2,256,128]{2,1,0:T(8,128)(2,1)S(1)} %collective-permute-done.6.refs_10_), channel_id=1, source_target_pairs={{0,1},{1,0},{2,3},{3,2},{4,5},{5,4},{6,7},{7,6},{8,9},{9,8},{10,11... | collective-permute-start | bytes 393224 | tf_op jit(solution)/shard_map/ppermute | solution.py:261
  31.1 8.1 %collective-permute-start.38 = (bf16[2,256,128]{2,1,0:T(8,128)(2,1)S(1)}, bf16[2,256,128]{2,1,0:T(8,128)(2,1)S(1)}, u32[]{:S(2)}, u32[]{:S(2)}) collective-permute-start(bf16[2,256,128]{2,1,0:T(8,128)(2,1)S(1)} %collective-permute-done.22.refs_10_), channel_id=1, source_target_pairs={{0,1},{1,0},{2,3},{3,2},{4,5},{5,4},{6,7},{7,6},{8,9},{9,8},{10,11... | collective-permute-start | bytes 393224 | tf_op jit(solution)/shard_map/ppermute | solution.py:261
  31.1 9.4 %collective-permute-start.23 = (bf16[2,256,128]{2,1,0:T(8,128)(2,1)S(1)}, bf16[2,256,128]{2,1,0:T(8,128)(2,1)S(1)}, u32[]{:S(2)}, u32[]{:S(2)}) collective-permute-start(bf16[2,256,128]{2,1,0:T(8,128)(2,1)S(1)} %collective-permute-done.22.refs_10_), channel_id=1, source_target_pairs={{4,0},{5,1},{6,2},{7,3},{8,4},{9,5},{10,6},{11,7},{20,16},{21,17},... | collective-permute-start | bytes 393224 | tf_op jit(solution)/shard_map/ppermute | solution.py:265
  37.9 8.2 %collective-permute-start.9 = (bf16[2,256,128]{2,1,0:T(8,128)(2,1)S(1)}, bf16[2,256,128]{2,1,0:T(8,128)(2,1)S(1)}, u32[]{:S(2)}, u32[]{:S(2)}) collective-permute-start(bf16[2,256,128]{2,1,0:T(8,128)(2,1)S(1)} %collective-permute-done.4.refs_4_.refs_12_), channel_id=1, source_target_pairs={{4,0},{5,1},{6,2},{7,3},{20,16},{21,17},{22,18},{23,19}} | collective-permute-start | bytes 393224 | tf_op jit(solution)/shard_map/ppermute | solution.py:265
  39.2 9.7 %collective-permute-start.25 = (bf16[2,256,128]{2,1,0:T(8,128)(2,1)S(1)}, bf16[2,256,128]{2,1,0:T(8,128)(2,1)S(1)}, u32[]{:S(2)}, u32[]{:S(2)}) collective-permute-start(bf16[2,256,128]{2,1,0:T(8,128)(2,1)S(1)} %collective-permute-done.20.refs_4_.refs_12_), channel_id=1, source_target_pairs={{4,0},{5,1},{6,2},{7,3},{20,16},{21,17},{22,18},{23,19}} | collective-permute-start | bytes 393224 | tf_op jit(solution)/shard_map/ppermute | solution.py:265
  40.5 8.4 %collective-permute-start.21 = (bf16[2,256,128]{2,1,0:T(8,128)(2,1)S(1)}, bf16[2,256,128]{2,1,0:T(8,128)(2,1)S(1)}, u32[]{:S(2)}, u32[]{:S(2)}) collective-permute-start(bf16[2,256,128]{2,1,0:T(8,128)(2,1)S(1)} %collective-permute-done.20.refs_4_.refs_12_), channel_id=1, source_target_pairs={{0,1},{1,0},{2,3},{3,2},{4,5},{5,4},{6,7},{7,6},{8,9},{9,8},{10,11... | collective-permute-start | bytes 393224 | tf_op jit(solution)/shard_map/ppermute | solution.py:261
  41.1 10.6 %collective-permute-start.11 = (bf16[2,256,128]{2,1,0:T(8,128)(2,1)S(1)}, bf16[2,256,128]{2,1,0:T(8,128)(2,1)S(1)}, u32[]{:S(2)}, u32[]{:S(2)}) collective-permute-start(bf16[2,256,128]{2,1,0:T(8,128)(2,1)S(1)} %collective-permute-done.7.refs_6_.refs_14_), channel_id=1, source_target_pairs={{4,0},{5,1},{6,2},{7,3},{20,16},{21,17},{22,18},{23,19}} | collective-permute-start | bytes 393224 | tf_op jit(solution)/shard_map/ppermute | solution.py:265
  42.4 11.3 %collective-permute-start.24 = (bf16[2,256,128]{2,1,0:T(8,128)(2,1)S(1)}, bf16[2,256,128]{2,1,0:T(8,128)(2,1)S(1)}, u32[]{:S(2)}, u32[]{:S(2)}) collective-permute-start(bf16[2,256,128]{2,1,0:T(8,128)(2,1)S(1)} %collective-permute-done.23.refs_6_.refs_14_), channel_id=1, source_target_pairs={{0,1},{1,0},{2,3},{3,2},{4,5},{5,4},{6,7},{7,6},{8,9},{9,8},{10,11... | collective-permute-start | bytes 393224 | tf_op jit(solution)/shard_map/ppermute | solution.py:261
  46.1 10.0 %collective-permute-start.27 = (bf16[2,256,128]{2,1,0:T(8,128)(2,1)S(1)}, bf16[2,256,128]{2,1,0:T(8,128)(2,1)S(1)}, u32[]{:S(2)}, u32[]{:S(2)}) collective-permute-start(bf16[2,256,128]{2,1,0:T(8,128)(2,1)S(1)} %collective-permute-done.23.refs_6_.refs_14_), channel_id=1, source_target_pairs={{4,0},{5,1},{6,2},{7,3},{20,16},{21,17},{22,18},{23,19}} | collective-permute-start | bytes 393224 | tf_op jit(solution)/shard_map/ppermute | solution.py:265
  48.9 7.8 %collective-permute-start.10 = (bf16[2,256,128]{2,1,0:T(8,128)(2,1)S(1)}, bf16[2,256,128]{2,1,0:T(8,128)(2,1)S(1)}, u32[]{:S(2)}, u32[]{:S(2)}) collective-permute-start(bf16[2,256,128]{2,1,0:T(8,128)(2,1)S(1)} %collective-permute-done.9.refs_8_), channel_id=1, source_target_pairs={{0,1},{1,0},{2,3},{3,2},{4,5},{5,4},{6,7},{7,6},{8,9},{9,8},{10,11... | collective-permute-start | bytes 393224 | tf_op jit(solution)/shard_map/ppermute | solution.py:261
  48.9 10.4 %collective-permute-start.26 = (bf16[2,256,128]{2,1,0:T(8,128)(2,1)S(1)}, bf16[2,256,128]{2,1,0:T(8,128)(2,1)S(1)}, u32[]{:S(2)}, u32[]{:S(2)}) collective-permute-start(bf16[2,256,128]{2,1,0:T(8,128)(2,1)S(1)} %collective-permute-done.25.refs_8_), channel_id=1, source_target_pairs={{0,1},{1,0},{2,3},{3,2},{4,5},{5,4},{6,7},{7,6},{8,9},{9,8},{10,11... | collective-permute-start | bytes 393224 | tf_op jit(solution)/shard_map/ppermute | solution.py:261
  51.7 10.0 %collective-permute-start.35 = (bf16[2,256,128]{2,1,0:T(8,128)(2,1)S(1)}, bf16[2,256,128]{2,1,0:T(8,128)(2,1)S(1)}, u32[]{:S(2)}, u32[]{:S(2)}) collective-permute-start(bf16[2,256,128]{2,1,0:T(8,128)(2,1)S(1)} %get-tuple-element.26), channel_id=1, source_target_pairs={{0,2},{1,3},{2,0},{3,1},{4,6},{5,7},{6,4},{7,5},{8,10},{9,11},{10,... | collective-permute-start | bytes 393224 | tf_op jit(solution)/shard_map/ppermute | solution.py:261
  56.1 8.1 %collective-permute-start.34 = (bf16[2,256,128]{2,1,0:T(8,128)(2,1)S(1)}, bf16[2,256,128]{2,1,0:T(8,128)(2,1)S(1)}, u32[]{:S(2)}, u32[]{:S(2)}) collective-permute-start(bf16[2,256,128]{2,1,0:T(8,128)(2,1)S(1)} %get-tuple-element.25.refs_0_), channel_id=1, source_target_pairs={{0,1},{1,0},{2,3},{3,2},{4,5},{5,4},{6,7},{7,6},{8,9},{9,8},{10,11... | collective-permute-start | bytes 393224 | tf_op jit(solution)/shard_map/ppermute | solution.py:261
  56.7 7.7 %collective-permute-start.40 = (bf16[2,256,128]{2,1,0:T(8,128)(2,1)S(1)}, bf16[2,256,128]{2,1,0:T(8,128)(2,1)S(1)}, u32[]{:S(2)}, u32[]{:S(2)}) collective-permute-start(bf16[2,256,128]{2,1,0:T(8,128)(2,1)S(1)} %get-tuple-element.28), channel_id=1, source_target_pairs={{0,2},{1,3},{2,0},{3,1},{4,6},{5,7},{6,4},{7,5},{8,10},{9,11},{10,... | collective-permute-start | bytes 393224 | tf_op jit(solution)/shard_map/ppermute | solution.py:261
  (23 other events, 146.4 us)

commit v3 on v2

v3 whole, which is shorter than its diff:
```python
import functools
import math

import jax
import jax.numpy as jnp
import ml_dtypes
import numpy as np
from jax import lax
from jax.experimental import pallas as pl
from jax.experimental.pallas import tpu as pltpu
from jax.sharding import PartitionSpec as P

F = 512
F0 = 6
LAGS = 2048
BAND = 512
TEAM = 4
HALVES = 2
LANES = 128
BINS = F // (TEAM * HALVES)
QUADRANTS = 4

MIB = 1024 * 1024


def busy(microseconds):
    return pl.CostEstimate(flops=int(microseconds * 1.1535e9), bytes_accessed=0, transcendentals=0)


def column_order():
    kinds = np.asarray([0, 2, 1, 3])[(F0 + np.arange(F)) % QUADRANTS]
    bins = np.argsort(kinds, kind="stable").reshape(TEAM, HALVES, 1, BINS)
    parts = np.arange(2).reshape(1, 1, 2, 1) * F
    return (bins + parts).reshape(-1)


def tables(length):
    freqs = F0 + np.arange(F, dtype=np.int64)
    unit = np.float32(2.0 * math.pi / length)

    def cut(phase):
        angle = unit * np.mod(phase, length).astype(np.float32)
        return np.cos(angle), -np.sin(angle)

    order = column_order()
    part = length // QUADRANTS
    forward = np.concatenate(cut(np.arange(part)[:, None] * freqs[None, :]), axis=1)[:, order]
    forward = forward.reshape(part, 2, F).transpose(1, 0, 2)
    shifts = np.arange(LAGS, dtype=np.int64) - LAGS // 2
    inverse = np.concatenate(cut(freqs[:, None] * shifts[None, :]), axis=0)[order]
    inverse = inverse.reshape(TEAM, 2 * F // TEAM, LAGS)
    return forward.astype(ml_dtypes.bfloat16), inverse.astype(ml_dtypes.bfloat16)


def spectra_kernel(windows, records_hbm, table_hbm, live_hbm, mine, sibling, far0, far1, records, table, live, spec, scales, sems):
    rows, length = records.shape
    count = rows // windows
    part = length // QUADRANTS
    pitch = windows + 1
    pairs = [(records_hbm, records), (table_hbm.at[0], table.at[0]), (table_hbm.at[1], table.at[1]), (live_hbm, live)]
    copies = [pltpu.make_async_copy(a, b, sems.at[n]) for n, (a, b) in enumerate(pairs)]
    for copy in copies:
        copy.start()
    me = lax.rem(lax.axis_index("chan"), TEAM)
    real_lane = lax.broadcasted_iota(jnp.int32, (rows, LANES), 1) < BINS
    copies[0].wait()
    x0, x1, x2, x3 = (records[:, q * part : (q + 1) * part] for q in range(QUADRANTS))

    def both(first, second, columns):
        total = jnp.dot(first, columns, preferred_element_type=jnp.float32)
        return total + jnp.dot(second, columns, preferred_element_type=jnp.float32)

    squares = jnp.zeros((rows, LANES), jnp.float32)
    for odd in range(2):
        copies[1 + odd].wait()
        columns = table[odd]
        if odd:
            left, right = both(x0, -x2, columns), both(x1, -x3, columns)
        else:
            left, right = both(x0, x2, columns), both(x1, x3, columns)
        for c in range(2):
            for half in range(HALVES):
                at = (c * HALVES + half) * LANES
                near, other = left[:, at : at + LANES], right[:, at : at + LANES]
                if odd:
                    other = pltpu.roll(other, BINS, 1)
                    value = near + jnp.where(real_lane == (c == 0), other, -other)
                else:
                    value = near + other if c == 0 else near - other
                squares = squares + value * value
                for channel in range(count):
                    rows_of = slice(channel * windows, (channel + 1) * windows)
                    spec[(2 * odd + c) * HALVES + half, channel * pitch : channel * pitch + windows, :] = value[rows_of]
    copies[3].wait()
    channel = lax.broadcasted_iota(jnp.int32, (rows, count), 0) // windows
    lane = lax.broadcasted_iota(jnp.int32, (rows, count), 1)
    mask = jnp.where(channel == lane, live[...].astype(jnp.float32), 0.0)
    gain = jnp.sum(mask, axis=1, keepdims=True)
    power = jnp.sum(squares, axis=1, keepdims=True)
    scale = jnp.broadcast_to(gain * lax.rsqrt(power * (1.0 / (2 * F)) + 1e-06), (rows, LANES))
    for channel in range(count):
        scales[channel * pitch : channel * pitch + windows, :] = scale[channel * windows : (channel + 1) * windows]
    for w in range(windows):
        every = pl.ds(w, count, stride=pitch)
        factor = scales[every, :]
        for half, far in enumerate((far0, far1)):
            places = [mine.at[half], sibling.at[half], far.at[0], far.at[1]]
            for d, place in enumerate(places):
                quarter = jnp.bitwise_xor(me, d)
                piece = spec[quarter * HALVES + half, every, :] * factor
                place[w * count : (w + 1) * count, :] = piece.astype(jnp.bfloat16)


def spectra(records, live_mask, table):
    count, windows, length = records.shape
    rows = count * windows
    return pl.pallas_call(
        functools.partial(spectra_kernel, windows),
        in_specs=[
            pl.BlockSpec(memory_space=pl.ANY),
            pl.BlockSpec(memory_space=pl.ANY),
            pl.BlockSpec(memory_space=pl.ANY),
        ],
        out_specs=[pl.BlockSpec(memory_space=pltpu.VMEM)] * 4,
        out_shape=[pltpu.VMEM((2, rows, LANES), jnp.bfloat16)] * 4,
        scratch_shapes=[
            pltpu.VMEM((rows, length), jnp.bfloat16),
            pltpu.VMEM(table.shape, jnp.bfloat16),
            pltpu.VMEM((1, count), jnp.int32),
            pltpu.VMEM((TEAM * HALVES, count * (windows + 1), LANES), jnp.float32),
            pltpu.VMEM((count * (windows + 1), LANES), jnp.float32),
            pltpu.SemaphoreType.DMA((4,)),
        ],
        compiler_params=pltpu.CompilerParams(vmem_limit_bytes=58 * MIB),
        cost_estimate=busy(3.0),
        name="spectra",
    )(records.reshape(rows, length), table, live_mask.reshape(1, count))


def join_kernel(first, second, out):
    for half in range(out.shape[0] // 2):
        out[2 * half] = first[half]
        out[2 * half + 1] = second[half]


def joined(first, second):
    vmem = pl.BlockSpec(memory_space=pltpu.VMEM)
    return pl.pallas_call(
        join_kernel,
        in_specs=[vmem] * 2,
        out_specs=vmem,
        out_shape=pltpu.VMEM((2 * first.shape[0],) + first.shape[1:], first.dtype),
        compiler_params=pltpu.CompilerParams(vmem_limit_bytes=2 * MIB),
        cost_estimate=busy(0.3),
        name="joined",
    )(first, second)


def far_kernel(straight, crossed, out):
    out[0] = straight[0]
    out[1] = crossed[1]


def far_joined(straight, crossed):
    vmem = pl.BlockSpec(memory_space=pltpu.VMEM)
    return pl.pallas_call(
        far_kernel,
        in_specs=[vmem] * 2,
        out_specs=vmem,
        out_shape=pltpu.VMEM(straight.shape, straight.dtype),
        compiler_params=pltpu.CompilerParams(vmem_limit_bytes=2 * MIB),
        cost_estimate=busy(0.3),
        name="far_joined",
    )(straight, crossed)


def cross_kernel(windows, count, halves, first, last, low, planes, offsets, *refs):
    each = 1 + len(halves)
    given, (near, far, side, extended, paired) = refs[: each * (planes + 1)], refs[each * (planes + 1) :]
    me = lax.rem(lax.axis_index("chan"), TEAM)
    span = TEAM * count
    number = last - first
    pitch = number + 1
    blocks = [jnp.bitwise_xor(me, d) for d in range(TEAM)]
    lane = lax.broadcasted_iota(jnp.int32, (8, LANES), 1)
    real_lane = lane < BINS
    sign = jnp.where(real_lane, 1.0 / windows, -1.0 / windows)
    tail = extended.shape[1] - planes * span
    if tail:
        extended[:, planes * span :, :] = jnp.zeros((windows, tail, LANES), jnp.float32)

    for n, half in enumerate(halves):

        def pieces(plane):
            own, across = given[each * plane], given[each * plane + 1 + n]
            return own.at[2 * half], own.at[2 * half + 1], across.at[0], across.at[1]

        for d, ref in enumerate(pieces(0)):
            for w in range(windows):
                side[w, d * count : (d + 1) * count, :] = ref[w * count : (w + 1) * count, :].astype(jnp.float32)
        for plane in range(planes):
            for d, ref in enumerate(pieces(plane + 1)):
                start = pl.multiple_of(plane * span + blocks[d] * count, count)
                for w in range(windows):
                    extended[w, pl.ds(start, count), :] = ref[w * count : (w + 1) * count, :].astype(jnp.float32)

        def group(step, carry):
            at = pl.multiple_of(step * 8, 8)
            d = step // (count // 8)
            within = lax.rem(step, count // 8) * 8
            channel = jnp.bitwise_xor(me, d) * count + within
            straight, turned = [], []
            for w in range(windows):
                value = side[w, pl.ds(at, 8), :]
                straight.append(value * (1.0 / windows))
                turned.append(pltpu.roll(value, BINS, 1) * sign)
            for j in range(number):
                place = channel + offsets[first + j] - low * span
                real_part, imag_part = None, None
                for w in range(windows):
                    partner = extended[w, pl.ds(place, 8), :]
                    r, i = straight[w] * partner, turned[w] * partner
                    real_part = r if w == 0 else real_part + r
                    imag_part = i if w == 0 else imag_part + i
                folded = pltpu.roll(jnp.where(real_lane, imag_part, real_part), BINS, 1)
                both = jnp.where(real_lane, real_part, imag_part) + folded
                paired[d, pl.ds(within * pitch + j, 8, stride=pitch), :] = both
            return carry

        lax.fori_loop(0, span // 8, group, 0, unroll=2)
        for d in range(TEAM):
            out = (near if d < 2 else far).at[2 * n + d % 2]
            for k in range(0, count, 2):
                rows = [paired[d, (k + m) * pitch : (k + m) * pitch + number, :] for m in range(2)]
                out[k * number : (k + 2) * number, :] = jnp.concatenate(rows, axis=0).astype(jnp.bfloat16)


def cross(windows, count, halves, first, last, offsets, team_planes):
    span = TEAM * count
    stride = BAND // offsets.shape[0]
    low = (first * stride + 1) // span
    high = (span - 1 + last * stride) // span
    planes = [team_planes[0]] + [team_planes[p] for p in range(low, min(high, len(team_planes) - 1) + 1)]
    given = [c for plane in planes for c in [plane[0]] + [plane[1 + half] for half in halves]]
    number = last - first
    vmem = pl.BlockSpec(memory_space=pltpu.VMEM)
    return pl.pallas_call(
        functools.partial(cross_kernel, windows, count, halves, first, last, low, len(planes) - 1),
        in_specs=[pl.BlockSpec(memory_space=pltpu.SMEM)] + [vmem] * len(given),
        out_specs=[vmem] * 2,
        out_shape=[pltpu.VMEM((2 * len(halves), count * number, LANES), jnp.bfloat16)] * 2,
        scratch_shapes=[
            pltpu.VMEM((windows, span, LANES), jnp.float32),
            pltpu.VMEM((windows, (high - low + 1) * span, LANES), jnp.float32),
            pltpu.VMEM((TEAM, count * (number + 1), LANES), jnp.float32),
        ],
        compiler_params=pltpu.CompilerParams(vmem_limit_bytes=8 * MIB),
        cost_estimate=busy(2.0 * len(halves)),
        name="cross",
    )(offsets, *given)


def lag_sum(given, table, columns):
    me = lax.rem(lax.axis_index("chan"), TEAM)
    total = None
    for d in range(TEAM):
        left = jnp.concatenate([given[h * TEAM + d] for h in range(HALVES)], axis=1)
        term = jnp.dot(left, table[jnp.bitwise_xor(me, d), :, columns], preferred_element_type=jnp.float32)
        total = term if d == 0 else total + term
    return total * (1.0 / math.sqrt(F))


def picked(refs, picks):
    return [refs[n][at] for n, at in picks]


def early_kernel(tile, picks, *refs):
    given, table, out = picked(refs, picks), refs[-2], refs[-1]
    for t in range(LAGS // tile):
        columns = pl.ds(t * tile, tile)
        out[:, columns] = lag_sum(given, table, columns)


def late_kernel(count, tile, picks, *refs):
    given, table, early, out = picked(refs, picks), refs[-3], refs[-2], refs[-1]
    columns = pl.ds(pl.multiple_of(pl.program_id(0) * tile, tile), tile)
    both = [early[:, columns], lag_sum(given, table, columns)]
    both = [v.reshape(count, v.shape[0] // count, tile) for v in both]
    out[...] = jnp.concatenate(both, axis=1).astype(jnp.bfloat16)


def lags_early(arrays, picks, table):
    vmem = pl.BlockSpec(memory_space=pltpu.VMEM)
    return pl.pallas_call(
        functools.partial(early_kernel, 512, picks),
        in_specs=[vmem] * (len(arrays) + 1),
        out_specs=vmem,
        out_shape=pltpu.VMEM((arrays[0].shape[1], LAGS), jnp.float32),
        compiler_params=pltpu.CompilerParams(vmem_limit_bytes=12 * MIB),
        cost_estimate=busy(1.5),
        name="lags_early",
    )(*arrays, table)


def lags_late(arrays, picks, table, early, count, number):
    vmem = pl.BlockSpec(memory_space=pltpu.VMEM)
    tile = 512
    return pl.pallas_call(
        functools.partial(late_kernel, count, tile, picks),
        grid=(LAGS // tile,),
        in_specs=[vmem] * (len(arrays) + 2),
        out_specs=pl.BlockSpec((count, number, tile), lambda i: (0, 0, i)),
        out_shape=jax.ShapeDtypeStruct((count, number, LAGS), jnp.bfloat16),
        compiler_params=pltpu.CompilerParams(vmem_limit_bytes=16 * MIB),
        cost_estimate=busy(2.0),
        name="lags_late",
    )(*arrays, table, early)


def solution(mesh):
    ring = mesh.shape["chan"]
    if ring % TEAM:
        raise ValueError("chan")

    def swapped(value, by):
        return lax.ppermute(value, "chan", [(i, i ^ by) for i in range(ring)])

    def down(value, hops):
        pairs = [(i, i - TEAM) for i in range(TEAM, ring) if i // TEAM + hops - 1 < ring // TEAM]
        return lax.ppermute(value, "chan", pairs)

    def shards(records, live_mask, offsets):
        count, windows, length = records.shape
        span = TEAM * count
        number = offsets.shape[0]
        forward, inverse = tables(length)
        mine, sibling, far0, far1 = spectra(records, live_mask, jnp.asarray(forward))
        inverse = jnp.asarray(inverse)
        near = joined(mine, swapped(sibling, 1))
        across = [swapped(far, 2) for far in (far0, far1)]
        chunks = [[near] + [far_joined(c, swapped(c, 1)) for c in across]]
        reach = min((span + BAND - 2) // span, ring // TEAM - 1)
        for hops in range(1, reach + 1):
            chunks.append([down(c, hops) for c in chunks[-1]])

        def returned(halves, first, last):
            near, far = cross(windows, count, halves, first, last, offsets, chunks)
            back = swapped(far, 2)
            arrays = [near, swapped(near, 1), back, swapped(back, 1)]
            return arrays, [(d, 2 * n + d % 2) for n in range(len(halves)) for d in range(TEAM)]

        middle = number // 2
        arrays, picks = returned((0, 1), 0, middle)
        early = lags_early(arrays, picks, inverse)
        arrays, picks = returned((0,), middle, number)
        more, rest = returned((1,), middle, number)
        picks = picks + [(len(arrays) + n, at) for n, at in rest]
        return lags_late(arrays + more, picks, inverse, early, count, number)

    in_specs = (P(("day", "chan"), None, None), P(("day", "chan")), P())
    out_specs = P(("day", "chan"), None, None)
    return jax.shard_map(shards, mesh=mesh, in_specs=in_specs, out_specs=out_specs, check_vma=False)
```

time: 74.9 us -> 65.2 us (0.87)
  starting transfers between devices: 26.8 us -> 19.6 us
  local copies, waits for them, and re-layouts: 3.47 us -> 0.01 us
  waiting for transfers between devices: 25.4 us -> 27.6 us
  Pallas kernels: 18.5 us -> 17.4 us
    ppermute x12 -> x9, starting transfers between devices: 15.4 us -> 11.6 us  [down(): return lax.ppermute(value, 'chan', pairs)]
    unnamed x10 -> x4, local copies, waits for them, and re-layouts: 3.47 us -> 0.01 us
    ppermute x30 -> x14, starting transfers between devices: 11.4 us -> 8.07 us  [swapped(): return lax.ppermute(value, 'chan', [(i, i ^ by) for i in range(ring)])]
    ppermute x30 -> x14, waiting for transfers between devices: 8.45 us -> 10.1 us  [swapped(): return lax.ppermute(value, 'chan', [(i, i ^ by) for i in range(ring)])]
    ppermute x12 -> x9, waiting for transfers between devices: 16.9 us -> 17.5 us  [down(): return lax.ppermute(value, 'chan', pairs)]
    pallas_call x6 -> x8, Pallas kernels: 13.9 us -> 13.4 us  [the longest x3 9.11 us: cross(): pl.pallas_call(functools.partial(cross_kernel, windows, count, halves, fi...]
  transfers between devices with their start and end apart: 42 -> 23, of which waited for: 13 -> 10; matrix products, arithmetic and copies ran while one was open for 0% -> 0% of each run, Pallas kernels for 15% -> 16%
where the time goes in v3:
time: 65.2 us; the launch traced here: 64.9 us
  waiting for transfers between devices  27.6 us (42%)
  starting transfers between devices  19.6 us (30%)
  Pallas kernels  17.4 us (27%)
    ppermute x9, waiting for transfers between devices, down(): return lax.ppermute(value, 'chan', pairs)  17.5 us
    ppermute x9, starting transfers between devices, down(): return lax.ppermute(value, 'chan', pairs)  11.6 us
    ppermute x14, waiting for transfers between devices, swapped(): return lax.ppermute(value, 'chan', [(i, i ^ by) for i in range(ring)])  10.1 us
    pallas_call x3, Pallas kernels, cross(): pl.pallas_call(functools.partial(cross_kernel, windows, count, halves, fi...  9.11 us
    ppermute x14, starting transfers between devices, swapped(): return lax.ppermute(value, 'chan', [(i, i ^ by) for i in range(ring)])  8.07 us
    pallas_call x1, Pallas kernels, spectra(): pl.pallas_call(functools.partial(spectra_kernel, windows), in_specs=[pl.B...  4.08 us
    pallas_call x1, Pallas kernels, lags_late(): pl.pallas_call(functools.partial(late_kernel, count, tile, picks), grid=(...  2.95 us
  transfers between devices with their start and end apart: 23, of which 10 were waited for; matrix products, arithmetic and copies ran while one was open for 0% of the time, Pallas kernels for 16%

profile of v3, /device:TPU:0, one launch (start us, length us, event | category | flops | bytes accessed | tf_op | source)
XLA Modules:
  0.0 64.9 jit_solution(14317430611730440376)
XLA Ops:
  0.0 4.1 %spectra.1 = (bf16[2,256,128]{2,1,0:T(8,128)(2,1)S(1)}, bf16[2,256,128]{2,1,0:T(8,128)(2,1)S(1)}, bf16[2,256,128]{2,1,0:T(8,128)(2,1)S(1)}, bf16[2,256,128]{2,1,0:T(8,128)(2,1)S(1)}) custom-call(bf16[256,3000]{1,0:T(8,128)(2,1)} %bitcast.2, bf16[2,750,512]{2,1,0:T(8,128)(2,1)} %constant.4.clone.table_hbm, s32[1,32]{1,0:T(1,128)} %bitcast.3), custom_call_target="tpu_custom_call" | custom-call | flops 3460499968 | tf_op jit(solution)/shard_map/spectra/pallas_call | solution.py:117
  4.6 2.6 %collective-permute-start.12 = (bf16[2,256,128]{2,1,0:T(8,128)(2,1)S(1)}, bf16[2,256,128]{2,1,0:T(8,128)(2,1)S(1)}, u32[]{:S(2)}, u32[]{:S(2)}) collective-permute-start(bf16[2,256,128]{2,1,0:T(8,128)(2,1)S(1)} %get-tuple-element.20), channel_id=1, source_target_pairs={{0,2},{1,3},{2,0},{3,1},{4,6},{5,7},{6,4},{7,5},{8,10},{9,11},{10,... | collective-permute-start | bytes 393224 | tf_op jit(solution)/shard_map/ppermute | solution.py:326
  7.3 1.3 %collective-permute-start.3 = (bf16[4,256,128]{2,1,0:T(8,128)(2,1)S(1)}, bf16[4,256,128]{2,1,0:T(8,128)(2,1)S(1)}, u32[]{:S(2)}, u32[]{:S(2)}) collective-permute-start(bf16[4,256,128]{2,1,0:T(8,128)(2,1)S(1)} %joined.1.refs_0_.refs_3_), channel_id=1, source_target_pairs={{4,0},{5,1},{6,2},{7,3},{8,4},{9,5},{10,6},{11,7},{12,8},{13,9},{1... | collective-permute-start | bytes 786440 | tf_op jit(solution)/shard_map/ppermute | solution.py:330
  8.6 2.9 %collective-permute-done.12.straight = bf16[2,256,128]{2,1,0:T(8,128)(2,1)S(1)} collective-permute-done((bf16[2,256,128]{2,1,0:T(8,128)(2,1)S(1)}, bf16[2,256,128]{2,1,0:T(8,128)(2,1)S(1)}, u32[]{:S(2)}, u32[]{:S(2)}) %collective-permute-start.12) | collective-permute-done | bytes 131104 | tf_op jit(solution)/shard_map/ppermute | solution.py:326
  11.6 2.5 %collective-permute-done.1.straight = bf16[2,256,128]{2,1,0:T(8,128)(2,1)S(1)} collective-permute-done((bf16[2,256,128]{2,1,0:T(8,128)(2,1)S(1)}, bf16[2,256,128]{2,1,0:T(8,128)(2,1)S(1)}, u32[]{:S(2)}, u32[]{:S(2)}) %collective-permute-start.1) | collective-permute-done | bytes 131104 | tf_op jit(solution)/shard_map/ppermute | solution.py:326
  14.1 1.3 %collective-permute-start.14 = (bf16[2,256,128]{2,1,0:T(8,128)(2,1)S(1)}, bf16[2,256,128]{2,1,0:T(8,128)(2,1)S(1)}, u32[]{:S(2)}, u32[]{:S(2)}) collective-permute-start(bf16[2,256,128]{2,1,0:T(8,128)(2,1)S(1)} %far_joined.3.refs_1_.refs_2_.refs_5_), channel_id=1, source_target_pairs={{4,0},{5,1},{6,2},{7,3},{8,4},{9,5},{10,6},{11,7},{12,8},{13,9},{1... | collective-permute-start | bytes 393224 | tf_op jit(solution)/shard_map/ppermute | solution.py:330
  15.5 2.1 %collective-permute-done.3.refs_6_ = bf16[4,256,128]{2,1,0:T(8,128)(2,1)S(1)} collective-permute-done((bf16[4,256,128]{2,1,0:T(8,128)(2,1)S(1)}, bf16[4,256,128]{2,1,0:T(8,128)(2,1)S(1)}, u32[]{:S(2)}, u32[]{:S(2)}) %collective-permute-start.3) | collective-permute-done | bytes 262176 | tf_op jit(solution)/shard_map/ppermute | solution.py:330
  17.6 1.3 %collective-permute-start.4 = (bf16[4,256,128]{2,1,0:T(8,128)(2,1)S(1)}, bf16[4,256,128]{2,1,0:T(8,128)(2,1)S(1)}, u32[]{:S(2)}, u32[]{:S(2)}) collective-permute-start(bf16[4,256,128]{2,1,0:T(8,128)(2,1)S(1)} %collective-permute-done.3.refs_6_), channel_id=1, source_target_pairs={{4,0},{5,1},{6,2},{7,3},{8,4},{9,5},{10,6},{11,7},{20,16},{21,17},... | collective-permute-start | bytes 786440 | tf_op jit(solution)/shard_map/ppermute | solution.py:330
  18.9 1.3 %collective-permute-start.5 = (bf16[2,256,128]{2,1,0:T(8,128)(2,1)S(1)}, bf16[2,256,128]{2,1,0:T(8,128)(2,1)S(1)}, u32[]{:S(2)}, u32[]{:S(2)}) collective-permute-start(bf16[2,256,128]{2,1,0:T(8,128)(2,1)S(1)} %far_joined.2.refs_1_.refs_4_), channel_id=1, source_target_pairs={{4,0},{5,1},{6,2},{7,3},{8,4},{9,5},{10,6},{11,7},{12,8},{13,9},{1... | collective-permute-start | bytes 393224 | tf_op jit(solution)/shard_map/ppermute | solution.py:330
  20.2 2.1 %collective-permute-done.14.refs_8_ = bf16[2,256,128]{2,1,0:T(8,128)(2,1)S(1)} collective-permute-done((bf16[2,256,128]{2,1,0:T(8,128)(2,1)S(1)}, bf16[2,256,128]{2,1,0:T(8,128)(2,1)S(1)}, u32[]{:S(2)}, u32[]{:S(2)}) %collective-permute-start.14) | collective-permute-done | bytes 131104 | tf_op jit(solution)/shard_map/ppermute | solution.py:330
  22.3 1.3 %collective-permute-start.15 = (bf16[2,256,128]{2,1,0:T(8,128)(2,1)S(1)}, bf16[2,256,128]{2,1,0:T(8,128)(2,1)S(1)}, u32[]{:S(2)}, u32[]{:S(2)}) collective-permute-start(bf16[2,256,128]{2,1,0:T(8,128)(2,1)S(1)} %collective-permute-done.14.refs_8_), channel_id=1, source_target_pairs={{4,0},{5,1},{6,2},{7,3},{8,4},{9,5},{10,6},{11,7},{20,16},{21,17},... | collective-permute-start | bytes 393224 | tf_op jit(solution)/shard_map/ppermute | solution.py:330
  23.6 7.9 %collective-permute-done.5.refs_7_ = bf16[2,256,128]{2,1,0:T(8,128)(2,1)S(1)} collective-permute-done((bf16[2,256,128]{2,1,0:T(8,128)(2,1)S(1)}, bf16[2,256,128]{2,1,0:T(8,128)(2,1)S(1)}, u32[]{:S(2)}, u32[]{:S(2)}) %collective-permute-start.5) | collective-permute-done | bytes 131104 | tf_op jit(solution)/shard_map/ppermute | solution.py:330
  31.5 1.3 %collective-permute-start.6 = (bf16[2,256,128]{2,1,0:T(8,128)(2,1)S(1)}, bf16[2,256,128]{2,1,0:T(8,128)(2,1)S(1)}, u32[]{:S(2)}, u32[]{:S(2)}) collective-permute-start(bf16[2,256,128]{2,1,0:T(8,128)(2,1)S(1)} %collective-permute-done.5.refs_7_), channel_id=1, source_target_pairs={{4,0},{5,1},{6,2},{7,3},{8,4},{9,5},{10,6},{11,7},{20,16},{21,17},... | collective-permute-start | bytes 393224 | tf_op jit(solution)/shard_map/ppermute | solution.py:330
  33.2 1.3 %collective-permute-start.16 = (bf16[2,256,128]{2,1,0:T(8,128)(2,1)S(1)}, bf16[2,256,128]{2,1,0:T(8,128)(2,1)S(1)}, u32[]{:S(2)}, u32[]{:S(2)}) collective-permute-start(bf16[2,256,128]{2,1,0:T(8,128)(2,1)S(1)} %collective-permute-done.15.refs_3_.refs_11_), channel_id=1, source_target_pairs={{4,0},{5,1},{6,2},{7,3},{20,16},{21,17},{22,18},{23,19}} | collective-permute-start | bytes 393224 | tf_op jit(solution)/shard_map/ppermute | solution.py:330
  34.5 1.3 %collective-permute-start.7 = (bf16[4,256,128]{2,1,0:T(8,128)(2,1)S(1)}, bf16[4,256,128]{2,1,0:T(8,128)(2,1)S(1)}, u32[]{:S(2)}, u32[]{:S(2)}) collective-permute-start(bf16[4,256,128]{2,1,0:T(8,128)(2,1)S(1)} %collective-permute-done.4.refs_2_.refs_9_), channel_id=1, source_target_pairs={{4,0},{5,1},{6,2},{7,3},{20,16},{21,17},{22,18},{23,19}} | collective-permute-start | bytes 786440 | tf_op jit(solution)/shard_map/ppermute | solution.py:330
  35.8 3.9 %collective-permute-done.6.refs_3_.refs_10_ = bf16[2,256,128]{2,1,0:T(8,128)(2,1)S(1)} collective-permute-done((bf16[2,256,128]{2,1,0:T(8,128)(2,1)S(1)}, bf16[2,256,128]{2,1,0:T(8,128)(2,1)S(1)}, u32[]{:S(2)}, u32[]{:S(2)}) %collective-permute-start.6) | collective-permute-done | bytes 131104 | tf_op jit(solution)/shard_map/ppermute | solution.py:330
  39.8 4.3 %cross.5 = (bf16[4,256,128]{2,1,0:T(8,128)(2,1)S(1)}, bf16[4,256,128]{2,1,0:T(8,128)(2,1)S(1)}) custom-call(s32[16]{0:T(128)S(1)} %copy-done.1, bf16[4,256,128]{2,1,0:T(8,128)(2,1)S(1)} %joined.1.refs_0_.refs_3_, bf16[2,256,128]{2,1,0:T(8,128)(2,1)S(1)} %far_joined.2.refs_1_.refs_4_, bf16[2,256,128]{2,1,0:T(8,128)(2,1)S(1)} %far_joined.3.refs_1_.refs_2_.refs_5_, ...), custom_call_target="tpu_custom_call" | custom-call | flops 4614000128 | tf_op jit(solution)/shard_map/cross/pallas_call | solution.py:247
  44.1 1.7 %collective-permute-start.21 = (bf16[4,256,128]{2,1,0:T(8,128)(2,1)S(1)}, bf16[4,256,128]{2,1,0:T(8,128)(2,1)S(1)}, u32[]{:S(2)}, u32[]{:S(2)}) collective-permute-start(bf16[4,256,128]{2,1,0:T(8,128)(2,1)S(1)} %get-tuple-element.24), channel_id=1, source_target_pairs={{0,2},{1,3},{2,0},{3,1},{4,6},{5,7},{6,4},{7,5},{8,10},{9,11},{10,... | collective-permute-start | bytes 786440 | tf_op jit(solution)/shard_map/ppermute | solution.py:326
  45.8 1.3 %collective-permute-start.8 = (bf16[2,256,128]{2,1,0:T(8,128)(2,1)S(1)}, bf16[2,256,128]{2,1,0:T(8,128)(2,1)S(1)}, u32[]{:S(2)}, u32[]{:S(2)}) collective-permute-start(bf16[2,256,128]{2,1,0:T(8,128)(2,1)S(1)} %collective-permute-done.6.refs_3_.refs_10_), channel_id=1, source_target_pairs={{4,0},{5,1},{6,2},{7,3},{20,16},{21,17},{22,18},{23,19}} | collective-permute-start | bytes 393224 | tf_op jit(solution)/shard_map/ppermute | solution.py:330
  47.7 2.4 %cross.4 = (bf16[2,256,128]{2,1,0:T(8,128)(2,1)S(1)}, bf16[2,256,128]{2,1,0:T(8,128)(2,1)S(1)}) custom-call(s32[16]{0:T(128)S(1)} %copy-done.1, bf16[4,256,128]{2,1,0:T(8,128)(2,1)S(1)} %joined.1.refs_0_.refs_3_, bf16[2,256,128]{2,1,0:T(8,128)(2,1)S(1)} %far_joined.3.refs_1_.refs_2_.refs_5_, bf16[4,256,128]{2,1,0:T(8,128)(2,1)S(1)} %collective-permute-done.4.refs_2_.refs_9_, ...), custom_call_target="tpu_custom_call" | custom-call | flops 2307000064 | tf_op jit(solution)/shard_map/cross/pallas_call | solution.py:247
  50.1 2.0 %collective-permute-start.18 = (bf16[2,256,128]{2,1,0:T(8,128)(2,1)S(1)}, bf16[2,256,128]{2,1,0:T(8,128)(2,1)S(1)}, u32[]{:S(2)}, u32[]{:S(2)}) collective-permute-start(bf16[2,256,128]{2,1,0:T(8,128)(2,1)S(1)} %get-tuple-element.22), channel_id=1, source_target_pairs={{0,2},{1,3},{2,0},{3,1},{4,6},{5,7},{6,4},{7,5},{8,10},{9,11},{10,... | collective-permute-start | bytes 393224 | tf_op jit(solution)/shard_map/ppermute | solution.py:326
  52.6 2.4 %cross.3 = (bf16[2,256,128]{2,1,0:T(8,128)(2,1)S(1)}, bf16[2,256,128]{2,1,0:T(8,128)(2,1)S(1)}) custom-call(s32[16]{0:T(128)S(1)} %copy-done.1, bf16[4,256,128]{2,1,0:T(8,128)(2,1)S(1)} %joined.1.refs_0_.refs_3_, bf16[2,256,128]{2,1,0:T(8,128)(2,1)S(1)} %far_joined.2.refs_1_.refs_4_, bf16[4,256,128]{2,1,0:T(8,128)(2,1)S(1)} %collective-permute-done.4.refs_2_.refs_9_, ...), custom_call_target="tpu_custom_call" | custom-call | flops 2307000064 | tf_op jit(solution)/shard_map/cross/pallas_call | solution.py:247
  56.1 4.5 %collective-permute-done.10.refs_2_ = bf16[2,256,128]{2,1,0:T(8,128)(2,1)S(1)} collective-permute-done((bf16[2,256,128]{2,1,0:T(8,128)(2,1)S(1)}, bf16[2,256,128]{2,1,0:T(8,128)(2,1)S(1)}, u32[]{:S(2)}, u32[]{:S(2)}) %collective-permute-start.10) | collective-permute-done | bytes 131104 | tf_op jit(solution)/shard_map/ppermute | solution.py:326
  61.9 3.0 %lags_late.1 = bf16[32,16,2048]{2,1,0:T(8,128)(2,1)} custom-call(bf16[2,256,128]{2,1,0:T(8,128)(2,1)S(1)} %get-tuple-element.18.refs_0_, bf16[2,256,128]{2,1,0:T(8,128)(2,1)S(1)} %collective-permute-done.9.refs_1_, bf16[2,256,128]{2,1,0:T(8,128)(2,1)S(1)} %collective-permute-done.10.refs_2_, bf16[2,256,128]{2,1,0:T(8,128)(2,1)S(1)} %collective-permute-done.11.refs_3_, ...), custom_call_target="tpu_custom_call" | custom-call | flops 2307000064 | tf_op jit(solution)/shard_map/lags_late/pallas_call | solution.py:308
  (35 shorter events, 4.5 us)
Async XLA Ops:
  4.1 35.7 %copy-start.1 = (s32[16]{0:T(128)S(1)}, s32[16]{0:T(128)}, u32[]{:S(2)}) copy-start(s32[16]{0:T(128)} %offsets.5) | copy-start | bytes 196
  4.1 3.2 %collective-permute-start = (bf16[2,256,128]{2,1,0:T(8,128)(2,1)S(1)}, bf16[2,256,128]{2,1,0:T(8,128)(2,1)S(1)}, u32[]{:S(2)}, u32[]{:S(2)}) collective-permute-start(bf16[2,256,128]{2,1,0:T(8,128)(2,1)S(1)} %get-tuple-element.16), channel_id=1, source_target_pairs={{0,1},{1,0},{2,3},{3,2},{4,5},{5,4},{6,7},{7,6},{8,9},{9,8},{10,11... | collective-permute-start | bytes 393224 | tf_op jit(solution)/shard_map/ppermute | solution.py:326
  4.6 6.9 %collective-permute-start.12 = (bf16[2,256,128]{2,1,0:T(8,128)(2,1)S(1)}, bf16[2,256,128]{2,1,0:T(8,128)(2,1)S(1)}, u32[]{:S(2)}, u32[]{:S(2)}) collective-permute-start(bf16[2,256,128]{2,1,0:T(8,128)(2,1)S(1)} %get-tuple-element.20), channel_id=1, source_target_pairs={{0,2},{1,3},{2,0},{3,1},{4,6},{5,7},{6,4},{7,5},{8,10},{9,11},{10,... | collective-permute-start | bytes 393224 | tf_op jit(solution)/shard_map/ppermute | solution.py:326
  7.2 6.9 %collective-permute-start.1 = (bf16[2,256,128]{2,1,0:T(8,128)(2,1)S(1)}, bf16[2,256,128]{2,1,0:T(8,128)(2,1)S(1)}, u32[]{:S(2)}, u32[]{:S(2)}) collective-permute-start(bf16[2,256,128]{2,1,0:T(8,128)(2,1)S(1)} %get-tuple-element.17), channel_id=1, source_target_pairs={{0,2},{1,3},{2,0},{3,1},{4,6},{5,7},{6,4},{7,5},{8,10},{9,11},{10,... | collective-permute-start | bytes 393224 | tf_op jit(solution)/shard_map/ppermute | solution.py:326
  7.3 10.2 %collective-permute-start.3 = (bf16[4,256,128]{2,1,0:T(8,128)(2,1)S(1)}, bf16[4,256,128]{2,1,0:T(8,128)(2,1)S(1)}, u32[]{:S(2)}, u32[]{:S(2)}) collective-permute-start(bf16[4,256,128]{2,1,0:T(8,128)(2,1)S(1)} %joined.1.refs_0_.refs_3_), channel_id=1, source_target_pairs={{4,0},{5,1},{6,2},{7,3},{8,4},{9,5},{10,6},{11,7},{12,8},{13,9},{1... | collective-permute-start | bytes 786440 | tf_op jit(solution)/shard_map/ppermute | solution.py:330
  11.6 2.6 %collective-permute-start.13 = (bf16[2,256,128]{2,1,0:T(8,128)(2,1)S(1)}, bf16[2,256,128]{2,1,0:T(8,128)(2,1)S(1)}, u32[]{:S(2)}, u32[]{:S(2)}) collective-permute-start(bf16[2,256,128]{2,1,0:T(8,128)(2,1)S(1)} %collective-permute-done.12.straight), channel_id=1, source_target_pairs={{0,1},{1,0},{2,3},{3,2},{4,5},{5,4},{6,7},{7,6},{8,9},{9,8},{10,11... | collective-permute-start | bytes 393224 | tf_op jit(solution)/shard_map/ppermute | solution.py:326
  14.1 1.3 %collective-permute-start.2 = (bf16[2,256,128]{2,1,0:T(8,128)(2,1)S(1)}, bf16[2,256,128]{2,1,0:T(8,128)(2,1)S(1)}, u32[]{:S(2)}, u32[]{:S(2)}) collective-permute-start(bf16[2,256,128]{2,1,0:T(8,128)(2,1)S(1)} %collective-permute-done.1.straight), channel_id=1, source_target_pairs={{0,1},{1,0},{2,3},{3,2},{4,5},{5,4},{6,7},{7,6},{8,9},{9,8},{10,11... | collective-permute-start | bytes 393224 | tf_op jit(solution)/shard_map/ppermute | solution.py:326
  14.1 8.2 %collective-permute-start.14 = (bf16[2,256,128]{2,1,0:T(8,128)(2,1)S(1)}, bf16[2,256,128]{2,1,0:T(8,128)(2,1)S(1)}, u32[]{:S(2)}, u32[]{:S(2)}) collective-permute-start(bf16[2,256,128]{2,1,0:T(8,128)(2,1)S(1)} %far_joined.3.refs_1_.refs_2_.refs_5_), channel_id=1, source_target_pairs={{4,0},{5,1},{6,2},{7,3},{8,4},{9,5},{10,6},{11,7},{12,8},{13,9},{1... | collective-permute-start | bytes 393224 | tf_op jit(solution)/shard_map/ppermute | solution.py:330
  17.6 17.0 %collective-permute-start.4 = (bf16[4,256,128]{2,1,0:T(8,128)(2,1)S(1)}, bf16[4,256,128]{2,1,0:T(8,128)(2,1)S(1)}, u32[]{:S(2)}, u32[]{:S(2)}) collective-permute-start(bf16[4,256,128]{2,1,0:T(8,128)(2,1)S(1)} %collective-permute-done.3.refs_6_), channel_id=1, source_target_pairs={{4,0},{5,1},{6,2},{7,3},{8,4},{9,5},{10,6},{11,7},{20,16},{21,17},... | collective-permute-start | bytes 786440 | tf_op jit(solution)/shard_map/ppermute | solution.py:330
  18.9 12.6 %collective-permute-start.5 = (bf16[2,256,128]{2,1,0:T(8,128)(2,1)S(1)}, bf16[2,256,128]{2,1,0:T(8,128)(2,1)S(1)}, u32[]{:S(2)}, u32[]{:S(2)}) collective-permute-start(bf16[2,256,128]{2,1,0:T(8,128)(2,1)S(1)} %far_joined.2.refs_1_.refs_4_), channel_id=1, source_target_pairs={{4,0},{5,1},{6,2},{7,3},{8,4},{9,5},{10,6},{11,7},{12,8},{13,9},{1... | collective-permute-start | bytes 393224 | tf_op jit(solution)/shard_map/ppermute | solution.py:330
  22.3 10.9 %collective-permute-start.15 = (bf16[2,256,128]{2,1,0:T(8,128)(2,1)S(1)}, bf16[2,256,128]{2,1,0:T(8,128)(2,1)S(1)}, u32[]{:S(2)}, u32[]{:S(2)}) collective-permute-start(bf16[2,256,128]{2,1,0:T(8,128)(2,1)S(1)} %collective-permute-done.14.refs_8_), channel_id=1, source_target_pairs={{4,0},{5,1},{6,2},{7,3},{8,4},{9,5},{10,6},{11,7},{20,16},{21,17},... | collective-permute-start | bytes 393224 | tf_op jit(solution)/shard_map/ppermute | solution.py:330
  31.5 8.3 %collective-permute-start.6 = (bf16[2,256,128]{2,1,0:T(8,128)(2,1)S(1)}, bf16[2,256,128]{2,1,0:T(8,128)(2,1)S(1)}, u32[]{:S(2)}, u32[]{:S(2)}) collective-permute-start(bf16[2,256,128]{2,1,0:T(8,128)(2,1)S(1)} %collective-permute-done.5.refs_7_), channel_id=1, source_target_pairs={{4,0},{5,1},{6,2},{7,3},{8,4},{9,5},{10,6},{11,7},{20,16},{21,17},... | collective-permute-start | bytes 393224 | tf_op jit(solution)/shard_map/ppermute | solution.py:330
  33.2 13.9 %collective-permute-start.16 = (bf16[2,256,128]{2,1,0:T(8,128)(2,1)S(1)}, bf16[2,256,128]{2,1,0:T(8,128)(2,1)S(1)}, u32[]{:S(2)}, u32[]{:S(2)}) collective-permute-start(bf16[2,256,128]{2,1,0:T(8,128)(2,1)S(1)} %collective-permute-done.15.refs_3_.refs_11_), channel_id=1, source_target_pairs={{4,0},{5,1},{6,2},{7,3},{20,16},{21,17},{22,18},{23,19}} | collective-permute-start | bytes 393224 | tf_op jit(solution)/shard_map/ppermute | solution.py:330
  34.5 13.2 %collective-permute-start.7 = (bf16[4,256,128]{2,1,0:T(8,128)(2,1)S(1)}, bf16[4,256,128]{2,1,0:T(8,128)(2,1)S(1)}, u32[]{:S(2)}, u32[]{:S(2)}) collective-permute-start(bf16[4,256,128]{2,1,0:T(8,128)(2,1)S(1)} %collective-permute-done.4.refs_2_.refs_9_), channel_id=1, source_target_pairs={{4,0},{5,1},{6,2},{7,3},{20,16},{21,17},{22,18},{23,19}} | collective-permute-start | bytes 786440 | tf_op jit(solution)/shard_map/ppermute | solution.py:330
  44.1 8.1 %collective-permute-start.21 = (bf16[4,256,128]{2,1,0:T(8,128)(2,1)S(1)}, bf16[4,256,128]{2,1,0:T(8,128)(2,1)S(1)}, u32[]{:S(2)}, u32[]{:S(2)}) collective-permute-start(bf16[4,256,128]{2,1,0:T(8,128)(2,1)S(1)} %get-tuple-element.24), channel_id=1, source_target_pairs={{0,2},{1,3},{2,0},{3,1},{4,6},{5,7},{6,4},{7,5},{8,10},{9,11},{10,... | collective-permute-start | bytes 786440 | tf_op jit(solution)/shard_map/ppermute | solution.py:326
  45.8 6.8 %collective-permute-start.8 = (bf16[2,256,128]{2,1,0:T(8,128)(2,1)S(1)}, bf16[2,256,128]{2,1,0:T(8,128)(2,1)S(1)}, u32[]{:S(2)}, u32[]{:S(2)}) collective-permute-start(bf16[2,256,128]{2,1,0:T(8,128)(2,1)S(1)} %collective-permute-done.6.refs_3_.refs_10_), channel_id=1, source_target_pairs={{4,0},{5,1},{6,2},{7,3},{20,16},{21,17},{22,18},{23,19}} | collective-permute-start | bytes 393224 | tf_op jit(solution)/shard_map/ppermute | solution.py:330
  47.1 8.4 %collective-permute-start.20 = (bf16[4,256,128]{2,1,0:T(8,128)(2,1)S(1)}, bf16[4,256,128]{2,1,0:T(8,128)(2,1)S(1)}, u32[]{:S(2)}, u32[]{:S(2)}) collective-permute-start(bf16[4,256,128]{2,1,0:T(8,128)(2,1)S(1)} %get-tuple-element.23.refs_0_), channel_id=1, source_target_pairs={{0,1},{1,0},{2,3},{3,2},{4,5},{5,4},{6,7},{7,6},{8,9},{9,8},{10,11... | collective-permute-start | bytes 786440 | tf_op jit(solution)/shard_map/ppermute | solution.py:326
  50.1 5.9 %collective-permute-start.18 = (bf16[2,256,128]{2,1,0:T(8,128)(2,1)S(1)}, bf16[2,256,128]{2,1,0:T(8,128)(2,1)S(1)}, u32[]{:S(2)}, u32[]{:S(2)}) collective-permute-start(bf16[2,256,128]{2,1,0:T(8,128)(2,1)S(1)} %get-tuple-element.22), channel_id=1, source_target_pairs={{0,2},{1,3},{2,0},{3,1},{4,6},{5,7},{6,4},{7,5},{8,10},{9,11},{10,... | collective-permute-start | bytes 393224 | tf_op jit(solution)/shard_map/ppermute | solution.py:326
  52.2 8.4 %collective-permute-start.22 = (bf16[4,256,128]{2,1,0:T(8,128)(2,1)S(1)}, bf16[4,256,128]{2,1,0:T(8,128)(2,1)S(1)}, u32[]{:S(2)}, u32[]{:S(2)}) collective-permute-start(bf16[4,256,128]{2,1,0:T(8,128)(2,1)S(1)} %collective-permute-done.21.refs_2_), channel_id=1, source_target_pairs={{0,1},{1,0},{2,3},{3,2},{4,5},{5,4},{6,7},{7,6},{8,9},{9,8},{10,11... | collective-permute-start | bytes 786440 | tf_op jit(solution)/shard_map/ppermute | solution.py:326
  55.1 5.5 %collective-permute-start.10 = (bf16[2,256,128]{2,1,0:T(8,128)(2,1)S(1)}, bf16[2,256,128]{2,1,0:T(8,128)(2,1)S(1)}, u32[]{:S(2)}, u32[]{:S(2)}) collective-permute-start(bf16[2,256,128]{2,1,0:T(8,128)(2,1)S(1)} %get-tuple-element.19), channel_id=1, source_target_pairs={{0,2},{1,3},{2,0},{3,1},{4,6},{5,7},{6,4},{7,5},{8,10},{9,11},{10,... | collective-permute-start | bytes 393224 | tf_op jit(solution)/shard_map/ppermute | solution.py:326
  55.5 6.4 %collective-permute-start.17 = (bf16[2,256,128]{2,1,0:T(8,128)(2,1)S(1)}, bf16[2,256,128]{2,1,0:T(8,128)(2,1)S(1)}, u32[]{:S(2)}, u32[]{:S(2)}) collective-permute-start(bf16[2,256,128]{2,1,0:T(8,128)(2,1)S(1)} %get-tuple-element.21.refs_4_), channel_id=1, source_target_pairs={{0,1},{1,0},{2,3},{3,2},{4,5},{5,4},{6,7},{7,6},{8,9},{9,8},{10,11... | collective-permute-start | bytes 393224 | tf_op jit(solution)/shard_map/ppermute | solution.py:326
  55.5 6.4 %collective-permute-start.9 = (bf16[2,256,128]{2,1,0:T(8,128)(2,1)S(1)}, bf16[2,256,128]{2,1,0:T(8,128)(2,1)S(1)}, u32[]{:S(2)}, u32[]{:S(2)}) collective-permute-start(bf16[2,256,128]{2,1,0:T(8,128)(2,1)S(1)} %get-tuple-element.18.refs_0_), channel_id=1, source_target_pairs={{0,1},{1,0},{2,3},{3,2},{4,5},{5,4},{6,7},{7,6},{8,9},{9,8},{10,11... | collective-permute-start | bytes 393224 | tf_op jit(solution)/shard_map/ppermute | solution.py:326
  56.0 5.9 %collective-permute-start.19 = (bf16[2,256,128]{2,1,0:T(8,128)(2,1)S(1)}, bf16[2,256,128]{2,1,0:T(8,128)(2,1)S(1)}, u32[]{:S(2)}, u32[]{:S(2)}) collective-permute-start(bf16[2,256,128]{2,1,0:T(8,128)(2,1)S(1)} %collective-permute-done.18.refs_6_), channel_id=1, source_target_pairs={{0,1},{1,0},{2,3},{3,2},{4,5},{5,4},{6,7},{7,6},{8,9},{9,8},{10,11... | collective-permute-start | bytes 393224 | tf_op jit(solution)/shard_map/ppermute | solution.py:326
  60.6 1.3 %collective-permute-start.11 = (bf16[2,256,128]{2,1,0:T(8,128)(2,1)S(1)}, bf16[2,256,128]{2,1,0:T(8,128)(2,1)S(1)}, u32[]{:S(2)}, u32[]{:S(2)}) collective-permute-start(bf16[2,256,128]{2,1,0:T(8,128)(2,1)S(1)} %collective-permute-done.10.refs_2_), channel_id=1, source_target_pairs={{0,1},{1,0},{2,3},{3,2},{4,5},{5,4},{6,7},{7,6},{8,9},{9,8},{10,11... | collective-permute-start | bytes 393224 | tf_op jit(solution)/shard_map/ppermute | solution.py:326
  (1 other events, 10.5 us)

commit v4 on v3

--- a/solution.py
+++ b/solution.py
@@ -21,6 +21,7 @@
 QUADRANTS = 4
 
 MIB = 1024 * 1024
+JOIN = 2
 
 
 def busy(microseconds):
@@ -48,7 +49,7 @@
     forward = forward.reshape(part, 2, F).transpose(1, 0, 2)
     shifts = np.arange(LAGS, dtype=np.int64) - LAGS // 2
     inverse = np.concatenate(cut(freqs[:, None] * shifts[None, :]), axis=0)[order]
-    inverse = inverse.reshape(TEAM, 2 * F // TEAM, LAGS)
+    inverse = inverse.reshape(TEAM, HALVES, LANES, LAGS).transpose(1, 0, 2, 3).reshape(HALVES, TEAM // 2, 2 * LANES, LAGS)
     return forward.astype(ml_dtypes.bfloat16), inverse.astype(ml_dtypes.bfloat16)
 
 
@@ -156,6 +157,25 @@
     )(first, second)
 
 
+def team_kernel(half, near, far, out):
+    for d in range(2):
+        out[d] = near[2 * half + d]
+        out[2 + d] = far[d]
+
+
+def team_joined(half, near, far):
+    vmem = pl.BlockSpec(memory_space=pltpu.VMEM)
+    return pl.pallas_call(
+        functools.partial(team_kernel, half),
+        in_specs=[vmem] * 2,
+        out_specs=vmem,
+        out_shape=pltpu.VMEM((TEAM,) + far.shape[1:], far.dtype),
+        compiler_params=pltpu.CompilerParams(vmem_limit_bytes=2 * MIB),
+        cost_estimate=busy(0.3),
+        name="team_joined",
+    )(near, far)
+
+
 def far_kernel(straight, crossed, out):
     out[0] = straight[0]
     out[1] = crossed[1]
@@ -174,9 +194,16 @@
     )(straight, crossed)
 
 
-def cross_kernel(windows, count, halves, first, last, low, planes, offsets, *refs):
-    each = 1 + len(halves)
-    given, (near, far, side, extended, paired) = refs[: each * (planes + 1)], refs[each * (planes + 1) :]
+def cross_kernel(windows, count, halves, sizes, first, last, low, planes, offsets, *refs):
+    near, far, side, extended, paired = refs[-5:]
+    given = list(refs[:-5])
+    pieces = []
+    for size in sizes:
+        arrays, given = given[:size], given[size:]
+        if size == len(halves):
+            pieces.append([[a.at[d] for d in range(TEAM)] for a in arrays])
+        else:
+            pieces.append([[arrays[0].at[2 * h + d] for d in range(2)] + [a.at[d] for d in range(2)] for h, a in zip(halves, arrays[1:])])
     me = lax.rem(lax.axis_index("chan"), TEAM)
     span = TEAM * count
     number = last - first
@@ -189,17 +216,12 @@
     if tail:
         extended[:, planes * span :, :] = jnp.zeros((windows, tail, LANES), jnp.float32)
 
-    for n, half in enumerate(halves):
-
-        def pieces(plane):
-            own, across = given[each * plane], given[each * plane + 1 + n]
-            return own.at[2 * half], own.at[2 * half + 1], across.at[0], across.at[1]
-
-        for d, ref in enumerate(pieces(0)):
+    for n in range(len(halves)):
+        for d, ref in enumerate(pieces[0][n]):
             for w in range(windows):
                 side[w, d * count : (d + 1) * count, :] = ref[w * count : (w + 1) * count, :].astype(jnp.float32)
         for plane in range(planes):
-            for d, ref in enumerate(pieces(plane + 1)):
+            for d, ref in enumerate(pieces[len(sizes) - planes + plane][n]):
                 start = pl.multiple_of(plane * span + blocks[d] * count, count)
                 for w in range(windows):
                     extended[w, pl.ds(start, count), :] = ref[w * count : (w + 1) * count, :].astype(jnp.float32)
@@ -227,7 +249,7 @@
                 paired[d, pl.ds(within * pitch + j, 8, stride=pitch), :] = both
             return carry
 
-        lax.fori_loop(0, span // 8, group, 0, unroll=2)
+        lax.fori_loop(0, span // 8, group, 0, unroll=True)
         for d in range(TEAM):
             out = (near if d < 2 else far).at[2 * n + d % 2]
             for k in range(0, count, 2):
@@ -240,12 +262,18 @@
     stride = BAND // offsets.shape[0]
     low = (first * stride + 1) // span
     high = (span - 1 + last * stride) // span
-    planes = [team_planes[0]] + [team_planes[p] for p in range(low, min(high, len(team_planes) - 1) + 1)]
-    given = [c for plane in planes for c in [plane[0]] + [plane[1 + half] for half in halves]]
+    top = min(high, len(team_planes) - 1)
+    used = [0] * (low > 0) + list(range(low, top + 1))
+    groups = []
+    for plane in (team_planes[p] for p in used):
+        split = len(plane) > HALVES
+        groups.append([plane[0]] * split + [plane[split + half] for half in halves])
+    sizes = tuple(len(g) for g in groups)
+    given = [c for g in groups for c in g]
     number = last - first
     vmem = pl.BlockSpec(memory_space=pltpu.VMEM)
     return pl.pallas_call(
-        functools.partial(cross_kernel, windows, count, halves, first, last, low, len(planes) - 1),
+        functools.partial(cross_kernel, windows, count, halves, sizes, first, last, low, top - low + 1),
         in_specs=[pl.BlockSpec(memory_space=pltpu.SMEM)] + [vmem] * len(given),
         out_specs=[vmem] * 2,
         out_shape=[pltpu.VMEM((2 * len(halves), count * number, LANES), jnp.bfloat16)] * 2,
@@ -255,72 +283,77 @@
             pltpu.VMEM((TEAM, count * (number + 1), LANES), jnp.float32),
         ],
         compiler_params=pltpu.CompilerParams(vmem_limit_bytes=8 * MIB),
-        cost_estimate=busy(2.0 * len(halves)),
+        cost_estimate=busy(0.5 * len(halves)),
         name="cross",
     )(offsets, *given)
 
 
-def lag_sum(given, table, columns):
+def lag_sum(pieces, table, half, columns):
     me = lax.rem(lax.axis_index("chan"), TEAM)
+    odd = lax.rem(me, 2) == 1
     total = None
-    for d in range(TEAM):
-        left = jnp.concatenate([given[h * TEAM + d] for h in range(HALVES)], axis=1)
-        term = jnp.dot(left, table[jnp.bitwise_xor(me, d), :, columns], preferred_element_type=jnp.float32)
-        total = term if d == 0 else total + term
+    for chip in range(TEAM // 2):
+        first, second = pieces[2 * chip], pieces[2 * chip + 1]
+        left = jnp.concatenate([jnp.where(odd, second, first), jnp.where(odd, first, second)], axis=1)
+        right = table[half, jnp.bitwise_xor(me // 2, chip), :, columns]
+        term = jnp.dot(left, right, preferred_element_type=jnp.float32)
+        total = term if chip == 0 else total + term
     return total * (1.0 / math.sqrt(F))
 
 
-def picked(refs, picks):
-    return [refs[n][at] for n, at in picks]
-
-
-def early_kernel(tile, picks, *refs):
-    given, table, out = picked(refs, picks), refs[-2], refs[-1]
+def early_kernel(tile, *refs):
+    low, high, (table, lower, upper) = refs[: HALVES * TEAM], refs[HALVES * TEAM : -3], refs[-3:]
     for t in range(LAGS // tile):
         columns = pl.ds(t * tile, tile)
-        out[:, columns] = lag_sum(given, table, columns)
-
-
-def late_kernel(count, tile, picks, *refs):
-    given, table, early, out = picked(refs, picks), refs[-3], refs[-2], refs[-1]
+        shares = [lag_sum([low[h * TEAM + d][d % 2] for d in range(TEAM)], table, h, columns) for h in range(HALVES)]
+        lower[:, columns] = shares[0] + shares[1]
+        upper[:, columns] = lag_sum([high[d][d % 2] for d in range(TEAM)], table, 0, columns)
+
+
+def late_kernel(count, tile, *refs):
+    high, table, lower, upper, out = refs[:TEAM], refs[-4], refs[-3], refs[-2], refs[-1]
     columns = pl.ds(pl.multiple_of(pl.program_id(0) * tile, tile), tile)
-    both = [early[:, columns], lag_sum(given, table, columns)]
+    rest = lag_sum([high[d][d % 2] for d in range(TEAM)], table, 1, columns)
+    both = [lower[:, columns], upper[:, columns] + rest]
     both = [v.reshape(count, v.shape[0] // count, tile) for v in both]
     out[...] = jnp.concatenate(both, axis=1).astype(jnp.bfloat16)
 
 
-def lags_early(arrays, picks, table):
-    vmem = pl.BlockSpec(memory_space=pltpu.VMEM)
-    return pl.pallas_call(
-        functools.partial(early_kernel, 512, picks),
-        in_specs=[vmem] * (len(arrays) + 1),
-        out_specs=vmem,
-        out_shape=pltpu.VMEM((arrays[0].shape[1], LAGS), jnp.float32),
+def lags_early(low, high, table):
+    vmem = pl.BlockSpec(memory_space=pltpu.VMEM)
+    return pl.pallas_call(
+        functools.partial(early_kernel, 512),
+        in_specs=[vmem] * (len(low) + len(high) + 1),
+        out_specs=[vmem] * 2,
+        out_shape=[pltpu.VMEM((v[0].shape[1], LAGS), jnp.float32) for v in (low, high)],
         compiler_params=pltpu.CompilerParams(vmem_limit_bytes=12 * MIB),
-        cost_estimate=busy(1.5),
+        cost_estimate=busy(0.1),
         name="lags_early",
-    )(*arrays, table)
-
-
-def lags_late(arrays, picks, table, early, count, number):
-    vmem = pl.BlockSpec(memory_space=pltpu.VMEM)
-    tile = 512
-    return pl.pallas_call(
-        functools.partial(late_kernel, count, tile, picks),
+    )(*low, *high, table)
+
+
+def lags_late(high, table, lower, upper, count, number):
+    vmem = pl.BlockSpec(memory_space=pltpu.VMEM)
+    tile = 1024
+    return pl.pallas_call(
+        functools.partial(late_kernel, count, tile),
         grid=(LAGS // tile,),
-        in_specs=[vmem] * (len(arrays) + 2),
+        in_specs=[vmem] * (TEAM + 3),
         out_specs=pl.BlockSpec((count, number, tile), lambda i: (0, 0, i)),
         out_shape=jax.ShapeDtypeStruct((count, number, LAGS), jnp.bfloat16),
         compiler_params=pltpu.CompilerParams(vmem_limit_bytes=16 * MIB),
         cost_estimate=busy(2.0),
         name="lags_late",
-    )(*arrays, table, early)
+    )(*high, table, lower, upper)
 
 
 def solution(mesh):
     ring = mesh.shape["chan"]
     if ring % TEAM:
         raise ValueError("chan")
+
+    def after(value, *others):
+        return lax.optimization_barrier((value,) + others)[0] if others else value
 
     def swapped(value, by):
         return lax.ppermute(value, "chan", [(i, i ^ by) for i in range(ring)])
@@ -338,24 +371,36 @@
         inverse = jnp.asarray(inverse)
         near = joined(mine, swapped(sibling, 1))
         across = [swapped(far, 2) for far in (far0, far1)]
-        chunks = [[near] + [far_joined(c, swapped(c, 1)) for c in across]]
+        own = [near] + [far_joined(c, swapped(c, 1)) for c in across]
         reach = min((span + BAND - 2) // span, ring // TEAM - 1)
+        middle = number // 2
+
+        def crossed(halves, first, last, planes, others=(), before=()):
+            planes = [[after(planes[0][0], *others)] + planes[0][1:]] + planes[1:]
+            near, far = cross(windows, count, halves, first, last, offsets, planes)
+            return near, swapped(after(far, *before), 2)
+
+        def gathered(near, back, *others):
+            return near, swapped(near, 1), back, swapped(after(back, *others), 1)
+
+        chunks = [own]
+        low = []
         for hops in range(1, reach + 1):
-            chunks.append([down(c, hops) for c in chunks[-1]])
-
-        def returned(halves, first, last):
-            near, far = cross(windows, count, halves, first, last, offsets, chunks)
-            back = swapped(far, 2)
-            arrays = [near, swapped(near, 1), back, swapped(back, 1)]
-            return arrays, [(d, 2 * n + d % 2) for n in range(len(halves)) for d in range(TEAM)]
-
-        middle = number // 2
-        arrays, picks = returned((0, 1), 0, middle)
-        early = lags_early(arrays, picks, inverse)
-        arrays, picks = returned((0,), middle, number)
-        more, rest = returned((1,), middle, number)
-        picks = picks + [(len(arrays) + n, at) for n, at in rest]
-        return lags_late(arrays + more, picks, inverse, early, count, number)
+            arrived = [down(c, hops) for c in chunks[-1]]
+            if hops == JOIN:
+                first = team_joined(0, arrived[0], arrived[1])
+                low = [crossed((0,), 0, middle, chunks + [[first, None]])]
+                arrived = [first, team_joined(1, arrived[0], after(arrived[2], low[0][0]))]
+            chunks.append(arrived)
+        for half in range(len(low), HALVES):
+            low.append(crossed((half,), 0, middle, chunks))
+        near0, back0 = crossed((0,), middle, number, chunks)
+        near1, back1 = crossed((1,), middle, number, chunks)
+        low = gathered(*low[0], near1) + gathered(*low[1], near1)
+        high = gathered(near0, back0, near1)
+        lower, upper = lags_early(low, high, inverse)
+        rest = gathered(near1, back1, lower)
+        return lags_late(rest, inverse, lower, upper, count, number)
 
     in_specs = (P(("day", "chan"), None, None), P(("day", "chan")), P())
     out_specs = P(("day", "chan"), None, None)

time: 65.2 us -> 61.8 us (0.948)
  Pallas kernels: 17.4 us -> 14.8 us
  waiting for transfers between devices: 27.6 us -> 25.8 us
  starting transfers between devices: 19.6 us -> 20.7 us
    pallas_call x5 -> x8, Pallas kernels: 13.3 us -> 10.7 us  [the longest x4 6.85 us: cross(): pl.pallas_call(functools.partial(cross_kernel, windows, count, halves, si...]
    ppermute x14 -> x17, starting transfers between devices: 8.07 us -> 10.4 us  [swapped(): return lax.ppermute(value, 'chan', [(i, i ^ by) for i in range(ring)])]
    ppermute x14 -> x17, waiting for transfers between devices: 10.1 us -> 8.16 us  [swapped(): return lax.ppermute(value, 'chan', [(i, i ^ by) for i in range(ring)])]
    ppermute x9 -> x8, starting transfers between devices: 11.6 us -> 10.3 us  [down(): return lax.ppermute(value, 'chan', pairs)]
    ppermute x9 -> x8, waiting for transfers between devices: 17.5 us -> 17.7 us  [down(): return lax.ppermute(value, 'chan', pairs)]
  transfers between devices with their start and end apart: 23 -> 25, of which waited for: 10 -> 11; matrix products, arithmetic and copies ran while one was open for 0% -> 0% of each run, Pallas kernels for 16% -> 14%
where the time goes in v4:
time: 61.8 us; the launch traced here: 61.5 us
  waiting for transfers between devices  25.8 us (42%)
  starting transfers between devices  20.7 us (33%)
  Pallas kernels  14.8 us (24%)
    ppermute x8, waiting for transfers between devices, down(): return lax.ppermute(value, 'chan', pairs)  17.7 us
    ppermute x17, starting transfers between devices, swapped(): return lax.ppermute(value, 'chan', [(i, i ^ by) for i in range(ring)])  10.4 us
    ppermute x8, starting transfers between devices, down(): return lax.ppermute(value, 'chan', pairs)  10.3 us
    ppermute x17, waiting for transfers between devices, swapped(): return lax.ppermute(value, 'chan', [(i, i ^ by) for i in range(ring)])  8.16 us
    pallas_call x4, Pallas kernels, cross(): pl.pallas_call(functools.partial(cross_kernel, windows, count, halves, si...  6.85 us
    pallas_call x1, Pallas kernels, spectra(): pl.pallas_call(functools.partial(spectra_kernel, windows), in_specs=[pl.B...  4.08 us
    pallas_call x1, Pallas kernels, lags_late(): pl.pallas_call(functools.partial(late_kernel, count, tile), grid=(LAGS //...  1.91 us
    pallas_call x1, Pallas kernels, lags_early(): pl.pallas_call(functools.partial(early_kernel, 512), in_specs=[vmem] * (l...  1.91 us
  transfers between devices with their start and end apart: 25, of which 11 were waited for; matrix products, arithmetic and copies ran while one was open for 0% of the time, Pallas kernels for 14%

profile of v4, /device:TPU:0, one launch (start us, length us, event | category | flops | bytes accessed | tf_op | source)
XLA Modules:
  0.0 61.5 jit_solution(14887442825176165259)
XLA Ops:
  0.0 4.1 %spectra.1 = (bf16[2,256,128]{2,1,0:T(8,128)(2,1)S(1)}, bf16[2,256,128]{2,1,0:T(8,128)(2,1)S(1)}, bf16[2,256,128]{2,1,0:T(8,128)(2,1)S(1)}, bf16[2,256,128]{2,1,0:T(8,128)(2,1)S(1)}) custom-call(bf16[256,3000]{1,0:T(8,128)(2,1)} %bitcast.2, bf16[2,750,512]{2,1,0:T(8,128)(2,1)} %constant.4.clone.table_hbm, s32[1,32]{1,0:T(1,128)} %bitcast.3), custom_call_target="tpu_custom_call" | custom-call | flops 3460499968 | tf_op jit(solution)/shard_map/spectra/pallas_call | solution.py:118
  4.6 2.6 %collective-permute-start.7 = (bf16[2,256,128]{2,1,0:T(8,128)(2,1)S(1)}, bf16[2,256,128]{2,1,0:T(8,128)(2,1)S(1)}, u32[]{:S(2)}, u32[]{:S(2)}) collective-permute-start(bf16[2,256,128]{2,1,0:T(8,128)(2,1)S(1)} %get-tuple-element.27), channel_id=1, source_target_pairs={{0,2},{1,3},{2,0},{3,1},{4,6},{5,7},{6,4},{7,5},{8,10},{9,11},{10,... | collective-permute-start | bytes 393224 | tf_op jit(solution)/shard_map/ppermute | solution.py:359
  7.2 1.3 %collective-permute-start.3 = (bf16[4,256,128]{2,1,0:T(8,128)(2,1)S(1)}, bf16[4,256,128]{2,1,0:T(8,128)(2,1)S(1)}, u32[]{:S(2)}, u32[]{:S(2)}) collective-permute-start(bf16[4,256,128]{2,1,0:T(8,128)(2,1)S(1)} %joined.1.refs_0_), channel_id=1, source_target_pairs={{4,0},{5,1},{6,2},{7,3},{8,4},{9,5},{10,6},{11,7},{12,8},{13,9},{1... | collective-permute-start | bytes 786440 | tf_op jit(solution)/shard_map/ppermute | solution.py:363
  8.5 1.3 %collective-permute-start.1 = (bf16[2,256,128]{2,1,0:T(8,128)(2,1)S(1)}, bf16[2,256,128]{2,1,0:T(8,128)(2,1)S(1)}, u32[]{:S(2)}, u32[]{:S(2)}) collective-permute-start(bf16[2,256,128]{2,1,0:T(8,128)(2,1)S(1)} %get-tuple-element.26), channel_id=1, source_target_pairs={{0,2},{1,3},{2,0},{3,1},{4,6},{5,7},{6,4},{7,5},{8,10},{9,11},{10,... | collective-permute-start | bytes 393224 | tf_op jit(solution)/shard_map/ppermute | solution.py:359
  9.9 1.4 %collective-permute-done.7.straight = bf16[2,256,128]{2,1,0:T(8,128)(2,1)S(1)} collective-permute-done((bf16[2,256,128]{2,1,0:T(8,128)(2,1)S(1)}, bf16[2,256,128]{2,1,0:T(8,128)(2,1)S(1)}, u32[]{:S(2)}, u32[]{:S(2)}) %collective-permute-start.7) | collective-permute-done | bytes 131104 | tf_op jit(solution)/shard_map/ppermute | solution.py:359
  11.3 2.9 %collective-permute-done.1.straight = bf16[2,256,128]{2,1,0:T(8,128)(2,1)S(1)} collective-permute-done((bf16[2,256,128]{2,1,0:T(8,128)(2,1)S(1)}, bf16[2,256,128]{2,1,0:T(8,128)(2,1)S(1)}, u32[]{:S(2)}, u32[]{:S(2)}) %collective-permute-start.1) | collective-permute-done | bytes 131104 | tf_op jit(solution)/shard_map/ppermute | solution.py:359
  14.2 1.3 %collective-permute-start.9 = (bf16[2,256,128]{2,1,0:T(8,128)(2,1)S(1)}, bf16[2,256,128]{2,1,0:T(8,128)(2,1)S(1)}, u32[]{:S(2)}, u32[]{:S(2)}) collective-permute-start(bf16[2,256,128]{2,1,0:T(8,128)(2,1)S(1)} %far_joined.3.refs_1_), channel_id=1, source_target_pairs={{4,0},{5,1},{6,2},{7,3},{8,4},{9,5},{10,6},{11,7},{12,8},{13,9},{1... | collective-permute-start | bytes 393224 | tf_op jit(solution)/shard_map/ppermute | solution.py:363
  15.5 2.0 %collective-permute-done.3.refs_2_ = bf16[4,256,128]{2,1,0:T(8,128)(2,1)S(1)} collective-permute-done((bf16[4,256,128]{2,1,0:T(8,128)(2,1)S(1)}, bf16[4,256,128]{2,1,0:T(8,128)(2,1)S(1)}, u32[]{:S(2)}, u32[]{:S(2)}) %collective-permute-start.3) | collective-permute-done | bytes 262176 | tf_op jit(solution)/shard_map/ppermute | solution.py:363
  18.8 1.3 %collective-permute-start.5 = (bf16[2,256,128]{2,1,0:T(8,128)(2,1)S(1)}, bf16[2,256,128]{2,1,0:T(8,128)(2,1)S(1)}, u32[]{:S(2)}, u32[]{:S(2)}) collective-permute-start(bf16[2,256,128]{2,1,0:T(8,128)(2,1)S(1)} %far_joined.2.refs_1_), channel_id=1, source_target_pairs={{4,0},{5,1},{6,2},{7,3},{8,4},{9,5},{10,6},{11,7},{12,8},{13,9},{1... | collective-permute-start | bytes 393224 | tf_op jit(solution)/shard_map/ppermute | solution.py:363
  20.1 2.7 %collective-permute-done.9.refs_3_ = bf16[2,256,128]{2,1,0:T(8,128)(2,1)S(1)} collective-permute-done((bf16[2,256,128]{2,1,0:T(8,128)(2,1)S(1)}, bf16[2,256,128]{2,1,0:T(8,128)(2,1)S(1)}, u32[]{:S(2)}, u32[]{:S(2)}) %collective-permute-start.9) | collective-permute-done | bytes 131104 | tf_op jit(solution)/shard_map/ppermute | solution.py:363
  24.1 7.4 %collective-permute-done.5.refs_3_ = bf16[2,256,128]{2,1,0:T(8,128)(2,1)S(1)} collective-permute-done((bf16[2,256,128]{2,1,0:T(8,128)(2,1)S(1)}, bf16[2,256,128]{2,1,0:T(8,128)(2,1)S(1)}, u32[]{:S(2)}, u32[]{:S(2)}) %collective-permute-start.5) | collective-permute-done | bytes 131104 | tf_op jit(solution)/shard_map/ppermute | solution.py:363
  35.2 1.7 %cross.4 = (bf16[2,256,128]{2,1,0:T(8,128)(2,1)S(1)}, bf16[2,256,128]{2,1,0:T(8,128)(2,1)S(1)}) custom-call(s32[16]{0:T(128)S(1)} %copy-done.1, bf16[4,256,128]{2,1,0:T(8,128)(2,1)S(1)} %joined.1.refs_0_, bf16[2,256,128]{2,1,0:T(8,128)(2,1)S(1)} %far_joined.3.refs_1_, bf16[4,256,128]{2,1,0:T(8,128)(2,1)S(1)} %collective-permute-done.3.refs_2_, ...), custom_call_target="tpu_custom_call" | custom-call | flops 576750016 | tf_op jit(solution)/shard_map/cross/pallas_call | solution.py:275
  36.9 1.6 %collective-permute-done.6.far = bf16[2,256,128]{2,1,0:T(8,128)(2,1)S(1)} collective-permute-done((bf16[2,256,128]{2,1,0:T(8,128)(2,1)S(1)}, bf16[2,256,128]{2,1,0:T(8,128)(2,1)S(1)}, u32[]{:S(2)}, u32[]{:S(2)}) %collective-permute-start.6) | collective-permute-done | bytes 131104 | tf_op jit(solution)/shard_map/ppermute | solution.py:363
  39.8 1.7 %cross.6 = (bf16[2,256,128]{2,1,0:T(8,128)(2,1)S(1)}, bf16[2,256,128]{2,1,0:T(8,128)(2,1)S(1)}) custom-call(s32[16]{0:T(128)S(1)} %copy-done.1, bf16[4,256,128]{2,1,0:T(8,128)(2,1)S(1)} %joined.1.refs_0_, bf16[2,256,128]{2,1,0:T(8,128)(2,1)S(1)} %far_joined.2.refs_1_, bf16[4,256,128]{2,1,0:T(8,128)(2,1)S(1)} %collective-permute-done.3.refs_2_, ...), custom_call_target="tpu_custom_call" | custom-call | flops 576750016 | tf_op jit(solution)/shard_map/cross/pallas_call | solution.py:275
  41.5 1.3 %collective-permute-start.18 = (bf16[2,256,128]{2,1,0:T(8,128)(2,1)S(1)}, bf16[2,256,128]{2,1,0:T(8,128)(2,1)S(1)}, u32[]{:S(2)}, u32[]{:S(2)}) collective-permute-start(bf16[2,256,128]{2,1,0:T(8,128)(2,1)S(1)} %get-tuple-element.35), channel_id=1, source_target_pairs={{0,2},{1,3},{2,0},{3,1},{4,6},{5,7},{6,4},{7,5},{8,10},{9,11},{10,... | collective-permute-start | bytes 393224 | tf_op jit(solution)/shard_map/ppermute | solution.py:359
  43.6 1.4 %collective-permute-done.20.refs_3_ = bf16[4,256,128]{2,1,0:T(8,128)(2,1)S(1)} collective-permute-done((bf16[4,256,128]{2,1,0:T(8,128)(2,1)S(1)}, bf16[4,256,128]{2,1,0:T(8,128)(2,1)S(1)}, u32[]{:S(2)}, u32[]{:S(2)}) %collective-permute-start.20) | collective-permute-done | bytes 262176 | tf_op jit(solution)/shard_map/ppermute | solution.py:363
  45.0 1.7 %cross.7 = (bf16[2,256,128]{2,1,0:T(8,128)(2,1)S(1)}, bf16[2,256,128]{2,1,0:T(8,128)(2,1)S(1)}) custom-call(s32[16]{0:T(128)S(1)} %copy-done.1, bf16[4,256,128]{2,1,0:T(8,128)(2,1)S(1)} %joined.1.refs_0_, bf16[2,256,128]{2,1,0:T(8,128)(2,1)S(1)} %far_joined.3.refs_1_, bf16[4,256,128]{2,1,0:T(8,128)(2,1)S(1)} %team_joined.2.refs_4_.refs_2_, ...), custom_call_target="tpu_custom_call" | custom-call | flops 576750016 | tf_op jit(solution)/shard_map/cross/pallas_call | solution.py:275
  46.7 1.3 %collective-permute-start.22 = (bf16[2,256,128]{2,1,0:T(8,128)(2,1)S(1)}, bf16[2,256,128]{2,1,0:T(8,128)(2,1)S(1)}, u32[]{:S(2)}, u32[]{:S(2)}) collective-permute-start(bf16[2,256,128]{2,1,0:T(8,128)(2,1)S(1)} %get-tuple-element.38), channel_id=1, source_target_pairs={{0,2},{1,3},{2,0},{3,1},{4,6},{5,7},{6,4},{7,5},{8,10},{9,11},{10,... | collective-permute-start | bytes 393224 | tf_op jit(solution)/shard_map/ppermute | solution.py:359
  48.0 1.5 %collective-permute-done.11.refs_3_ = bf16[4,256,128]{2,1,0:T(8,128)(2,1)S(1)} collective-permute-done((bf16[4,256,128]{2,1,0:T(8,128)(2,1)S(1)}, bf16[4,256,128]{2,1,0:T(8,128)(2,1)S(1)}, u32[]{:S(2)}, u32[]{:S(2)}) %collective-permute-start.11) | collective-permute-done | bytes 262176 | tf_op jit(solution)/shard_map/ppermute | solution.py:363
  49.5 1.7 %cross.5 = (bf16[2,256,128]{2,1,0:T(8,128)(2,1)S(1)}, bf16[2,256,128]{2,1,0:T(8,128)(2,1)S(1)}) custom-call(s32[16]{0:T(128)S(1)} %copy-done.1, bf16[4,256,128]{2,1,0:T(8,128)(2,1)S(1)} %joined.1.refs_0_, bf16[2,256,128]{2,1,0:T(8,128)(2,1)S(1)} %far_joined.2.refs_1_, bf16[4,256,128]{2,1,0:T(8,128)(2,1)S(1)} %team_joined.3.refs_2_.refs_4_, ...), custom_call_target="tpu_custom_call" | custom-call | flops 576750016 | tf_op jit(solution)/shard_map/cross/pallas_call | solution.py:275
  53.9 1.9 %lags_early.1 = (f32[256,2048]{1,0:T(8,128)S(1)}, f32[256,2048]{1,0:T(8,128)S(1)}) custom-call(bf16[2,256,128]{2,1,0:T(8,128)(2,1)S(1)} %get-tuple-element.28.refs_0_, bf16[2,256,128]{2,1,0:T(8,128)(2,1)S(1)} %collective-permute-done.14.refs_1_, bf16[2,256,128]{2,1,0:T(8,128)(2,1)S(1)} %collective-permute-done.15.refs_2_, ...), custom_call_target="tpu_custom_call" | custom-call | flops 115350000 | tf_op jit(solution)/shard_map/lags_early/pallas_call | solution.py:324
  55.8 2.5 %collective-permute-done.13.refs_2_ = bf16[2,256,128]{2,1,0:T(8,128)(2,1)S(1)} collective-permute-done((bf16[2,256,128]{2,1,0:T(8,128)(2,1)S(1)}, bf16[2,256,128]{2,1,0:T(8,128)(2,1)S(1)}, u32[]{:S(2)}, u32[]{:S(2)}) %collective-permute-start.13) | collective-permute-done | bytes 131104 | tf_op jit(solution)/shard_map/ppermute | solution.py:359
  58.3 1.3 %collective-permute-done.24.refs_3_ = bf16[2,256,128]{2,1,0:T(8,128)(2,1)S(1)} collective-permute-done((bf16[2,256,128]{2,1,0:T(8,128)(2,1)S(1)}, bf16[2,256,128]{2,1,0:T(8,128)(2,1)S(1)}, u32[]{:S(2)}, u32[]{:S(2)}) %collective-permute-start.24) | collective-permute-done | bytes 131104 | tf_op jit(solution)/shard_map/ppermute | solution.py:359
  59.6 1.9 %lags_late.1 = bf16[32,16,2048]{2,1,0:T(8,128)(2,1)} custom-call(bf16[2,256,128]{2,1,0:T(8,128)(2,1)S(1)} %get-tuple-element.30.refs_0_, bf16[2,256,128]{2,1,0:T(8,128)(2,1)S(1)} %collective-permute-done.12.refs_1_, bf16[2,256,128]{2,1,0:T(8,128)(2,1)S(1)} %collective-permute-done.13.refs_2_, bf16[2,256,128]{2,1,0:T(8,128)(2,1)S(1)} %collective-permute-done.24.refs_3_, ...), custom_call_target="tpu_custom_call" | custom-call | flops 2307000064 | tf_op jit(solution)/shard_map/lags_late/pallas_call | solution.py:338
  (42 shorter events, 11.6 us)
Async XLA Ops:
  4.1 3.1 %collective-permute-start = (bf16[2,256,128]{2,1,0:T(8,128)(2,1)S(1)}, bf16[2,256,128]{2,1,0:T(8,128)(2,1)S(1)}, u32[]{:S(2)}, u32[]{:S(2)}) collective-permute-start(bf16[2,256,128]{2,1,0:T(8,128)(2,1)S(1)} %get-tuple-element.25), channel_id=1, source_target_pairs={{0,1},{1,0},{2,3},{3,2},{4,5},{5,4},{6,7},{7,6},{8,9},{9,8},{10,11... | collective-permute-start | bytes 393224 | tf_op jit(solution)/shard_map/ppermute | solution.py:359
  4.6 6.7 %collective-permute-start.7 = (bf16[2,256,128]{2,1,0:T(8,128)(2,1)S(1)}, bf16[2,256,128]{2,1,0:T(8,128)(2,1)S(1)}, u32[]{:S(2)}, u32[]{:S(2)}) collective-permute-start(bf16[2,256,128]{2,1,0:T(8,128)(2,1)S(1)} %get-tuple-element.27), channel_id=1, source_target_pairs={{0,2},{1,3},{2,0},{3,1},{4,6},{5,7},{6,4},{7,5},{8,10},{9,11},{10,... | collective-permute-start | bytes 393224 | tf_op jit(solution)/shard_map/ppermute | solution.py:359
  7.2 10.3 %collective-permute-start.3 = (bf16[4,256,128]{2,1,0:T(8,128)(2,1)S(1)}, bf16[4,256,128]{2,1,0:T(8,128)(2,1)S(1)}, u32[]{:S(2)}, u32[]{:S(2)}) collective-permute-start(bf16[4,256,128]{2,1,0:T(8,128)(2,1)S(1)} %joined.1.refs_0_), channel_id=1, source_target_pairs={{4,0},{5,1},{6,2},{7,3},{8,4},{9,5},{10,6},{11,7},{12,8},{13,9},{1... | collective-permute-start | bytes 786440 | tf_op jit(solution)/shard_map/ppermute | solution.py:363
  8.5 5.6 %collective-permute-start.1 = (bf16[2,256,128]{2,1,0:T(8,128)(2,1)S(1)}, bf16[2,256,128]{2,1,0:T(8,128)(2,1)S(1)}, u32[]{:S(2)}, u32[]{:S(2)}) collective-permute-start(bf16[2,256,128]{2,1,0:T(8,128)(2,1)S(1)} %get-tuple-element.26), channel_id=1, source_target_pairs={{0,2},{1,3},{2,0},{3,1},{4,6},{5,7},{6,4},{7,5},{8,10},{9,11},{10,... | collective-permute-start | bytes 393224 | tf_op jit(solution)/shard_map/ppermute | solution.py:359
  11.3 2.9 %collective-permute-start.8 = (bf16[2,256,128]{2,1,0:T(8,128)(2,1)S(1)}, bf16[2,256,128]{2,1,0:T(8,128)(2,1)S(1)}, u32[]{:S(2)}, u32[]{:S(2)}) collective-permute-start(bf16[2,256,128]{2,1,0:T(8,128)(2,1)S(1)} %collective-permute-done.7.straight), channel_id=1, source_target_pairs={{0,1},{1,0},{2,3},{3,2},{4,5},{5,4},{6,7},{7,6},{8,9},{9,8},{10,11... | collective-permute-start | bytes 393224 | tf_op jit(solution)/shard_map/ppermute | solution.py:359
  14.2 4.6 %collective-permute-start.2 = (bf16[2,256,128]{2,1,0:T(8,128)(2,1)S(1)}, bf16[2,256,128]{2,1,0:T(8,128)(2,1)S(1)}, u32[]{:S(2)}, u32[]{:S(2)}) collective-permute-start(bf16[2,256,128]{2,1,0:T(8,128)(2,1)S(1)} %collective-permute-done.1.straight), channel_id=1, source_target_pairs={{0,1},{1,0},{2,3},{3,2},{4,5},{5,4},{6,7},{7,6},{8,9},{9,8},{10,11... | collective-permute-start | bytes 393224 | tf_op jit(solution)/shard_map/ppermute | solution.py:359
  14.2 8.6 %collective-permute-start.9 = (bf16[2,256,128]{2,1,0:T(8,128)(2,1)S(1)}, bf16[2,256,128]{2,1,0:T(8,128)(2,1)S(1)}, u32[]{:S(2)}, u32[]{:S(2)}) collective-permute-start(bf16[2,256,128]{2,1,0:T(8,128)(2,1)S(1)} %far_joined.3.refs_1_), channel_id=1, source_target_pairs={{4,0},{5,1},{6,2},{7,3},{8,4},{9,5},{10,6},{11,7},{12,8},{13,9},{1... | collective-permute-start | bytes 393224 | tf_op jit(solution)/shard_map/ppermute | solution.py:363
  17.5 16.4 %collective-permute-start.4 = (bf16[4,256,128]{2,1,0:T(8,128)(2,1)S(1)}, bf16[4,256,128]{2,1,0:T(8,128)(2,1)S(1)}, u32[]{:S(2)}, u32[]{:S(2)}) collective-permute-start(bf16[4,256,128]{2,1,0:T(8,128)(2,1)S(1)} %collective-permute-done.3.refs_2_), channel_id=1, source_target_pairs={{4,0},{5,1},{6,2},{7,3},{8,4},{9,5},{10,6},{11,7},{20,16},{21,17},... | collective-permute-start | bytes 786440 | tf_op jit(solution)/shard_map/ppermute | solution.py:363
  18.8 12.6 %collective-permute-start.5 = (bf16[2,256,128]{2,1,0:T(8,128)(2,1)S(1)}, bf16[2,256,128]{2,1,0:T(8,128)(2,1)S(1)}, u32[]{:S(2)}, u32[]{:S(2)}) collective-permute-start(bf16[2,256,128]{2,1,0:T(8,128)(2,1)S(1)} %far_joined.2.refs_1_), channel_id=1, source_target_pairs={{4,0},{5,1},{6,2},{7,3},{8,4},{9,5},{10,6},{11,7},{12,8},{13,9},{1... | collective-permute-start | bytes 393224 | tf_op jit(solution)/shard_map/ppermute | solution.py:363
  22.8 11.1 %collective-permute-start.10 = (bf16[2,256,128]{2,1,0:T(8,128)(2,1)S(1)}, bf16[2,256,128]{2,1,0:T(8,128)(2,1)S(1)}, u32[]{:S(2)}, u32[]{:S(2)}) collective-permute-start(bf16[2,256,128]{2,1,0:T(8,128)(2,1)S(1)} %collective-permute-done.9.refs_3_), channel_id=1, source_target_pairs={{4,0},{5,1},{6,2},{7,3},{8,4},{9,5},{10,6},{11,7},{20,16},{21,17},... | collective-permute-start | bytes 393224 | tf_op jit(solution)/shard_map/ppermute | solution.py:363
  31.4 7.0 %collective-permute-start.6 = (bf16[2,256,128]{2,1,0:T(8,128)(2,1)S(1)}, bf16[2,256,128]{2,1,0:T(8,128)(2,1)S(1)}, u32[]{:S(2)}, u32[]{:S(2)}) collective-permute-start(bf16[2,256,128]{2,1,0:T(8,128)(2,1)S(1)} %collective-permute-done.5.refs_3_), channel_id=1, source_target_pairs={{4,0},{5,1},{6,2},{7,3},{8,4},{9,5},{10,6},{11,7},{20,16},{21,17},... | collective-permute-start | bytes 393224 | tf_op jit(solution)/shard_map/ppermute | solution.py:363
  33.9 11.1 %collective-permute-start.20 = (bf16[4,256,128]{2,1,0:T(8,128)(2,1)S(1)}, bf16[4,256,128]{2,1,0:T(8,128)(2,1)S(1)}, u32[]{:S(2)}, u32[]{:S(2)}) collective-permute-start(bf16[4,256,128]{2,1,0:T(8,128)(2,1)S(1)} %team_joined.2.refs_4_.refs_2_), channel_id=1, source_target_pairs={{4,0},{5,1},{6,2},{7,3},{20,16},{21,17},{22,18},{23,19}} | collective-permute-start | bytes 786440 | tf_op jit(solution)/shard_map/ppermute | solution.py:363
  38.5 11.0 %collective-permute-start.11 = (bf16[4,256,128]{2,1,0:T(8,128)(2,1)S(1)}, bf16[4,256,128]{2,1,0:T(8,128)(2,1)S(1)}, u32[]{:S(2)}, u32[]{:S(2)}) collective-permute-start(bf16[4,256,128]{2,1,0:T(8,128)(2,1)S(1)} %team_joined.3.refs_2_.refs_4_), channel_id=1, source_target_pairs={{4,0},{5,1},{6,2},{7,3},{20,16},{21,17},{22,18},{23,19}} | collective-permute-start | bytes 786440 | tf_op jit(solution)/shard_map/ppermute | solution.py:363
  41.5 9.8 %collective-permute-start.18 = (bf16[2,256,128]{2,1,0:T(8,128)(2,1)S(1)}, bf16[2,256,128]{2,1,0:T(8,128)(2,1)S(1)}, u32[]{:S(2)}, u32[]{:S(2)}) collective-permute-start(bf16[2,256,128]{2,1,0:T(8,128)(2,1)S(1)} %get-tuple-element.35), channel_id=1, source_target_pairs={{0,2},{1,3},{2,0},{3,1},{4,6},{5,7},{6,4},{7,5},{8,10},{9,11},{10,... | collective-permute-start | bytes 393224 | tf_op jit(solution)/shard_map/ppermute | solution.py:359
  42.8 8.5 %collective-permute-start.15 = (bf16[2,256,128]{2,1,0:T(8,128)(2,1)S(1)}, bf16[2,256,128]{2,1,0:T(8,128)(2,1)S(1)}, u32[]{:S(2)}, u32[]{:S(2)}) collective-permute-start(bf16[2,256,128]{2,1,0:T(8,128)(2,1)S(1)} %get-tuple-element.32), channel_id=1, source_target_pairs={{0,2},{1,3},{2,0},{3,1},{4,6},{5,7},{6,4},{7,5},{8,10},{9,11},{10,... | collective-permute-start | bytes 393224 | tf_op jit(solution)/shard_map/ppermute | solution.py:359
  46.7 5.2 %collective-permute-start.22 = (bf16[2,256,128]{2,1,0:T(8,128)(2,1)S(1)}, bf16[2,256,128]{2,1,0:T(8,128)(2,1)S(1)}, u32[]{:S(2)}, u32[]{:S(2)}) collective-permute-start(bf16[2,256,128]{2,1,0:T(8,128)(2,1)S(1)} %get-tuple-element.38), channel_id=1, source_target_pairs={{0,2},{1,3},{2,0},{3,1},{4,6},{5,7},{6,4},{7,5},{8,10},{9,11},{10,... | collective-permute-start | bytes 393224 | tf_op jit(solution)/shard_map/ppermute | solution.py:359
  48.0 4.3 %collective-permute-start.17 = (bf16[2,256,128]{2,1,0:T(8,128)(2,1)S(1)}, bf16[2,256,128]{2,1,0:T(8,128)(2,1)S(1)}, u32[]{:S(2)}, u32[]{:S(2)}) collective-permute-start(bf16[2,256,128]{2,1,0:T(8,128)(2,1)S(1)} %get-tuple-element.34.refs_4_), channel_id=1, source_target_pairs={{0,1},{1,0},{2,3},{3,2},{4,5},{5,4},{6,7},{7,6},{8,9},{9,8},{10,11... | collective-permute-start | bytes 393224 | tf_op jit(solution)/shard_map/ppermute | solution.py:359
  49.5 2.9 %collective-permute-start.14 = (bf16[2,256,128]{2,1,0:T(8,128)(2,1)S(1)}, bf16[2,256,128]{2,1,0:T(8,128)(2,1)S(1)}, u32[]{:S(2)}, u32[]{:S(2)}) collective-permute-start(bf16[2,256,128]{2,1,0:T(8,128)(2,1)S(1)} %get-tuple-element.28.refs_0_), channel_id=1, source_target_pairs={{0,1},{1,0},{2,3},{3,2},{4,5},{5,4},{6,7},{7,6},{8,9},{9,8},{10,11... | collective-permute-start | bytes 393224 | tf_op jit(solution)/shard_map/ppermute | solution.py:359
  51.3 2.4 %collective-permute-start.16 = (bf16[2,256,128]{2,1,0:T(8,128)(2,1)S(1)}, bf16[2,256,128]{2,1,0:T(8,128)(2,1)S(1)}, u32[]{:S(2)}, u32[]{:S(2)}) collective-permute-start(bf16[2,256,128]{2,1,0:T(8,128)(2,1)S(1)} %collective-permute-done.15.refs_2_), channel_id=1, source_target_pairs={{0,1},{1,0},{2,3},{3,2},{4,5},{5,4},{6,7},{7,6},{8,9},{9,8},{10,11... | collective-permute-start | bytes 393224 | tf_op jit(solution)/shard_map/ppermute | solution.py:359
  51.8 2.0 %collective-permute-start.19 = (bf16[2,256,128]{2,1,0:T(8,128)(2,1)S(1)}, bf16[2,256,128]{2,1,0:T(8,128)(2,1)S(1)}, u32[]{:S(2)}, u32[]{:S(2)}) collective-permute-start(bf16[2,256,128]{2,1,0:T(8,128)(2,1)S(1)} %collective-permute-done.18.refs_6_), channel_id=1, source_target_pairs={{0,1},{1,0},{2,3},{3,2},{4,5},{5,4},{6,7},{7,6},{8,9},{9,8},{10,11... | collective-permute-start | bytes 393224 | tf_op jit(solution)/shard_map/ppermute | solution.py:359
  51.9 1.9 %collective-permute-start.21 = (bf16[2,256,128]{2,1,0:T(8,128)(2,1)S(1)}, bf16[2,256,128]{2,1,0:T(8,128)(2,1)S(1)}, u32[]{:S(2)}, u32[]{:S(2)}) collective-permute-start(bf16[2,256,128]{2,1,0:T(8,128)(2,1)S(1)} %get-tuple-element.37.refs_8_), channel_id=1, source_target_pairs={{0,1},{1,0},{2,3},{3,2},{4,5},{5,4},{6,7},{7,6},{8,9},{9,8},{10,11... | collective-permute-start | bytes 393224 | tf_op jit(solution)/shard_map/ppermute | solution.py:359
  52.4 1.5 %collective-permute-start.23 = (bf16[2,256,128]{2,1,0:T(8,128)(2,1)S(1)}, bf16[2,256,128]{2,1,0:T(8,128)(2,1)S(1)}, u32[]{:S(2)}, u32[]{:S(2)}) collective-permute-start(bf16[2,256,128]{2,1,0:T(8,128)(2,1)S(1)} %collective-permute-done.22.refs_10_), channel_id=1, source_target_pairs={{0,1},{1,0},{2,3},{3,2},{4,5},{5,4},{6,7},{7,6},{8,9},{9,8},{10,11... | collective-permute-start | bytes 393224 | tf_op jit(solution)/shard_map/ppermute | solution.py:359
  52.4 5.8 %collective-permute-start.13 = (bf16[2,256,128]{2,1,0:T(8,128)(2,1)S(1)}, bf16[2,256,128]{2,1,0:T(8,128)(2,1)S(1)}, u32[]{:S(2)}, u32[]{:S(2)}) collective-permute-start(bf16[2,256,128]{2,1,0:T(8,128)(2,1)S(1)} %get-tuple-element.31), channel_id=1, source_target_pairs={{0,2},{1,3},{2,0},{3,1},{4,6},{5,7},{6,4},{7,5},{8,10},{9,11},{10,... | collective-permute-start | bytes 393224 | tf_op jit(solution)/shard_map/ppermute | solution.py:359
  53.7 4.6 %collective-permute-start.12 = (bf16[2,256,128]{2,1,0:T(8,128)(2,1)S(1)}, bf16[2,256,128]{2,1,0:T(8,128)(2,1)S(1)}, u32[]{:S(2)}, u32[]{:S(2)}) collective-permute-start(bf16[2,256,128]{2,1,0:T(8,128)(2,1)S(1)} %get-tuple-element.30.refs_0_), channel_id=1, source_target_pairs={{0,1},{1,0},{2,3},{3,2},{4,5},{5,4},{6,7},{7,6},{8,9},{9,8},{10,11... | collective-permute-start | bytes 393224 | tf_op jit(solution)/shard_map/ppermute | solution.py:359
  (3 other events, 40.4 us)

commit v5 on v4

--- a/solution.py
+++ b/solution.py
@@ -194,9 +194,9 @@
     )(straight, crossed)
 
 
-def cross_kernel(windows, count, halves, sizes, first, last, low, planes, offsets, *refs):
-    near, far, side, extended, paired = refs[-5:]
-    given = list(refs[:-5])
+def cross_kernel(windows, count, halves, sizes, first, last, low, planes, apart, offsets, *refs):
+    outs, (side, extended, paired) = refs[-5 - apart : -3], refs[-3:]
+    given = list(refs[: -5 - apart])
     pieces = []
     for size in sizes:
         arrays, given = given[:size], given[size:]
@@ -251,13 +251,13 @@
 
         lax.fori_loop(0, span // 8, group, 0, unroll=True)
         for d in range(TEAM):
-            out = (near if d < 2 else far).at[2 * n + d % 2]
+            out = outs[d - 1].at[0] if apart and d > 1 else outs[d // 2].at[2 * n + d % 2]
             for k in range(0, count, 2):
                 rows = [paired[d, (k + m) * pitch : (k + m) * pitch + number, :] for m in range(2)]
                 out[k * number : (k + 2) * number, :] = jnp.concatenate(rows, axis=0).astype(jnp.bfloat16)
 
 
-def cross(windows, count, halves, first, last, offsets, team_planes):
+def cross(windows, count, halves, first, last, offsets, team_planes, apart=False):
     span = TEAM * count
     stride = BAND // offsets.shape[0]
     low = (first * stride + 1) // span
@@ -269,14 +269,15 @@
         split = len(plane) > HALVES
         groups.append([plane[0]] * split + [plane[split + half] for half in halves])
     sizes = tuple(len(g) for g in groups)
+    shares = [2 * len(halves)] * 2 if not apart else [2, 1, 1]
     given = [c for g in groups for c in g]
     number = last - first
     vmem = pl.BlockSpec(memory_space=pltpu.VMEM)
     return pl.pallas_call(
-        functools.partial(cross_kernel, windows, count, halves, sizes, first, last, low, top - low + 1),
+        functools.partial(cross_kernel, windows, count, halves, sizes, first, last, low, top - low + 1, int(apart)),
         in_specs=[pl.BlockSpec(memory_space=pltpu.SMEM)] + [vmem] * len(given),
-        out_specs=[vmem] * 2,
-        out_shape=[pltpu.VMEM((2 * len(halves), count * number, LANES), jnp.bfloat16)] * 2,
+        out_specs=[vmem] * len(shares),
+        out_shape=[pltpu.VMEM((n, count * number, LANES), jnp.bfloat16) for n in shares],
         scratch_shapes=[
             pltpu.VMEM((windows, span, LANES), jnp.float32),
             pltpu.VMEM((windows, (high - low + 1) * span, LANES), jnp.float32),
@@ -311,12 +312,18 @@
 
 
 def late_kernel(count, tile, *refs):
-    high, table, lower, upper, out = refs[:TEAM], refs[-4], refs[-3], refs[-2], refs[-1]
-    columns = pl.ds(pl.multiple_of(pl.program_id(0) * tile, tile), tile)
-    rest = lag_sum([high[d][d % 2] for d in range(TEAM)], table, 1, columns)
-    both = [lower[:, columns], upper[:, columns] + rest]
-    both = [v.reshape(count, v.shape[0] // count, tile) for v in both]
-    out[...] = jnp.concatenate(both, axis=1).astype(jnp.bfloat16)
+    high, (table, lower, upper, out, held, sems) = refs[:TEAM], refs[TEAM:]
+    copies = []
+    for t in range(LAGS // tile):
+        columns = pl.ds(t * tile, tile)
+        rest = lag_sum([high[d][min(d % 2, high[d].shape[0] - 1)] for d in range(TEAM)], table, 1, columns)
+        both = [lower[:, columns], upper[:, columns] + rest]
+        both = [v.reshape(count, v.shape[0] // count, tile) for v in both]
+        held[t] = jnp.concatenate(both, axis=1).astype(jnp.bfloat16)
+        copies.append(pltpu.make_async_copy(held.at[t], out.at[:, :, columns], sems.at[t]))
+        copies[-1].start()
+    for copy in copies:
+        copy.wait()
 
 
 def lags_early(low, high, table):
@@ -334,13 +341,16 @@
 
 def lags_late(high, table, lower, upper, count, number):
     vmem = pl.BlockSpec(memory_space=pltpu.VMEM)
-    tile = 1024
+    tile = 512
     return pl.pallas_call(
         functools.partial(late_kernel, count, tile),
-        grid=(LAGS // tile,),
         in_specs=[vmem] * (TEAM + 3),
-        out_specs=pl.BlockSpec((count, number, tile), lambda i: (0, 0, i)),
+        out_specs=pl.BlockSpec(memory_space=pltpu.HBM),
         out_shape=jax.ShapeDtypeStruct((count, number, LAGS), jnp.bfloat16),
+        scratch_shapes=[
+            pltpu.VMEM((LAGS // tile, count, number, tile), jnp.bfloat16),
+            pltpu.SemaphoreType.DMA((LAGS // tile,)),
+        ],
         compiler_params=pltpu.CompilerParams(vmem_limit_bytes=16 * MIB),
         cost_estimate=busy(2.0),
         name="lags_late",
@@ -395,11 +405,11 @@
         for half in range(len(low), HALVES):
             low.append(crossed((half,), 0, middle, chunks))
         near0, back0 = crossed((0,), middle, number, chunks)
-        near1, back1 = crossed((1,), middle, number, chunks)
-        low = gathered(*low[0], near1) + gathered(*low[1], near1)
+        near1, across1, diagonal1 = cross(windows, count, (1,), middle, number, offsets, chunks, True)
+        low = gathered(*low[0], near0) + gathered(*low[1], near0)
         high = gathered(near0, back0, near1)
         lower, upper = lags_early(low, high, inverse)
-        rest = gathered(near1, back1, lower)
+        rest = near1, swapped(near1, 1), swapped(across1, 2), swapped(diagonal1, 3)
         return lags_late(rest, inverse, lower, upper, count, number)
 
     in_specs = (P(("day", "chan"), None, None), P(("day", "chan")), P())

time: 61.8 us -> 59.9 us (0.969)
  waiting for transfers between devices: 25.8 us -> 23.8 us
    ppermute x17, waiting for transfers between devices: 8.16 us -> 6.69 us  [swapped(): return lax.ppermute(value, 'chan', [(i, i ^ by) for i in range(ring)])]
  transfers between devices with their start and end apart: 25 -> 25, of which waited for: 11 -> 12; matrix products, arithmetic and copies ran while one was open for 0% -> 0% of each run, Pallas kernels for 14% -> 15%
where the time goes in v5:
time: 59.9 us; the launch traced here: 59.6 us
  waiting for transfers between devices  23.8 us (40%)
  starting transfers between devices  21.1 us (35%)
  Pallas kernels  14.6 us (24%)
    ppermute x8, waiting for transfers between devices, down(): return lax.ppermute(value, 'chan', pairs)  17.1 us
    ppermute x17, starting transfers between devices, swapped(): return lax.ppermute(value, 'chan', [(i, i ^ by) for i in range(ring)])  10.8 us
    ppermute x8, starting transfers between devices, down(): return lax.ppermute(value, 'chan', pairs)  10.3 us
    pallas_call x4, Pallas kernels, cross(): pl.pallas_call(functools.partial(cross_kernel, windows, count, halves, si...  6.85 us
    ppermute x17, waiting for transfers between devices, swapped(): return lax.ppermute(value, 'chan', [(i, i ^ by) for i in range(ring)])  6.69 us
    pallas_call x1, Pallas kernels, spectra(): pl.pallas_call(functools.partial(spectra_kernel, windows), in_specs=[pl.B...  4.08 us
    pallas_call x1, Pallas kernels, lags_early(): pl.pallas_call(functools.partial(early_kernel, 512), in_specs=[vmem] * (l...  1.91 us
    pallas_call x1, Pallas kernels, lags_late(): pl.pallas_call(functools.partial(late_kernel, count, tile), in_specs=[vme...  1.69 us
  transfers between devices with their start and end apart: 25, of which 12 were waited for; matrix products, arithmetic and copies ran while one was open for 0% of the time, Pallas kernels for 15%

profile of v5, /device:TPU:0, one launch (start us, length us, event | category | flops | bytes accessed | tf_op | source)
XLA Modules:
  0.0 59.6 jit_solution(7907352995246497030)
XLA Ops:
  0.0 4.1 %spectra.1 = (bf16[2,256,128]{2,1,0:T(8,128)(2,1)S(1)}, bf16[2,256,128]{2,1,0:T(8,128)(2,1)S(1)}, bf16[2,256,128]{2,1,0:T(8,128)(2,1)S(1)}, bf16[2,256,128]{2,1,0:T(8,128)(2,1)S(1)}) custom-call(bf16[256,3000]{1,0:T(8,128)(2,1)} %bitcast.2, bf16[2,750,512]{2,1,0:T(8,128)(2,1)} %constant.4.clone.table_hbm, s32[1,32]{1,0:T(1,128)} %bitcast.3), custom_call_target="tpu_custom_call" | custom-call | flops 3460499968 | tf_op jit(solution)/shard_map/spectra/pallas_call | solution.py:118
  4.6 2.6 %collective-permute-start.7 = (bf16[2,256,128]{2,1,0:T(8,128)(2,1)S(1)}, bf16[2,256,128]{2,1,0:T(8,128)(2,1)S(1)}, u32[]{:S(2)}, u32[]{:S(2)}) collective-permute-start(bf16[2,256,128]{2,1,0:T(8,128)(2,1)S(1)} %get-tuple-element.27), channel_id=1, source_target_pairs={{0,2},{1,3},{2,0},{3,1},{4,6},{5,7},{6,4},{7,5},{8,10},{9,11},{10,... | collective-permute-start | bytes 393224 | tf_op jit(solution)/shard_map/ppermute | solution.py:369
  7.2 1.3 %collective-permute-start.3 = (bf16[4,256,128]{2,1,0:T(8,128)(2,1)S(1)}, bf16[4,256,128]{2,1,0:T(8,128)(2,1)S(1)}, u32[]{:S(2)}, u32[]{:S(2)}) collective-permute-start(bf16[4,256,128]{2,1,0:T(8,128)(2,1)S(1)} %joined.1.refs_0_), channel_id=1, source_target_pairs={{4,0},{5,1},{6,2},{7,3},{8,4},{9,5},{10,6},{11,7},{12,8},{13,9},{1... | collective-permute-start | bytes 786440 | tf_op jit(solution)/shard_map/ppermute | solution.py:373
  8.5 1.3 %collective-permute-start.1 = (bf16[2,256,128]{2,1,0:T(8,128)(2,1)S(1)}, bf16[2,256,128]{2,1,0:T(8,128)(2,1)S(1)}, u32[]{:S(2)}, u32[]{:S(2)}) collective-permute-start(bf16[2,256,128]{2,1,0:T(8,128)(2,1)S(1)} %get-tuple-element.26), channel_id=1, source_target_pairs={{0,2},{1,3},{2,0},{3,1},{4,6},{5,7},{6,4},{7,5},{8,10},{9,11},{10,... | collective-permute-start | bytes 393224 | tf_op jit(solution)/shard_map/ppermute | solution.py:369
  9.9 1.4 %collective-permute-done.7.straight = bf16[2,256,128]{2,1,0:T(8,128)(2,1)S(1)} collective-permute-done((bf16[2,256,128]{2,1,0:T(8,128)(2,1)S(1)}, bf16[2,256,128]{2,1,0:T(8,128)(2,1)S(1)}, u32[]{:S(2)}, u32[]{:S(2)}) %collective-permute-start.7) | collective-permute-done | bytes 131104 | tf_op jit(solution)/shard_map/ppermute | solution.py:369
  11.3 2.9 %collective-permute-done.1.straight = bf16[2,256,128]{2,1,0:T(8,128)(2,1)S(1)} collective-permute-done((bf16[2,256,128]{2,1,0:T(8,128)(2,1)S(1)}, bf16[2,256,128]{2,1,0:T(8,128)(2,1)S(1)}, u32[]{:S(2)}, u32[]{:S(2)}) %collective-permute-start.1) | collective-permute-done | bytes 131104 | tf_op jit(solution)/shard_map/ppermute | solution.py:369
  14.2 1.3 %collective-permute-start.9 = (bf16[2,256,128]{2,1,0:T(8,128)(2,1)S(1)}, bf16[2,256,128]{2,1,0:T(8,128)(2,1)S(1)}, u32[]{:S(2)}, u32[]{:S(2)}) collective-permute-start(bf16[2,256,128]{2,1,0:T(8,128)(2,1)S(1)} %far_joined.3.refs_1_), channel_id=1, source_target_pairs={{4,0},{5,1},{6,2},{7,3},{8,4},{9,5},{10,6},{11,7},{12,8},{13,9},{1... | collective-permute-start | bytes 393224 | tf_op jit(solution)/shard_map/ppermute | solution.py:373
  15.5 2.0 %collective-permute-done.3.refs_2_ = bf16[4,256,128]{2,1,0:T(8,128)(2,1)S(1)} collective-permute-done((bf16[4,256,128]{2,1,0:T(8,128)(2,1)S(1)}, bf16[4,256,128]{2,1,0:T(8,128)(2,1)S(1)}, u32[]{:S(2)}, u32[]{:S(2)}) %collective-permute-start.3) | collective-permute-done | bytes 262176 | tf_op jit(solution)/shard_map/ppermute | solution.py:373
  18.8 1.3 %collective-permute-start.5 = (bf16[2,256,128]{2,1,0:T(8,128)(2,1)S(1)}, bf16[2,256,128]{2,1,0:T(8,128)(2,1)S(1)}, u32[]{:S(2)}, u32[]{:S(2)}) collective-permute-start(bf16[2,256,128]{2,1,0:T(8,128)(2,1)S(1)} %far_joined.2.refs_1_), channel_id=1, source_target_pairs={{4,0},{5,1},{6,2},{7,3},{8,4},{9,5},{10,6},{11,7},{12,8},{13,9},{1... | collective-permute-start | bytes 393224 | tf_op jit(solution)/shard_map/ppermute | solution.py:373
  20.1 2.7 %collective-permute-done.9.refs_3_ = bf16[2,256,128]{2,1,0:T(8,128)(2,1)S(1)} collective-permute-done((bf16[2,256,128]{2,1,0:T(8,128)(2,1)S(1)}, bf16[2,256,128]{2,1,0:T(8,128)(2,1)S(1)}, u32[]{:S(2)}, u32[]{:S(2)}) %collective-permute-start.9) | collective-permute-done | bytes 131104 | tf_op jit(solution)/shard_map/ppermute | solution.py:373
  22.8 1.3 %collective-permute-start.10 = (bf16[2,256,128]{2,1,0:T(8,128)(2,1)S(1)}, bf16[2,256,128]{2,1,0:T(8,128)(2,1)S(1)}, u32[]{:S(2)}, u32[]{:S(2)}) collective-permute-start(bf16[2,256,128]{2,1,0:T(8,128)(2,1)S(1)} %collective-permute-done.9.refs_3_), channel_id=1, source_target_pairs={{4,0},{5,1},{6,2},{7,3},{8,4},{9,5},{10,6},{11,7},{20,16},{21,17},... | collective-permute-start | bytes 393224 | tf_op jit(solution)/shard_map/ppermute | solution.py:373
  24.1 7.4 %collective-permute-done.5.refs_3_ = bf16[2,256,128]{2,1,0:T(8,128)(2,1)S(1)} collective-permute-done((bf16[2,256,128]{2,1,0:T(8,128)(2,1)S(1)}, bf16[2,256,128]{2,1,0:T(8,128)(2,1)S(1)}, u32[]{:S(2)}, u32[]{:S(2)}) %collective-permute-start.5) | collective-permute-done | bytes 131104 | tf_op jit(solution)/shard_map/ppermute | solution.py:373
  33.9 1.3 %collective-permute-start.17 = (bf16[4,256,128]{2,1,0:T(8,128)(2,1)S(1)}, bf16[4,256,128]{2,1,0:T(8,128)(2,1)S(1)}, u32[]{:S(2)}, u32[]{:S(2)}) collective-permute-start(bf16[4,256,128]{2,1,0:T(8,128)(2,1)S(1)} %team_joined.2.refs_4_.refs_2_), channel_id=1, source_target_pairs={{4,0},{5,1},{6,2},{7,3},{20,16},{21,17},{22,18},{23,19}} | collective-permute-start | bytes 786440 | tf_op jit(solution)/shard_map/ppermute | solution.py:373
  35.2 1.7 %cross.4 = (bf16[2,256,128]{2,1,0:T(8,128)(2,1)S(1)}, bf16[2,256,128]{2,1,0:T(8,128)(2,1)S(1)}) custom-call(s32[16]{0:T(128)S(1)} %copy-done.1, bf16[4,256,128]{2,1,0:T(8,128)(2,1)S(1)} %joined.1.refs_0_, bf16[2,256,128]{2,1,0:T(8,128)(2,1)S(1)} %far_joined.3.refs_1_, bf16[4,256,128]{2,1,0:T(8,128)(2,1)S(1)} %collective-permute-done.3.refs_2_, ...), custom_call_target="tpu_custom_call" | custom-call | flops 576750016 | tf_op jit(solution)/shard_map/cross/pallas_call | solution.py:276
  36.9 1.6 %collective-permute-done.6.far = bf16[2,256,128]{2,1,0:T(8,128)(2,1)S(1)} collective-permute-done((bf16[2,256,128]{2,1,0:T(8,128)(2,1)S(1)}, bf16[2,256,128]{2,1,0:T(8,128)(2,1)S(1)}, u32[]{:S(2)}, u32[]{:S(2)}) %collective-permute-start.6) | collective-permute-done | bytes 131104 | tf_op jit(solution)/shard_map/ppermute | solution.py:373
  38.5 1.3 %collective-permute-start.11 = (bf16[4,256,128]{2,1,0:T(8,128)(2,1)S(1)}, bf16[4,256,128]{2,1,0:T(8,128)(2,1)S(1)}, u32[]{:S(2)}, u32[]{:S(2)}) collective-permute-start(bf16[4,256,128]{2,1,0:T(8,128)(2,1)S(1)} %team_joined.3.refs_2_.refs_4_), channel_id=1, source_target_pairs={{4,0},{5,1},{6,2},{7,3},{20,16},{21,17},{22,18},{23,19}} | collective-permute-start | bytes 786440 | tf_op jit(solution)/shard_map/ppermute | solution.py:373
  39.8 1.7 %cross.7 = (bf16[2,256,128]{2,1,0:T(8,128)(2,1)S(1)}, bf16[2,256,128]{2,1,0:T(8,128)(2,1)S(1)}) custom-call(s32[16]{0:T(128)S(1)} %copy-done.1, bf16[4,256,128]{2,1,0:T(8,128)(2,1)S(1)} %joined.1.refs_0_, bf16[2,256,128]{2,1,0:T(8,128)(2,1)S(1)} %far_joined.2.refs_1_, bf16[4,256,128]{2,1,0:T(8,128)(2,1)S(1)} %collective-permute-done.3.refs_2_, ...), custom_call_target="tpu_custom_call" | custom-call | flops 576750016 | tf_op jit(solution)/shard_map/cross/pallas_call | solution.py:276
  41.5 1.3 %collective-permute-start.20 = (bf16[2,256,128]{2,1,0:T(8,128)(2,1)S(1)}, bf16[2,256,128]{2,1,0:T(8,128)(2,1)S(1)}, u32[]{:S(2)}, u32[]{:S(2)}) collective-permute-start(bf16[2,256,128]{2,1,0:T(8,128)(2,1)S(1)} %get-tuple-element.37), channel_id=1, source_target_pairs={{0,2},{1,3},{2,0},{3,1},{4,6},{5,7},{6,4},{7,5},{8,10},{9,11},{10,... | collective-permute-start | bytes 393224 | tf_op jit(solution)/shard_map/ppermute | solution.py:369
  43.6 1.4 %collective-permute-done.17.refs_3_ = bf16[4,256,128]{2,1,0:T(8,128)(2,1)S(1)} collective-permute-done((bf16[4,256,128]{2,1,0:T(8,128)(2,1)S(1)}, bf16[4,256,128]{2,1,0:T(8,128)(2,1)S(1)}, u32[]{:S(2)}, u32[]{:S(2)}) %collective-permute-start.17) | collective-permute-done | bytes 262176 | tf_op jit(solution)/shard_map/ppermute | solution.py:373
  45.0 1.7 %cross.6 = (bf16[2,256,128]{2,1,0:T(8,128)(2,1)S(1)}, bf16[2,256,128]{2,1,0:T(8,128)(2,1)S(1)}) custom-call(s32[16]{0:T(128)S(1)} %copy-done.1, bf16[4,256,128]{2,1,0:T(8,128)(2,1)S(1)} %joined.1.refs_0_, bf16[2,256,128]{2,1,0:T(8,128)(2,1)S(1)} %far_joined.3.refs_1_, bf16[4,256,128]{2,1,0:T(8,128)(2,1)S(1)} %team_joined.2.refs_4_.refs_2_, ...), custom_call_target="tpu_custom_call" | custom-call | flops 576750016 | tf_op jit(solution)/shard_map/cross/pallas_call | solution.py:276
  46.7 1.3 %collective-permute-start.23 = (bf16[2,256,128]{2,1,0:T(8,128)(2,1)S(1)}, bf16[2,256,128]{2,1,0:T(8,128)(2,1)S(1)}, u32[]{:S(2)}, u32[]{:S(2)}) collective-permute-start(bf16[2,256,128]{2,1,0:T(8,128)(2,1)S(1)} %get-tuple-element.39), channel_id=1, source_target_pairs={{0,2},{1,3},{2,0},{3,1},{4,6},{5,7},{6,4},{7,5},{8,10},{9,11},{10,... | collective-permute-start | bytes 393224 | tf_op jit(solution)/shard_map/ppermute | solution.py:369
  49.5 1.7 %cross.5 = (bf16[2,256,128]{2,1,0:T(8,128)(2,1)S(1)}, bf16[1,256,128]{2,1,0:T(8,128)(2,1)S(1)}, bf16[1,256,128]{2,1,0:T(8,128)(2,1)S(1)}) custom-call(s32[16]{0:T(128)S(1)} %copy-done.1, bf16[4,256,128]{2,1,0:T(8,128)(2,1)S(1)} %joined.1.refs_0_, bf16[2,256,128]{2,1,0:T(8,128)(2,1)S(1)} %far_joined.2.refs_1_, ...), custom_call_target="tpu_custom_call" | custom-call | flops 576750016 | tf_op jit(solution)/shard_map/cross/pallas_call | solution.py:276
  54.1 1.9 %lags_early.1 = (f32[256,2048]{1,0:T(8,128)S(1)}, f32[256,2048]{1,0:T(8,128)S(1)}) custom-call(bf16[2,256,128]{2,1,0:T(8,128)(2,1)S(1)} %get-tuple-element.28.refs_0_, bf16[2,256,128]{2,1,0:T(8,128)(2,1)S(1)} %collective-permute-done.15.refs_1_, bf16[2,256,128]{2,1,0:T(8,128)(2,1)S(1)} %collective-permute-done.16.refs_2_, ...), custom_call_target="tpu_custom_call" | custom-call | flops 115350000 | tf_op jit(solution)/shard_map/lags_early/pallas_call | solution.py:331
  57.9 1.7 %lags_late.1 = bf16[32,16,2048]{2,1,0:T(8,128)(2,1)} custom-call(bf16[2,256,128]{2,1,0:T(8,128)(2,1)S(1)} %get-tuple-element.30.refs_0_, bf16[2,256,128]{2,1,0:T(8,128)(2,1)S(1)} %collective-permute-done.12.refs_1_, bf16[1,256,128]{2,1,0:T(8,128)(2,1)S(1)} %collective-permute-done.13.refs_2_, bf16[1,256,128]{2,1,0:T(8,128)(2,1)S(1)} %collective-permute-done.14.refs_3_, ...), custom_call_target="tpu_custom_call" | custom-call | flops 2307000064 | tf_op jit(solution)/shard_map/lags_late/pallas_call | solution.py:345
  (42 shorter events, 11.4 us)
Async XLA Ops:
  4.1 3.1 %collective-permute-start = (bf16[2,256,128]{2,1,0:T(8,128)(2,1)S(1)}, bf16[2,256,128]{2,1,0:T(8,128)(2,1)S(1)}, u32[]{:S(2)}, u32[]{:S(2)}) collective-permute-start(bf16[2,256,128]{2,1,0:T(8,128)(2,1)S(1)} %get-tuple-element.25), channel_id=1, source_target_pairs={{0,1},{1,0},{2,3},{3,2},{4,5},{5,4},{6,7},{7,6},{8,9},{9,8},{10,11... | collective-permute-start | bytes 393224 | tf_op jit(solution)/shard_map/ppermute | solution.py:369
  4.6 6.7 %collective-permute-start.7 = (bf16[2,256,128]{2,1,0:T(8,128)(2,1)S(1)}, bf16[2,256,128]{2,1,0:T(8,128)(2,1)S(1)}, u32[]{:S(2)}, u32[]{:S(2)}) collective-permute-start(bf16[2,256,128]{2,1,0:T(8,128)(2,1)S(1)} %get-tuple-element.27), channel_id=1, source_target_pairs={{0,2},{1,3},{2,0},{3,1},{4,6},{5,7},{6,4},{7,5},{8,10},{9,11},{10,... | collective-permute-start | bytes 393224 | tf_op jit(solution)/shard_map/ppermute | solution.py:369
  7.2 10.3 %collective-permute-start.3 = (bf16[4,256,128]{2,1,0:T(8,128)(2,1)S(1)}, bf16[4,256,128]{2,1,0:T(8,128)(2,1)S(1)}, u32[]{:S(2)}, u32[]{:S(2)}) collective-permute-start(bf16[4,256,128]{2,1,0:T(8,128)(2,1)S(1)} %joined.1.refs_0_), channel_id=1, source_target_pairs={{4,0},{5,1},{6,2},{7,3},{8,4},{9,5},{10,6},{11,7},{12,8},{13,9},{1... | collective-permute-start | bytes 786440 | tf_op jit(solution)/shard_map/ppermute | solution.py:373
  8.5 5.6 %collective-permute-start.1 = (bf16[2,256,128]{2,1,0:T(8,128)(2,1)S(1)}, bf16[2,256,128]{2,1,0:T(8,128)(2,1)S(1)}, u32[]{:S(2)}, u32[]{:S(2)}) collective-permute-start(bf16[2,256,128]{2,1,0:T(8,128)(2,1)S(1)} %get-tuple-element.26), channel_id=1, source_target_pairs={{0,2},{1,3},{2,0},{3,1},{4,6},{5,7},{6,4},{7,5},{8,10},{9,11},{10,... | collective-permute-start | bytes 393224 | tf_op jit(solution)/shard_map/ppermute | solution.py:369
  11.3 2.9 %collective-permute-start.8 = (bf16[2,256,128]{2,1,0:T(8,128)(2,1)S(1)}, bf16[2,256,128]{2,1,0:T(8,128)(2,1)S(1)}, u32[]{:S(2)}, u32[]{:S(2)}) collective-permute-start(bf16[2,256,128]{2,1,0:T(8,128)(2,1)S(1)} %collective-permute-done.7.straight), channel_id=1, source_target_pairs={{0,1},{1,0},{2,3},{3,2},{4,5},{5,4},{6,7},{7,6},{8,9},{9,8},{10,11... | collective-permute-start | bytes 393224 | tf_op jit(solution)/shard_map/ppermute | solution.py:369
  14.2 4.6 %collective-permute-start.2 = (bf16[2,256,128]{2,1,0:T(8,128)(2,1)S(1)}, bf16[2,256,128]{2,1,0:T(8,128)(2,1)S(1)}, u32[]{:S(2)}, u32[]{:S(2)}) collective-permute-start(bf16[2,256,128]{2,1,0:T(8,128)(2,1)S(1)} %collective-permute-done.1.straight), channel_id=1, source_target_pairs={{0,1},{1,0},{2,3},{3,2},{4,5},{5,4},{6,7},{7,6},{8,9},{9,8},{10,11... | collective-permute-start | bytes 393224 | tf_op jit(solution)/shard_map/ppermute | solution.py:369
  14.2 8.6 %collective-permute-start.9 = (bf16[2,256,128]{2,1,0:T(8,128)(2,1)S(1)}, bf16[2,256,128]{2,1,0:T(8,128)(2,1)S(1)}, u32[]{:S(2)}, u32[]{:S(2)}) collective-permute-start(bf16[2,256,128]{2,1,0:T(8,128)(2,1)S(1)} %far_joined.3.refs_1_), channel_id=1, source_target_pairs={{4,0},{5,1},{6,2},{7,3},{8,4},{9,5},{10,6},{11,7},{12,8},{13,9},{1... | collective-permute-start | bytes 393224 | tf_op jit(solution)/shard_map/ppermute | solution.py:373
  17.5 16.4 %collective-permute-start.4 = (bf16[4,256,128]{2,1,0:T(8,128)(2,1)S(1)}, bf16[4,256,128]{2,1,0:T(8,128)(2,1)S(1)}, u32[]{:S(2)}, u32[]{:S(2)}) collective-permute-start(bf16[4,256,128]{2,1,0:T(8,128)(2,1)S(1)} %collective-permute-done.3.refs_2_), channel_id=1, source_target_pairs={{4,0},{5,1},{6,2},{7,3},{8,4},{9,5},{10,6},{11,7},{20,16},{21,17},... | collective-permute-start | bytes 786440 | tf_op jit(solution)/shard_map/ppermute | solution.py:373
  18.8 12.6 %collective-permute-start.5 = (bf16[2,256,128]{2,1,0:T(8,128)(2,1)S(1)}, bf16[2,256,128]{2,1,0:T(8,128)(2,1)S(1)}, u32[]{:S(2)}, u32[]{:S(2)}) collective-permute-start(bf16[2,256,128]{2,1,0:T(8,128)(2,1)S(1)} %far_joined.2.refs_1_), channel_id=1, source_target_pairs={{4,0},{5,1},{6,2},{7,3},{8,4},{9,5},{10,6},{11,7},{12,8},{13,9},{1... | collective-permute-start | bytes 393224 | tf_op jit(solution)/shard_map/ppermute | solution.py:373
  22.8 11.1 %collective-permute-start.10 = (bf16[2,256,128]{2,1,0:T(8,128)(2,1)S(1)}, bf16[2,256,128]{2,1,0:T(8,128)(2,1)S(1)}, u32[]{:S(2)}, u32[]{:S(2)}) collective-permute-start(bf16[2,256,128]{2,1,0:T(8,128)(2,1)S(1)} %collective-permute-done.9.refs_3_), channel_id=1, source_target_pairs={{4,0},{5,1},{6,2},{7,3},{8,4},{9,5},{10,6},{11,7},{20,16},{21,17},... | collective-permute-start | bytes 393224 | tf_op jit(solution)/shard_map/ppermute | solution.py:373
  31.4 7.0 %collective-permute-start.6 = (bf16[2,256,128]{2,1,0:T(8,128)(2,1)S(1)}, bf16[2,256,128]{2,1,0:T(8,128)(2,1)S(1)}, u32[]{:S(2)}, u32[]{:S(2)}) collective-permute-start(bf16[2,256,128]{2,1,0:T(8,128)(2,1)S(1)} %collective-permute-done.5.refs_3_), channel_id=1, source_target_pairs={{4,0},{5,1},{6,2},{7,3},{8,4},{9,5},{10,6},{11,7},{20,16},{21,17},... | collective-permute-start | bytes 393224 | tf_op jit(solution)/shard_map/ppermute | solution.py:373
  33.9 11.1 %collective-permute-start.17 = (bf16[4,256,128]{2,1,0:T(8,128)(2,1)S(1)}, bf16[4,256,128]{2,1,0:T(8,128)(2,1)S(1)}, u32[]{:S(2)}, u32[]{:S(2)}) collective-permute-start(bf16[4,256,128]{2,1,0:T(8,128)(2,1)S(1)} %team_joined.2.refs_4_.refs_2_), channel_id=1, source_target_pairs={{4,0},{5,1},{6,2},{7,3},{20,16},{21,17},{22,18},{23,19}} | collective-permute-start | bytes 786440 | tf_op jit(solution)/shard_map/ppermute | solution.py:373
  38.5 11.0 %collective-permute-start.11 = (bf16[4,256,128]{2,1,0:T(8,128)(2,1)S(1)}, bf16[4,256,128]{2,1,0:T(8,128)(2,1)S(1)}, u32[]{:S(2)}, u32[]{:S(2)}) collective-permute-start(bf16[4,256,128]{2,1,0:T(8,128)(2,1)S(1)} %team_joined.3.refs_2_.refs_4_), channel_id=1, source_target_pairs={{4,0},{5,1},{6,2},{7,3},{20,16},{21,17},{22,18},{23,19}} | collective-permute-start | bytes 786440 | tf_op jit(solution)/shard_map/ppermute | solution.py:373
  41.5 6.5 %collective-permute-start.20 = (bf16[2,256,128]{2,1,0:T(8,128)(2,1)S(1)}, bf16[2,256,128]{2,1,0:T(8,128)(2,1)S(1)}, u32[]{:S(2)}, u32[]{:S(2)}) collective-permute-start(bf16[2,256,128]{2,1,0:T(8,128)(2,1)S(1)} %get-tuple-element.37), channel_id=1, source_target_pairs={{0,2},{1,3},{2,0},{3,1},{4,6},{5,7},{6,4},{7,5},{8,10},{9,11},{10,... | collective-permute-start | bytes 393224 | tf_op jit(solution)/shard_map/ppermute | solution.py:369
  42.8 5.7 %collective-permute-start.16 = (bf16[2,256,128]{2,1,0:T(8,128)(2,1)S(1)}, bf16[2,256,128]{2,1,0:T(8,128)(2,1)S(1)}, u32[]{:S(2)}, u32[]{:S(2)}) collective-permute-start(bf16[2,256,128]{2,1,0:T(8,128)(2,1)S(1)} %get-tuple-element.33), channel_id=1, source_target_pairs={{0,2},{1,3},{2,0},{3,1},{4,6},{5,7},{6,4},{7,5},{8,10},{9,11},{10,... | collective-permute-start | bytes 393224 | tf_op jit(solution)/shard_map/ppermute | solution.py:369
  46.7 5.0 %collective-permute-start.23 = (bf16[2,256,128]{2,1,0:T(8,128)(2,1)S(1)}, bf16[2,256,128]{2,1,0:T(8,128)(2,1)S(1)}, u32[]{:S(2)}, u32[]{:S(2)}) collective-permute-start(bf16[2,256,128]{2,1,0:T(8,128)(2,1)S(1)} %get-tuple-element.39), channel_id=1, source_target_pairs={{0,2},{1,3},{2,0},{3,1},{4,6},{5,7},{6,4},{7,5},{8,10},{9,11},{10,... | collective-permute-start | bytes 393224 | tf_op jit(solution)/shard_map/ppermute | solution.py:369
  48.0 3.8 %collective-permute-start.19 = (bf16[2,256,128]{2,1,0:T(8,128)(2,1)S(1)}, bf16[2,256,128]{2,1,0:T(8,128)(2,1)S(1)}, u32[]{:S(2)}, u32[]{:S(2)}) collective-permute-start(bf16[2,256,128]{2,1,0:T(8,128)(2,1)S(1)} %get-tuple-element.36.refs_4_), channel_id=1, source_target_pairs={{0,1},{1,0},{2,3},{3,2},{4,5},{5,4},{6,7},{7,6},{8,9},{9,8},{10,11... | collective-permute-start | bytes 393224 | tf_op jit(solution)/shard_map/ppermute | solution.py:369
  48.0 4.2 %collective-permute-start.15 = (bf16[2,256,128]{2,1,0:T(8,128)(2,1)S(1)}, bf16[2,256,128]{2,1,0:T(8,128)(2,1)S(1)}, u32[]{:S(2)}, u32[]{:S(2)}) collective-permute-start(bf16[2,256,128]{2,1,0:T(8,128)(2,1)S(1)} %get-tuple-element.28.refs_0_), channel_id=1, source_target_pairs={{0,1},{1,0},{2,3},{3,2},{4,5},{5,4},{6,7},{7,6},{8,9},{9,8},{10,11... | collective-permute-start | bytes 393224 | tf_op jit(solution)/shard_map/ppermute | solution.py:369
  48.5 3.8 %collective-permute-start.18 = (bf16[2,256,128]{2,1,0:T(8,128)(2,1)S(1)}, bf16[2,256,128]{2,1,0:T(8,128)(2,1)S(1)}, u32[]{:S(2)}, u32[]{:S(2)}) collective-permute-start(bf16[2,256,128]{2,1,0:T(8,128)(2,1)S(1)} %collective-permute-done.16.refs_2_), channel_id=1, source_target_pairs={{0,1},{1,0},{2,3},{3,2},{4,5},{5,4},{6,7},{7,6},{8,9},{9,8},{10,11... | collective-permute-start | bytes 393224 | tf_op jit(solution)/shard_map/ppermute | solution.py:369
  49.5 4.1 %collective-permute-start.21 = (bf16[2,256,128]{2,1,0:T(8,128)(2,1)S(1)}, bf16[2,256,128]{2,1,0:T(8,128)(2,1)S(1)}, u32[]{:S(2)}, u32[]{:S(2)}) collective-permute-start(bf16[2,256,128]{2,1,0:T(8,128)(2,1)S(1)} %collective-permute-done.20.refs_6_), channel_id=1, source_target_pairs={{0,1},{1,0},{2,3},{3,2},{4,5},{5,4},{6,7},{7,6},{8,9},{9,8},{10,11... | collective-permute-start | bytes 393224 | tf_op jit(solution)/shard_map/ppermute | solution.py:369
  51.7 2.4 %collective-permute-start.22 = (bf16[2,256,128]{2,1,0:T(8,128)(2,1)S(1)}, bf16[2,256,128]{2,1,0:T(8,128)(2,1)S(1)}, u32[]{:S(2)}, u32[]{:S(2)}) collective-permute-start(bf16[2,256,128]{2,1,0:T(8,128)(2,1)S(1)} %get-tuple-element.34.refs_8_), channel_id=1, source_target_pairs={{0,1},{1,0},{2,3},{3,2},{4,5},{5,4},{6,7},{7,6},{8,9},{9,8},{10,11... | collective-permute-start | bytes 393224 | tf_op jit(solution)/shard_map/ppermute | solution.py:369
  52.2 5.7 %collective-permute-start.12 = (bf16[2,256,128]{2,1,0:T(8,128)(2,1)S(1)}, bf16[2,256,128]{2,1,0:T(8,128)(2,1)S(1)}, u32[]{:S(2)}, u32[]{:S(2)}) collective-permute-start(bf16[2,256,128]{2,1,0:T(8,128)(2,1)S(1)} %get-tuple-element.30.refs_0_), channel_id=1, source_target_pairs={{0,1},{1,0},{2,3},{3,2},{4,5},{5,4},{6,7},{7,6},{8,9},{9,8},{10,11... | collective-permute-start | bytes 393224 | tf_op jit(solution)/shard_map/ppermute | solution.py:369
  52.3 4.7 %collective-permute-start.13 = (bf16[1,256,128]{2,1,0:T(8,128)(2,1)S(1)}, bf16[1,256,128]{2,1,0:T(8,128)(2,1)S(1)}, u32[]{:S(2)}, u32[]{:S(2)}) collective-permute-start(bf16[1,256,128]{2,1,0:T(8,128)(2,1)S(1)} %get-tuple-element.31), channel_id=1, source_target_pairs={{0,2},{1,3},{2,0},{3,1},{4,6},{5,7},{6,4},{7,5},{8,10},{9,11},{10,... | collective-permute-start | bytes 196616 | tf_op jit(solution)/shard_map/ppermute | solution.py:369
  53.6 4.3 %collective-permute-start.14 = (bf16[1,256,128]{2,1,0:T(8,128)(2,1)S(1)}, bf16[1,256,128]{2,1,0:T(8,128)(2,1)S(1)}, u32[]{:S(2)}, u32[]{:S(2)}) collective-permute-start(bf16[1,256,128]{2,1,0:T(8,128)(2,1)S(1)} %get-tuple-element.32), channel_id=1, source_target_pairs={{0,3},{1,2},{2,1},{3,0},{4,7},{5,6},{6,5},{7,4},{8,11},{9,10},{10,... | collective-permute-start | bytes 196616 | tf_op jit(solution)/shard_map/ppermute | solution.py:369
  (3 other events, 41.6 us)

commit v6 on v5

--- a/solution.py
+++ b/solution.py
@@ -391,22 +391,32 @@
             return near, swapped(after(far, *before), 2)
 
         def gathered(near, back, *others):
-            return near, swapped(near, 1), back, swapped(after(back, *others), 1)
-
+            return near, swapped(after(near, *others), 1), back, swapped(after(back, *others), 1)
+
+        lower_planes = (span - 1 + middle * (BAND // number)) // span
         chunks = [own]
         low = []
         for hops in range(1, reach + 1):
-            arrived = [down(c, hops) for c in chunks[-1]]
+            last = chunks[-1]
+            if hops == JOIN:
+                last = [last[0], after(last[1], last[2]), last[2]]
+            arrived = [down(c, hops) for c in last]
+            early = hops == lower_planes and hops >= JOIN
             if hops == JOIN:
                 first = team_joined(0, arrived[0], arrived[1])
+            elif hops > JOIN:
+                first = arrived[0]
+            if early:
                 low = [crossed((0,), 0, middle, chunks + [[first, None]])]
-                arrived = [first, team_joined(1, arrived[0], after(arrived[2], low[0][0]))]
+                arrived[-1] = after(arrived[-1], low[0][0])
+            if hops == JOIN:
+                arrived = [first, team_joined(1, arrived[0], arrived[2])]
             chunks.append(arrived)
         for half in range(len(low), HALVES):
             low.append(crossed((half,), 0, middle, chunks))
         near0, back0 = crossed((0,), middle, number, chunks)
         near1, across1, diagonal1 = cross(windows, count, (1,), middle, number, offsets, chunks, True)
-        low = gathered(*low[0], near0) + gathered(*low[1], near0)
+        low = gathered(*low[0]) + gathered(*low[1])
         high = gathered(near0, back0, near1)
         lower, upper = lags_early(low, high, inverse)
         rest = near1, swapped(near1, 1), swapped(across1, 2), swapped(diagonal1, 3)

time: 59.9 us -> 59.8 us (level)
    ppermute x17, waiting for transfers between devices: 6.69 us -> 7.97 us  [swapped(): return lax.ppermute(value, 'chan', [(i, i ^ by) for i in range(ring)])]
    ppermute x8, waiting for transfers between devices: 17.1 us -> 15.9 us  [down(): return lax.ppermute(value, 'chan', pairs)]
  transfers between devices with their start and end apart: 25 -> 25, of which waited for: 12 -> 10; matrix products, arithmetic and copies ran while one was open for 0% -> 0% of each run, Pallas kernels for 15% -> 15%
where the time goes in v6:
time: 59.8 us; the launch traced here: 59.5 us
  waiting for transfers between devices  23.8 us (40%)
  starting transfers between devices  20.9 us (35%)
  Pallas kernels  14.6 us (24%)
    ppermute x8, waiting for transfers between devices, down(): return lax.ppermute(value, 'chan', pairs)  15.9 us
    ppermute x17, starting transfers between devices, swapped(): return lax.ppermute(value, 'chan', [(i, i ^ by) for i in range(ring)])  10.6 us
    ppermute x8, starting transfers between devices, down(): return lax.ppermute(value, 'chan', pairs)  10.3 us
    ppermute x17, waiting for transfers between devices, swapped(): return lax.ppermute(value, 'chan', [(i, i ^ by) for i in range(ring)])  7.97 us
    pallas_call x4, Pallas kernels, cross(): pl.pallas_call(functools.partial(cross_kernel, windows, count, halves, si...  6.87 us
    pallas_call x1, Pallas kernels, spectra(): pl.pallas_call(functools.partial(spectra_kernel, windows), in_specs=[pl.B...  4.08 us
    pallas_call x1, Pallas kernels, lags_early(): pl.pallas_call(functools.partial(early_kernel, 512), in_specs=[vmem] * (l...  1.91 us
    pallas_call x1, Pallas kernels, lags_late(): pl.pallas_call(functools.partial(late_kernel, count, tile), in_specs=[vme...  1.69 us
  transfers between devices with their start and end apart: 25, of which 10 were waited for; matrix products, arithmetic and copies ran while one was open for 0% of the time, Pallas kernels for 15%

profile of v6, /device:TPU:0, one launch (start us, length us, event | category | flops | bytes accessed | tf_op | source)
XLA Modules:
  0.0 59.5 jit_solution(12479795135478310155)
XLA Ops:
  0.0 4.1 %spectra.1 = (bf16[2,256,128]{2,1,0:T(8,128)(2,1)S(1)}, bf16[2,256,128]{2,1,0:T(8,128)(2,1)S(1)}, bf16[2,256,128]{2,1,0:T(8,128)(2,1)S(1)}, bf16[2,256,128]{2,1,0:T(8,128)(2,1)S(1)}) custom-call(bf16[256,3000]{1,0:T(8,128)(2,1)} %bitcast.2, bf16[2,750,512]{2,1,0:T(8,128)(2,1)} %constant.4.clone.table_hbm, s32[1,32]{1,0:T(1,128)} %bitcast.3), custom_call_target="tpu_custom_call" | custom-call | flops 3460499968 | tf_op jit(solution)/shard_map/spectra/pallas_call | solution.py:118
  4.6 2.6 %collective-permute-start.1 = (bf16[2,256,128]{2,1,0:T(8,128)(2,1)S(1)}, bf16[2,256,128]{2,1,0:T(8,128)(2,1)S(1)}, u32[]{:S(2)}, u32[]{:S(2)}) collective-permute-start(bf16[2,256,128]{2,1,0:T(8,128)(2,1)S(1)} %get-tuple-element.26), channel_id=1, source_target_pairs={{0,2},{1,3},{2,0},{3,1},{4,6},{5,7},{6,4},{7,5},{8,10},{9,11},{10,... | collective-permute-start | bytes 393224 | tf_op jit(solution)/shard_map/ppermute | solution.py:369
  7.3 1.3 %collective-permute-start.3 = (bf16[4,256,128]{2,1,0:T(8,128)(2,1)S(1)}, bf16[4,256,128]{2,1,0:T(8,128)(2,1)S(1)}, u32[]{:S(2)}, u32[]{:S(2)}) collective-permute-start(bf16[4,256,128]{2,1,0:T(8,128)(2,1)S(1)} %joined.1.refs_0_), channel_id=1, source_target_pairs={{4,0},{5,1},{6,2},{7,3},{8,4},{9,5},{10,6},{11,7},{12,8},{13,9},{1... | collective-permute-start | bytes 786440 | tf_op jit(solution)/shard_map/ppermute | solution.py:373
  8.6 2.9 %collective-permute-done.1.straight = bf16[2,256,128]{2,1,0:T(8,128)(2,1)S(1)} collective-permute-done((bf16[2,256,128]{2,1,0:T(8,128)(2,1)S(1)}, bf16[2,256,128]{2,1,0:T(8,128)(2,1)S(1)}, u32[]{:S(2)}, u32[]{:S(2)}) %collective-permute-start.1) | collective-permute-done | bytes 131104 | tf_op jit(solution)/shard_map/ppermute | solution.py:369
  11.5 2.5 %collective-permute-done.7.straight = bf16[2,256,128]{2,1,0:T(8,128)(2,1)S(1)} collective-permute-done((bf16[2,256,128]{2,1,0:T(8,128)(2,1)S(1)}, bf16[2,256,128]{2,1,0:T(8,128)(2,1)S(1)}, u32[]{:S(2)}, u32[]{:S(2)}) %collective-permute-start.7) | collective-permute-done | bytes 131104 | tf_op jit(solution)/shard_map/ppermute | solution.py:369
  14.1 1.3 %collective-permute-start.5 = (bf16[2,256,128]{2,1,0:T(8,128)(2,1)S(1)}, bf16[2,256,128]{2,1,0:T(8,128)(2,1)S(1)}, u32[]{:S(2)}, u32[]{:S(2)}) collective-permute-start(bf16[2,256,128]{2,1,0:T(8,128)(2,1)S(1)} %far_joined.2.refs_1_), channel_id=1, source_target_pairs={{4,0},{5,1},{6,2},{7,3},{8,4},{9,5},{10,6},{11,7},{12,8},{13,9},{1... | collective-permute-start | bytes 393224 | tf_op jit(solution)/shard_map/ppermute | solution.py:373
  15.5 1.3 %collective-permute-start.9 = (bf16[2,256,128]{2,1,0:T(8,128)(2,1)S(1)}, bf16[2,256,128]{2,1,0:T(8,128)(2,1)S(1)}, u32[]{:S(2)}, u32[]{:S(2)}) collective-permute-start(bf16[2,256,128]{2,1,0:T(8,128)(2,1)S(1)} %far_joined.3.refs_1_), channel_id=1, source_target_pairs={{4,0},{5,1},{6,2},{7,3},{8,4},{9,5},{10,6},{11,7},{12,8},{13,9},{1... | collective-permute-start | bytes 393224 | tf_op jit(solution)/shard_map/ppermute | solution.py:373
  18.9 3.4 %collective-permute-done.5.refs_3_ = bf16[2,256,128]{2,1,0:T(8,128)(2,1)S(1)} collective-permute-done((bf16[2,256,128]{2,1,0:T(8,128)(2,1)S(1)}, bf16[2,256,128]{2,1,0:T(8,128)(2,1)S(1)}, u32[]{:S(2)}, u32[]{:S(2)}) %collective-permute-start.5) | collective-permute-done | bytes 131104 | tf_op jit(solution)/shard_map/ppermute | solution.py:373
  22.3 2.8 %collective-permute-done.9.refs_3_ = bf16[2,256,128]{2,1,0:T(8,128)(2,1)S(1)} collective-permute-done((bf16[2,256,128]{2,1,0:T(8,128)(2,1)S(1)}, bf16[2,256,128]{2,1,0:T(8,128)(2,1)S(1)}, u32[]{:S(2)}, u32[]{:S(2)}) %collective-permute-start.9) | collective-permute-done | bytes 131104 | tf_op jit(solution)/shard_map/ppermute | solution.py:373
  26.4 1.3 %collective-permute-start.6 = (bf16[2,256,128]{2,1,0:T(8,128)(2,1)S(1)}, bf16[2,256,128]{2,1,0:T(8,128)(2,1)S(1)}, u32[]{:S(2)}, u32[]{:S(2)}) collective-permute-start(bf16[2,256,128]{2,1,0:T(8,128)(2,1)S(1)} %collective-permute-done.5.refs_3_), channel_id=1, source_target_pairs={{4,0},{5,1},{6,2},{7,3},{8,4},{9,5},{10,6},{11,7},{20,16},{21,17},... | collective-permute-start | bytes 393224 | tf_op jit(solution)/shard_map/ppermute | solution.py:373
  27.7 5.8 %collective-permute-done.10.far = bf16[2,256,128]{2,1,0:T(8,128)(2,1)S(1)} collective-permute-done((bf16[2,256,128]{2,1,0:T(8,128)(2,1)S(1)}, bf16[2,256,128]{2,1,0:T(8,128)(2,1)S(1)}, u32[]{:S(2)}, u32[]{:S(2)}) %collective-permute-start.10) | collective-permute-done | bytes 131104 | tf_op jit(solution)/shard_map/ppermute | solution.py:373
  33.6 1.3 %collective-permute-start.21 = (bf16[4,256,128]{2,1,0:T(8,128)(2,1)S(1)}, bf16[4,256,128]{2,1,0:T(8,128)(2,1)S(1)}, u32[]{:S(2)}, u32[]{:S(2)}) collective-permute-start(bf16[4,256,128]{2,1,0:T(8,128)(2,1)S(1)} %team_joined.2.refs_4_.refs_2_), channel_id=1, source_target_pairs={{4,0},{5,1},{6,2},{7,3},{20,16},{21,17},{22,18},{23,19}} | collective-permute-start | bytes 786440 | tf_op jit(solution)/shard_map/ppermute | solution.py:373
  34.9 1.7 %cross.4 = (bf16[2,256,128]{2,1,0:T(8,128)(2,1)S(1)}, bf16[2,256,128]{2,1,0:T(8,128)(2,1)S(1)}) custom-call(s32[16]{0:T(128)S(1)} %copy-done.1, bf16[4,256,128]{2,1,0:T(8,128)(2,1)S(1)} %joined.1.refs_0_, bf16[2,256,128]{2,1,0:T(8,128)(2,1)S(1)} %far_joined.3.refs_1_, bf16[4,256,128]{2,1,0:T(8,128)(2,1)S(1)} %collective-permute-done.3.refs_2_, ...), custom_call_target="tpu_custom_call" | custom-call | flops 576750016 | tf_op jit(solution)/shard_map/cross/pallas_call | solution.py:276
  36.6 1.3 %collective-permute-start.11 = (bf16[4,256,128]{2,1,0:T(8,128)(2,1)S(1)}, bf16[4,256,128]{2,1,0:T(8,128)(2,1)S(1)}, u32[]{:S(2)}, u32[]{:S(2)}) collective-permute-start(bf16[4,256,128]{2,1,0:T(8,128)(2,1)S(1)} %team_joined.3.refs_2_.refs_4_), channel_id=1, source_target_pairs={{4,0},{5,1},{6,2},{7,3},{20,16},{21,17},{22,18},{23,19}} | collective-permute-start | bytes 786440 | tf_op jit(solution)/shard_map/ppermute | solution.py:373
  37.9 1.7 %cross.6 = (bf16[2,256,128]{2,1,0:T(8,128)(2,1)S(1)}, bf16[2,256,128]{2,1,0:T(8,128)(2,1)S(1)}) custom-call(s32[16]{0:T(128)S(1)} %copy-done.1, bf16[4,256,128]{2,1,0:T(8,128)(2,1)S(1)} %joined.1.refs_0_, bf16[2,256,128]{2,1,0:T(8,128)(2,1)S(1)} %far_joined.2.refs_1_, bf16[4,256,128]{2,1,0:T(8,128)(2,1)S(1)} %collective-permute-done.3.refs_2_, ...), custom_call_target="tpu_custom_call" | custom-call | flops 576750016 | tf_op jit(solution)/shard_map/cross/pallas_call | solution.py:276
  39.6 1.8 %collective-permute-start.19 = (bf16[2,256,128]{2,1,0:T(8,128)(2,1)S(1)}, bf16[2,256,128]{2,1,0:T(8,128)(2,1)S(1)}, u32[]{:S(2)}, u32[]{:S(2)}) collective-permute-start(bf16[2,256,128]{2,1,0:T(8,128)(2,1)S(1)} %get-tuple-element.36), channel_id=1, source_target_pairs={{0,2},{1,3},{2,0},{3,1},{4,6},{5,7},{6,4},{7,5},{8,10},{9,11},{10,... | collective-permute-start | bytes 393224 | tf_op jit(solution)/shard_map/ppermute | solution.py:369
  41.7 3.0 %collective-permute-done.21.refs_3_ = bf16[4,256,128]{2,1,0:T(8,128)(2,1)S(1)} collective-permute-done((bf16[4,256,128]{2,1,0:T(8,128)(2,1)S(1)}, bf16[4,256,128]{2,1,0:T(8,128)(2,1)S(1)}, u32[]{:S(2)}, u32[]{:S(2)}) %collective-permute-start.21) | collective-permute-done | bytes 262176 | tf_op jit(solution)/shard_map/ppermute | solution.py:373
  44.7 1.7 %cross.7 = (bf16[2,256,128]{2,1,0:T(8,128)(2,1)S(1)}, bf16[2,256,128]{2,1,0:T(8,128)(2,1)S(1)}) custom-call(s32[16]{0:T(128)S(1)} %copy-done.1, bf16[4,256,128]{2,1,0:T(8,128)(2,1)S(1)} %joined.1.refs_0_, bf16[2,256,128]{2,1,0:T(8,128)(2,1)S(1)} %far_joined.3.refs_1_, bf16[4,256,128]{2,1,0:T(8,128)(2,1)S(1)} %team_joined.2.refs_4_.refs_2_, ...), custom_call_target="tpu_custom_call" | custom-call | flops 576750016 | tf_op jit(solution)/shard_map/cross/pallas_call | solution.py:276
  46.4 1.8 %collective-permute-start.23 = (bf16[2,256,128]{2,1,0:T(8,128)(2,1)S(1)}, bf16[2,256,128]{2,1,0:T(8,128)(2,1)S(1)}, u32[]{:S(2)}, u32[]{:S(2)}) collective-permute-start(bf16[2,256,128]{2,1,0:T(8,128)(2,1)S(1)} %get-tuple-element.39), channel_id=1, source_target_pairs={{0,2},{1,3},{2,0},{3,1},{4,6},{5,7},{6,4},{7,5},{8,10},{9,11},{10,... | collective-permute-start | bytes 393224 | tf_op jit(solution)/shard_map/ppermute | solution.py:369
  49.3 1.7 %cross.5 = (bf16[2,256,128]{2,1,0:T(8,128)(2,1)S(1)}, bf16[1,256,128]{2,1,0:T(8,128)(2,1)S(1)}, bf16[1,256,128]{2,1,0:T(8,128)(2,1)S(1)}) custom-call(s32[16]{0:T(128)S(1)} %copy-done.1, bf16[4,256,128]{2,1,0:T(8,128)(2,1)S(1)} %joined.1.refs_0_, bf16[2,256,128]{2,1,0:T(8,128)(2,1)S(1)} %far_joined.2.refs_1_, ...), custom_call_target="tpu_custom_call" | custom-call | flops 576750016 | tf_op jit(solution)/shard_map/cross/pallas_call | solution.py:276
  52.0 1.8 %collective-permute-start.13 = (bf16[1,256,128]{2,1,0:T(8,128)(2,1)S(1)}, bf16[1,256,128]{2,1,0:T(8,128)(2,1)S(1)}, u32[]{:S(2)}, u32[]{:S(2)}) collective-permute-start(bf16[1,256,128]{2,1,0:T(8,128)(2,1)S(1)} %get-tuple-element.32), channel_id=1, source_target_pairs={{0,2},{1,3},{2,0},{3,1},{4,6},{5,7},{6,4},{7,5},{8,10},{9,11},{10,... | collective-permute-start | bytes 196616 | tf_op jit(solution)/shard_map/ppermute | solution.py:369
  53.9 1.9 %lags_early.1 = (f32[256,2048]{1,0:T(8,128)S(1)}, f32[256,2048]{1,0:T(8,128)S(1)}) custom-call(bf16[2,256,128]{2,1,0:T(8,128)(2,1)S(1)} %get-tuple-element.29.refs_0_, bf16[2,256,128]{2,1,0:T(8,128)(2,1)S(1)} %collective-permute-done.15.refs_1_, bf16[2,256,128]{2,1,0:T(8,128)(2,1)S(1)} %collective-permute-done.16.refs_2_, ...), custom_call_target="tpu_custom_call" | custom-call | flops 115350000 | tf_op jit(solution)/shard_map/lags_early/pallas_call | solution.py:331
  56.5 1.4 %collective-permute-done.14.refs_3_ = bf16[1,256,128]{2,1,0:T(8,128)(2,1)S(1)} collective-permute-done((bf16[1,256,128]{2,1,0:T(8,128)(2,1)S(1)}, bf16[1,256,128]{2,1,0:T(8,128)(2,1)S(1)}, u32[]{:S(2)}, u32[]{:S(2)}) %collective-permute-start.14) | collective-permute-done | bytes 65568 | tf_op jit(solution)/shard_map/ppermute | solution.py:369
  57.9 1.7 %lags_late.1 = bf16[32,16,2048]{2,1,0:T(8,128)(2,1)} custom-call(bf16[2,256,128]{2,1,0:T(8,128)(2,1)S(1)} %get-tuple-element.31.refs_0_, bf16[2,256,128]{2,1,0:T(8,128)(2,1)S(1)} %collective-permute-done.12.refs_1_, bf16[1,256,128]{2,1,0:T(8,128)(2,1)S(1)} %collective-permute-done.13.refs_2_, bf16[1,256,128]{2,1,0:T(8,128)(2,1)S(1)} %collective-permute-done.14.refs_3_, ...), custom_call_target="tpu_custom_call" | custom-call | flops 2307000064 | tf_op jit(solution)/shard_map/lags_late/pallas_call | solution.py:345
  (42 shorter events, 7.2 us)
Async XLA Ops:
  4.1 3.2 %collective-permute-start = (bf16[2,256,128]{2,1,0:T(8,128)(2,1)S(1)}, bf16[2,256,128]{2,1,0:T(8,128)(2,1)S(1)}, u32[]{:S(2)}, u32[]{:S(2)}) collective-permute-start(bf16[2,256,128]{2,1,0:T(8,128)(2,1)S(1)} %get-tuple-element.25), channel_id=1, source_target_pairs={{0,1},{1,0},{2,3},{3,2},{4,5},{5,4},{6,7},{7,6},{8,9},{9,8},{10,11... | collective-permute-start | bytes 393224 | tf_op jit(solution)/shard_map/ppermute | solution.py:369
  4.6 6.9 %collective-permute-start.1 = (bf16[2,256,128]{2,1,0:T(8,128)(2,1)S(1)}, bf16[2,256,128]{2,1,0:T(8,128)(2,1)S(1)}, u32[]{:S(2)}, u32[]{:S(2)}) collective-permute-start(bf16[2,256,128]{2,1,0:T(8,128)(2,1)S(1)} %get-tuple-element.26), channel_id=1, source_target_pairs={{0,2},{1,3},{2,0},{3,1},{4,6},{5,7},{6,4},{7,5},{8,10},{9,11},{10,... | collective-permute-start | bytes 393224 | tf_op jit(solution)/shard_map/ppermute | solution.py:369
  7.2 6.9 %collective-permute-start.7 = (bf16[2,256,128]{2,1,0:T(8,128)(2,1)S(1)}, bf16[2,256,128]{2,1,0:T(8,128)(2,1)S(1)}, u32[]{:S(2)}, u32[]{:S(2)}) collective-permute-start(bf16[2,256,128]{2,1,0:T(8,128)(2,1)S(1)} %get-tuple-element.27), channel_id=1, source_target_pairs={{0,2},{1,3},{2,0},{3,1},{4,6},{5,7},{6,4},{7,5},{8,10},{9,11},{10,... | collective-permute-start | bytes 393224 | tf_op jit(solution)/shard_map/ppermute | solution.py:369
  7.3 10.2 %collective-permute-start.3 = (bf16[4,256,128]{2,1,0:T(8,128)(2,1)S(1)}, bf16[4,256,128]{2,1,0:T(8,128)(2,1)S(1)}, u32[]{:S(2)}, u32[]{:S(2)}) collective-permute-start(bf16[4,256,128]{2,1,0:T(8,128)(2,1)S(1)} %joined.1.refs_0_), channel_id=1, source_target_pairs={{4,0},{5,1},{6,2},{7,3},{8,4},{9,5},{10,6},{11,7},{12,8},{13,9},{1... | collective-permute-start | bytes 786440 | tf_op jit(solution)/shard_map/ppermute | solution.py:373
  11.5 2.6 %collective-permute-start.2 = (bf16[2,256,128]{2,1,0:T(8,128)(2,1)S(1)}, bf16[2,256,128]{2,1,0:T(8,128)(2,1)S(1)}, u32[]{:S(2)}, u32[]{:S(2)}) collective-permute-start(bf16[2,256,128]{2,1,0:T(8,128)(2,1)S(1)} %collective-permute-done.1.straight), channel_id=1, source_target_pairs={{0,1},{1,0},{2,3},{3,2},{4,5},{5,4},{6,7},{7,6},{8,9},{9,8},{10,11... | collective-permute-start | bytes 393224 | tf_op jit(solution)/shard_map/ppermute | solution.py:369
  14.1 8.2 %collective-permute-start.5 = (bf16[2,256,128]{2,1,0:T(8,128)(2,1)S(1)}, bf16[2,256,128]{2,1,0:T(8,128)(2,1)S(1)}, u32[]{:S(2)}, u32[]{:S(2)}) collective-permute-start(bf16[2,256,128]{2,1,0:T(8,128)(2,1)S(1)} %far_joined.2.refs_1_), channel_id=1, source_target_pairs={{4,0},{5,1},{6,2},{7,3},{8,4},{9,5},{10,6},{11,7},{12,8},{13,9},{1... | collective-permute-start | bytes 393224 | tf_op jit(solution)/shard_map/ppermute | solution.py:373
  15.5 9.6 %collective-permute-start.9 = (bf16[2,256,128]{2,1,0:T(8,128)(2,1)S(1)}, bf16[2,256,128]{2,1,0:T(8,128)(2,1)S(1)}, u32[]{:S(2)}, u32[]{:S(2)}) collective-permute-start(bf16[2,256,128]{2,1,0:T(8,128)(2,1)S(1)} %far_joined.3.refs_1_), channel_id=1, source_target_pairs={{4,0},{5,1},{6,2},{7,3},{8,4},{9,5},{10,6},{11,7},{12,8},{13,9},{1... | collective-permute-start | bytes 393224 | tf_op jit(solution)/shard_map/ppermute | solution.py:373
  17.6 16.0 %collective-permute-start.4 = (bf16[4,256,128]{2,1,0:T(8,128)(2,1)S(1)}, bf16[4,256,128]{2,1,0:T(8,128)(2,1)S(1)}, u32[]{:S(2)}, u32[]{:S(2)}) collective-permute-start(bf16[4,256,128]{2,1,0:T(8,128)(2,1)S(1)} %collective-permute-done.3.refs_2_), channel_id=1, source_target_pairs={{4,0},{5,1},{6,2},{7,3},{8,4},{9,5},{10,6},{11,7},{20,16},{21,17},... | collective-permute-start | bytes 786440 | tf_op jit(solution)/shard_map/ppermute | solution.py:373
  25.1 8.4 %collective-permute-start.10 = (bf16[2,256,128]{2,1,0:T(8,128)(2,1)S(1)}, bf16[2,256,128]{2,1,0:T(8,128)(2,1)S(1)}, u32[]{:S(2)}, u32[]{:S(2)}) collective-permute-start(bf16[2,256,128]{2,1,0:T(8,128)(2,1)S(1)} %collective-permute-done.9.refs_3_), channel_id=1, source_target_pairs={{4,0},{5,1},{6,2},{7,3},{8,4},{9,5},{10,6},{11,7},{20,16},{21,17},... | collective-permute-start | bytes 393224 | tf_op jit(solution)/shard_map/ppermute | solution.py:373
  26.4 10.2 %collective-permute-start.6 = (bf16[2,256,128]{2,1,0:T(8,128)(2,1)S(1)}, bf16[2,256,128]{2,1,0:T(8,128)(2,1)S(1)}, u32[]{:S(2)}, u32[]{:S(2)}) collective-permute-start(bf16[2,256,128]{2,1,0:T(8,128)(2,1)S(1)} %collective-permute-done.5.refs_3_), channel_id=1, source_target_pairs={{4,0},{5,1},{6,2},{7,3},{8,4},{9,5},{10,6},{11,7},{20,16},{21,17},... | collective-permute-start | bytes 393224 | tf_op jit(solution)/shard_map/ppermute | solution.py:373
  33.6 11.1 %collective-permute-start.21 = (bf16[4,256,128]{2,1,0:T(8,128)(2,1)S(1)}, bf16[4,256,128]{2,1,0:T(8,128)(2,1)S(1)}, u32[]{:S(2)}, u32[]{:S(2)}) collective-permute-start(bf16[4,256,128]{2,1,0:T(8,128)(2,1)S(1)} %team_joined.2.refs_4_.refs_2_), channel_id=1, source_target_pairs={{4,0},{5,1},{6,2},{7,3},{20,16},{21,17},{22,18},{23,19}} | collective-permute-start | bytes 786440 | tf_op jit(solution)/shard_map/ppermute | solution.py:373
  36.6 12.2 %collective-permute-start.11 = (bf16[4,256,128]{2,1,0:T(8,128)(2,1)S(1)}, bf16[4,256,128]{2,1,0:T(8,128)(2,1)S(1)}, u32[]{:S(2)}, u32[]{:S(2)}) collective-permute-start(bf16[4,256,128]{2,1,0:T(8,128)(2,1)S(1)} %team_joined.3.refs_2_.refs_4_), channel_id=1, source_target_pairs={{4,0},{5,1},{6,2},{7,3},{20,16},{21,17},{22,18},{23,19}} | collective-permute-start | bytes 786440 | tf_op jit(solution)/shard_map/ppermute | solution.py:373
  39.6 8.6 %collective-permute-start.19 = (bf16[2,256,128]{2,1,0:T(8,128)(2,1)S(1)}, bf16[2,256,128]{2,1,0:T(8,128)(2,1)S(1)}, u32[]{:S(2)}, u32[]{:S(2)}) collective-permute-start(bf16[2,256,128]{2,1,0:T(8,128)(2,1)S(1)} %get-tuple-element.36), channel_id=1, source_target_pairs={{0,2},{1,3},{2,0},{3,1},{4,6},{5,7},{6,4},{7,5},{8,10},{9,11},{10,... | collective-permute-start | bytes 393224 | tf_op jit(solution)/shard_map/ppermute | solution.py:369
  41.5 7.3 %collective-permute-start.16 = (bf16[2,256,128]{2,1,0:T(8,128)(2,1)S(1)}, bf16[2,256,128]{2,1,0:T(8,128)(2,1)S(1)}, u32[]{:S(2)}, u32[]{:S(2)}) collective-permute-start(bf16[2,256,128]{2,1,0:T(8,128)(2,1)S(1)} %get-tuple-element.34), channel_id=1, source_target_pairs={{0,2},{1,3},{2,0},{3,1},{4,6},{5,7},{6,4},{7,5},{8,10},{9,11},{10,... | collective-permute-start | bytes 393224 | tf_op jit(solution)/shard_map/ppermute | solution.py:369
  46.4 5.0 %collective-permute-start.23 = (bf16[2,256,128]{2,1,0:T(8,128)(2,1)S(1)}, bf16[2,256,128]{2,1,0:T(8,128)(2,1)S(1)}, u32[]{:S(2)}, u32[]{:S(2)}) collective-permute-start(bf16[2,256,128]{2,1,0:T(8,128)(2,1)S(1)} %get-tuple-element.39), channel_id=1, source_target_pairs={{0,2},{1,3},{2,0},{3,1},{4,6},{5,7},{6,4},{7,5},{8,10},{9,11},{10,... | collective-permute-start | bytes 393224 | tf_op jit(solution)/shard_map/ppermute | solution.py:369
  48.2 3.2 %collective-permute-start.18 = (bf16[2,256,128]{2,1,0:T(8,128)(2,1)S(1)}, bf16[2,256,128]{2,1,0:T(8,128)(2,1)S(1)}, u32[]{:S(2)}, u32[]{:S(2)}) collective-permute-start(bf16[2,256,128]{2,1,0:T(8,128)(2,1)S(1)} %get-tuple-element.35.refs_4_), channel_id=1, source_target_pairs={{0,1},{1,0},{2,3},{3,2},{4,5},{5,4},{6,7},{7,6},{8,9},{9,8},{10,11... | collective-permute-start | bytes 393224 | tf_op jit(solution)/shard_map/ppermute | solution.py:369
  48.2 3.7 %collective-permute-start.15 = (bf16[2,256,128]{2,1,0:T(8,128)(2,1)S(1)}, bf16[2,256,128]{2,1,0:T(8,128)(2,1)S(1)}, u32[]{:S(2)}, u32[]{:S(2)}) collective-permute-start(bf16[2,256,128]{2,1,0:T(8,128)(2,1)S(1)} %get-tuple-element.29.refs_0_), channel_id=1, source_target_pairs={{0,1},{1,0},{2,3},{3,2},{4,5},{5,4},{6,7},{7,6},{8,9},{9,8},{10,11... | collective-permute-start | bytes 393224 | tf_op jit(solution)/shard_map/ppermute | solution.py:369
  48.8 3.3 %collective-permute-start.20 = (bf16[2,256,128]{2,1,0:T(8,128)(2,1)S(1)}, bf16[2,256,128]{2,1,0:T(8,128)(2,1)S(1)}, u32[]{:S(2)}, u32[]{:S(2)}) collective-permute-start(bf16[2,256,128]{2,1,0:T(8,128)(2,1)S(1)} %collective-permute-done.19.refs_6_), channel_id=1, source_target_pairs={{0,1},{1,0},{2,3},{3,2},{4,5},{5,4},{6,7},{7,6},{8,9},{9,8},{10,11... | collective-permute-start | bytes 393224 | tf_op jit(solution)/shard_map/ppermute | solution.py:369
  48.8 5.0 %collective-permute-start.17 = (bf16[2,256,128]{2,1,0:T(8,128)(2,1)S(1)}, bf16[2,256,128]{2,1,0:T(8,128)(2,1)S(1)}, u32[]{:S(2)}, u32[]{:S(2)}) collective-permute-start(bf16[2,256,128]{2,1,0:T(8,128)(2,1)S(1)} %collective-permute-done.16.refs_2_), channel_id=1, source_target_pairs={{0,1},{1,0},{2,3},{3,2},{4,5},{5,4},{6,7},{7,6},{8,9},{9,8},{10,11... | collective-permute-start | bytes 393224 | tf_op jit(solution)/shard_map/ppermute | solution.py:369
  51.4 2.5 %collective-permute-start.22 = (bf16[2,256,128]{2,1,0:T(8,128)(2,1)S(1)}, bf16[2,256,128]{2,1,0:T(8,128)(2,1)S(1)}, u32[]{:S(2)}, u32[]{:S(2)}) collective-permute-start(bf16[2,256,128]{2,1,0:T(8,128)(2,1)S(1)} %get-tuple-element.38.refs_8_), channel_id=1, source_target_pairs={{0,1},{1,0},{2,3},{3,2},{4,5},{5,4},{6,7},{7,6},{8,9},{9,8},{10,11... | collective-permute-start | bytes 393224 | tf_op jit(solution)/shard_map/ppermute | solution.py:369
  51.4 2.5 %collective-permute-start.24 = (bf16[2,256,128]{2,1,0:T(8,128)(2,1)S(1)}, bf16[2,256,128]{2,1,0:T(8,128)(2,1)S(1)}, u32[]{:S(2)}, u32[]{:S(2)}) collective-permute-start(bf16[2,256,128]{2,1,0:T(8,128)(2,1)S(1)} %collective-permute-done.23.refs_10_), channel_id=1, source_target_pairs={{0,1},{1,0},{2,3},{3,2},{4,5},{5,4},{6,7},{7,6},{8,9},{9,8},{10,11... | collective-permute-start | bytes 393224 | tf_op jit(solution)/shard_map/ppermute | solution.py:369
  51.9 5.9 %collective-permute-start.12 = (bf16[2,256,128]{2,1,0:T(8,128)(2,1)S(1)}, bf16[2,256,128]{2,1,0:T(8,128)(2,1)S(1)}, u32[]{:S(2)}, u32[]{:S(2)}) collective-permute-start(bf16[2,256,128]{2,1,0:T(8,128)(2,1)S(1)} %get-tuple-element.31.refs_0_), channel_id=1, source_target_pairs={{0,1},{1,0},{2,3},{3,2},{4,5},{5,4},{6,7},{7,6},{8,9},{9,8},{10,11... | collective-permute-start | bytes 393224 | tf_op jit(solution)/shard_map/ppermute | solution.py:369
  52.0 4.5 %collective-permute-start.13 = (bf16[1,256,128]{2,1,0:T(8,128)(2,1)S(1)}, bf16[1,256,128]{2,1,0:T(8,128)(2,1)S(1)}, u32[]{:S(2)}, u32[]{:S(2)}) collective-permute-start(bf16[1,256,128]{2,1,0:T(8,128)(2,1)S(1)} %get-tuple-element.32), channel_id=1, source_target_pairs={{0,2},{1,3},{2,0},{3,1},{4,6},{5,7},{6,4},{7,5},{8,10},{9,11},{10,... | collective-permute-start | bytes 196616 | tf_op jit(solution)/shard_map/ppermute | solution.py:369
  53.8 4.1 %collective-permute-start.14 = (bf16[1,256,128]{2,1,0:T(8,128)(2,1)S(1)}, bf16[1,256,128]{2,1,0:T(8,128)(2,1)S(1)}, u32[]{:S(2)}, u32[]{:S(2)}) collective-permute-start(bf16[1,256,128]{2,1,0:T(8,128)(2,1)S(1)} %get-tuple-element.33), channel_id=1, source_target_pairs={{0,3},{1,2},{2,1},{3,0},{4,7},{5,6},{6,5},{7,4},{8,11},{9,10},{10,... | collective-permute-start | bytes 196616 | tf_op jit(solution)/shard_map/ppermute | solution.py:369
  (3 other events, 41.4 us)

commit v7 on v6

--- a/solution.py
+++ b/solution.py
@@ -341,7 +341,7 @@
 
 def lags_late(high, table, lower, upper, count, number):
     vmem = pl.BlockSpec(memory_space=pltpu.VMEM)
-    tile = 512
+    tile = 256
     return pl.pallas_call(
         functools.partial(late_kernel, count, tile),
         in_specs=[vmem] * (TEAM + 3),

time: 59.8 us -> 59.9 us (level)
  no operation moved by 1% of the time
where the time goes in v7:
time: 59.9 us; the launch traced here: 59.6 us
  waiting for transfers between devices  23.8 us (40%)
  starting transfers between devices  20.9 us (35%)
  Pallas kernels  14.7 us (25%)
    ppermute x8, waiting for transfers between devices, down(): return lax.ppermute(value, 'chan', pairs)  15.8 us
    ppermute x17, starting transfers between devices, swapped(): return lax.ppermute(value, 'chan', [(i, i ^ by) for i in range(ring)])  10.6 us
    ppermute x8, starting transfers between devices, down(): return lax.ppermute(value, 'chan', pairs)  10.3 us
    ppermute x17, waiting for transfers between devices, swapped(): return lax.ppermute(value, 'chan', [(i, i ^ by) for i in range(ring)])  7.97 us
    pallas_call x4, Pallas kernels, cross(): pl.pallas_call(functools.partial(cross_kernel, windows, count, halves, si...  6.9 us
    pallas_call x1, Pallas kernels, spectra(): pl.pallas_call(functools.partial(spectra_kernel, windows), in_specs=[pl.B...  4.08 us
    pallas_call x1, Pallas kernels, lags_early(): pl.pallas_call(functools.partial(early_kernel, 512), in_specs=[vmem] * (l...  1.91 us
    pallas_call x1, Pallas kernels, lags_late(): pl.pallas_call(functools.partial(late_kernel, count, tile), in_specs=[vme...  1.7 us
  transfers between devices with their start and end apart: 25, of which 10 were waited for; matrix products, arithmetic and copies ran while one was open for 0% of the time, Pallas kernels for 15%

profile of v7, /device:TPU:0, one launch (start us, length us, event | category | flops | bytes accessed | tf_op | source)
XLA Modules:
  0.0 59.6 jit_solution(9873529540398870450)
XLA Ops:
  0.0 4.1 %spectra.1 = (bf16[2,256,128]{2,1,0:T(8,128)(2,1)S(1)}, bf16[2,256,128]{2,1,0:T(8,128)(2,1)S(1)}, bf16[2,256,128]{2,1,0:T(8,128)(2,1)S(1)}, bf16[2,256,128]{2,1,0:T(8,128)(2,1)S(1)}) custom-call(bf16[256,3000]{1,0:T(8,128)(2,1)} %bitcast.2, bf16[2,750,512]{2,1,0:T(8,128)(2,1)} %constant.4.clone.table_hbm, s32[1,32]{1,0:T(1,128)} %bitcast.3), custom_call_target="tpu_custom_call" | custom-call | flops 3460499968 | tf_op jit(solution)/shard_map/spectra/pallas_call | solution.py:118
  4.6 2.6 %collective-permute-start.1 = (bf16[2,256,128]{2,1,0:T(8,128)(2,1)S(1)}, bf16[2,256,128]{2,1,0:T(8,128)(2,1)S(1)}, u32[]{:S(2)}, u32[]{:S(2)}) collective-permute-start(bf16[2,256,128]{2,1,0:T(8,128)(2,1)S(1)} %get-tuple-element.26), channel_id=1, source_target_pairs={{0,2},{1,3},{2,0},{3,1},{4,6},{5,7},{6,4},{7,5},{8,10},{9,11},{10,... | collective-permute-start | bytes 393224 | tf_op jit(solution)/shard_map/ppermute | solution.py:369
  7.3 1.3 %collective-permute-start.3 = (bf16[4,256,128]{2,1,0:T(8,128)(2,1)S(1)}, bf16[4,256,128]{2,1,0:T(8,128)(2,1)S(1)}, u32[]{:S(2)}, u32[]{:S(2)}) collective-permute-start(bf16[4,256,128]{2,1,0:T(8,128)(2,1)S(1)} %joined.1.refs_0_), channel_id=1, source_target_pairs={{4,0},{5,1},{6,2},{7,3},{8,4},{9,5},{10,6},{11,7},{12,8},{13,9},{1... | collective-permute-start | bytes 786440 | tf_op jit(solution)/shard_map/ppermute | solution.py:373
  8.6 2.9 %collective-permute-done.1.straight = bf16[2,256,128]{2,1,0:T(8,128)(2,1)S(1)} collective-permute-done((bf16[2,256,128]{2,1,0:T(8,128)(2,1)S(1)}, bf16[2,256,128]{2,1,0:T(8,128)(2,1)S(1)}, u32[]{:S(2)}, u32[]{:S(2)}) %collective-permute-start.1) | collective-permute-done | bytes 131104 | tf_op jit(solution)/shard_map/ppermute | solution.py:369
  11.5 2.5 %collective-permute-done.7.straight = bf16[2,256,128]{2,1,0:T(8,128)(2,1)S(1)} collective-permute-done((bf16[2,256,128]{2,1,0:T(8,128)(2,1)S(1)}, bf16[2,256,128]{2,1,0:T(8,128)(2,1)S(1)}, u32[]{:S(2)}, u32[]{:S(2)}) %collective-permute-start.7) | collective-permute-done | bytes 131104 | tf_op jit(solution)/shard_map/ppermute | solution.py:369
  14.1 1.3 %collective-permute-start.5 = (bf16[2,256,128]{2,1,0:T(8,128)(2,1)S(1)}, bf16[2,256,128]{2,1,0:T(8,128)(2,1)S(1)}, u32[]{:S(2)}, u32[]{:S(2)}) collective-permute-start(bf16[2,256,128]{2,1,0:T(8,128)(2,1)S(1)} %far_joined.2.refs_1_), channel_id=1, source_target_pairs={{4,0},{5,1},{6,2},{7,3},{8,4},{9,5},{10,6},{11,7},{12,8},{13,9},{1... | collective-permute-start | bytes 393224 | tf_op jit(solution)/shard_map/ppermute | solution.py:373
  15.5 1.3 %collective-permute-start.9 = (bf16[2,256,128]{2,1,0:T(8,128)(2,1)S(1)}, bf16[2,256,128]{2,1,0:T(8,128)(2,1)S(1)}, u32[]{:S(2)}, u32[]{:S(2)}) collective-permute-start(bf16[2,256,128]{2,1,0:T(8,128)(2,1)S(1)} %far_joined.3.refs_1_), channel_id=1, source_target_pairs={{4,0},{5,1},{6,2},{7,3},{8,4},{9,5},{10,6},{11,7},{12,8},{13,9},{1... | collective-permute-start | bytes 393224 | tf_op jit(solution)/shard_map/ppermute | solution.py:373
  18.9 3.4 %collective-permute-done.5.refs_3_ = bf16[2,256,128]{2,1,0:T(8,128)(2,1)S(1)} collective-permute-done((bf16[2,256,128]{2,1,0:T(8,128)(2,1)S(1)}, bf16[2,256,128]{2,1,0:T(8,128)(2,1)S(1)}, u32[]{:S(2)}, u32[]{:S(2)}) %collective-permute-start.5) | collective-permute-done | bytes 131104 | tf_op jit(solution)/shard_map/ppermute | solution.py:373
  22.3 2.8 %collective-permute-done.9.refs_3_ = bf16[2,256,128]{2,1,0:T(8,128)(2,1)S(1)} collective-permute-done((bf16[2,256,128]{2,1,0:T(8,128)(2,1)S(1)}, bf16[2,256,128]{2,1,0:T(8,128)(2,1)S(1)}, u32[]{:S(2)}, u32[]{:S(2)}) %collective-permute-start.9) | collective-permute-done | bytes 131104 | tf_op jit(solution)/shard_map/ppermute | solution.py:373
  26.4 1.3 %collective-permute-start.6 = (bf16[2,256,128]{2,1,0:T(8,128)(2,1)S(1)}, bf16[2,256,128]{2,1,0:T(8,128)(2,1)S(1)}, u32[]{:S(2)}, u32[]{:S(2)}) collective-permute-start(bf16[2,256,128]{2,1,0:T(8,128)(2,1)S(1)} %collective-permute-done.5.refs_3_), channel_id=1, source_target_pairs={{4,0},{5,1},{6,2},{7,3},{8,4},{9,5},{10,6},{11,7},{20,16},{21,17},... | collective-permute-start | bytes 393224 | tf_op jit(solution)/shard_map/ppermute | solution.py:373
  27.7 5.8 %collective-permute-done.10.far = bf16[2,256,128]{2,1,0:T(8,128)(2,1)S(1)} collective-permute-done((bf16[2,256,128]{2,1,0:T(8,128)(2,1)S(1)}, bf16[2,256,128]{2,1,0:T(8,128)(2,1)S(1)}, u32[]{:S(2)}, u32[]{:S(2)}) %collective-permute-start.10) | collective-permute-done | bytes 131104 | tf_op jit(solution)/shard_map/ppermute | solution.py:373
  33.6 1.3 %collective-permute-start.21 = (bf16[4,256,128]{2,1,0:T(8,128)(2,1)S(1)}, bf16[4,256,128]{2,1,0:T(8,128)(2,1)S(1)}, u32[]{:S(2)}, u32[]{:S(2)}) collective-permute-start(bf16[4,256,128]{2,1,0:T(8,128)(2,1)S(1)} %team_joined.2.refs_4_.refs_2_), channel_id=1, source_target_pairs={{4,0},{5,1},{6,2},{7,3},{20,16},{21,17},{22,18},{23,19}} | collective-permute-start | bytes 786440 | tf_op jit(solution)/shard_map/ppermute | solution.py:373
  34.9 1.7 %cross.4 = (bf16[2,256,128]{2,1,0:T(8,128)(2,1)S(1)}, bf16[2,256,128]{2,1,0:T(8,128)(2,1)S(1)}) custom-call(s32[16]{0:T(128)S(1)} %copy-done.1, bf16[4,256,128]{2,1,0:T(8,128)(2,1)S(1)} %joined.1.refs_0_, bf16[2,256,128]{2,1,0:T(8,128)(2,1)S(1)} %far_joined.3.refs_1_, bf16[4,256,128]{2,1,0:T(8,128)(2,1)S(1)} %collective-permute-done.3.refs_2_, ...), custom_call_target="tpu_custom_call" | custom-call | flops 576750016 | tf_op jit(solution)/shard_map/cross/pallas_call | solution.py:276
  36.6 1.3 %collective-permute-start.11 = (bf16[4,256,128]{2,1,0:T(8,128)(2,1)S(1)}, bf16[4,256,128]{2,1,0:T(8,128)(2,1)S(1)}, u32[]{:S(2)}, u32[]{:S(2)}) collective-permute-start(bf16[4,256,128]{2,1,0:T(8,128)(2,1)S(1)} %team_joined.3.refs_2_.refs_4_), channel_id=1, source_target_pairs={{4,0},{5,1},{6,2},{7,3},{20,16},{21,17},{22,18},{23,19}} | collective-permute-start | bytes 786440 | tf_op jit(solution)/shard_map/ppermute | solution.py:373
  37.9 1.7 %cross.6 = (bf16[2,256,128]{2,1,0:T(8,128)(2,1)S(1)}, bf16[2,256,128]{2,1,0:T(8,128)(2,1)S(1)}) custom-call(s32[16]{0:T(128)S(1)} %copy-done.1, bf16[4,256,128]{2,1,0:T(8,128)(2,1)S(1)} %joined.1.refs_0_, bf16[2,256,128]{2,1,0:T(8,128)(2,1)S(1)} %far_joined.2.refs_1_, bf16[4,256,128]{2,1,0:T(8,128)(2,1)S(1)} %collective-permute-done.3.refs_2_, ...), custom_call_target="tpu_custom_call" | custom-call | flops 576750016 | tf_op jit(solution)/shard_map/cross/pallas_call | solution.py:276
  39.7 1.8 %collective-permute-start.19 = (bf16[2,256,128]{2,1,0:T(8,128)(2,1)S(1)}, bf16[2,256,128]{2,1,0:T(8,128)(2,1)S(1)}, u32[]{:S(2)}, u32[]{:S(2)}) collective-permute-start(bf16[2,256,128]{2,1,0:T(8,128)(2,1)S(1)} %get-tuple-element.36), channel_id=1, source_target_pairs={{0,2},{1,3},{2,0},{3,1},{4,6},{5,7},{6,4},{7,5},{8,10},{9,11},{10,... | collective-permute-start | bytes 393224 | tf_op jit(solution)/shard_map/ppermute | solution.py:369
  41.7 2.9 %collective-permute-done.21.refs_3_ = bf16[4,256,128]{2,1,0:T(8,128)(2,1)S(1)} collective-permute-done((bf16[4,256,128]{2,1,0:T(8,128)(2,1)S(1)}, bf16[4,256,128]{2,1,0:T(8,128)(2,1)S(1)}, u32[]{:S(2)}, u32[]{:S(2)}) %collective-permute-start.21) | collective-permute-done | bytes 262176 | tf_op jit(solution)/shard_map/ppermute | solution.py:373
  44.7 1.7 %cross.7 = (bf16[2,256,128]{2,1,0:T(8,128)(2,1)S(1)}, bf16[2,256,128]{2,1,0:T(8,128)(2,1)S(1)}) custom-call(s32[16]{0:T(128)S(1)} %copy-done.1, bf16[4,256,128]{2,1,0:T(8,128)(2,1)S(1)} %joined.1.refs_0_, bf16[2,256,128]{2,1,0:T(8,128)(2,1)S(1)} %far_joined.3.refs_1_, bf16[4,256,128]{2,1,0:T(8,128)(2,1)S(1)} %team_joined.2.refs_4_.refs_2_, ...), custom_call_target="tpu_custom_call" | custom-call | flops 576750016 | tf_op jit(solution)/shard_map/cross/pallas_call | solution.py:276
  46.4 1.8 %collective-permute-start.23 = (bf16[2,256,128]{2,1,0:T(8,128)(2,1)S(1)}, bf16[2,256,128]{2,1,0:T(8,128)(2,1)S(1)}, u32[]{:S(2)}, u32[]{:S(2)}) collective-permute-start(bf16[2,256,128]{2,1,0:T(8,128)(2,1)S(1)} %get-tuple-element.39), channel_id=1, source_target_pairs={{0,2},{1,3},{2,0},{3,1},{4,6},{5,7},{6,4},{7,5},{8,10},{9,11},{10,... | collective-permute-start | bytes 393224 | tf_op jit(solution)/shard_map/ppermute | solution.py:369
  49.3 1.7 %cross.5 = (bf16[2,256,128]{2,1,0:T(8,128)(2,1)S(1)}, bf16[1,256,128]{2,1,0:T(8,128)(2,1)S(1)}, bf16[1,256,128]{2,1,0:T(8,128)(2,1)S(1)}) custom-call(s32[16]{0:T(128)S(1)} %copy-done.1, bf16[4,256,128]{2,1,0:T(8,128)(2,1)S(1)} %joined.1.refs_0_, bf16[2,256,128]{2,1,0:T(8,128)(2,1)S(1)} %far_joined.2.refs_1_, ...), custom_call_target="tpu_custom_call" | custom-call | flops 576750016 | tf_op jit(solution)/shard_map/cross/pallas_call | solution.py:276
  52.0 1.8 %collective-permute-start.13 = (bf16[1,256,128]{2,1,0:T(8,128)(2,1)S(1)}, bf16[1,256,128]{2,1,0:T(8,128)(2,1)S(1)}, u32[]{:S(2)}, u32[]{:S(2)}) collective-permute-start(bf16[1,256,128]{2,1,0:T(8,128)(2,1)S(1)} %get-tuple-element.32), channel_id=1, source_target_pairs={{0,2},{1,3},{2,0},{3,1},{4,6},{5,7},{6,4},{7,5},{8,10},{9,11},{10,... | collective-permute-start | bytes 196616 | tf_op jit(solution)/shard_map/ppermute | solution.py:369
  53.9 1.9 %lags_early.1 = (f32[256,2048]{1,0:T(8,128)S(1)}, f32[256,2048]{1,0:T(8,128)S(1)}) custom-call(bf16[2,256,128]{2,1,0:T(8,128)(2,1)S(1)} %get-tuple-element.29.refs_0_, bf16[2,256,128]{2,1,0:T(8,128)(2,1)S(1)} %collective-permute-done.15.refs_1_, bf16[2,256,128]{2,1,0:T(8,128)(2,1)S(1)} %collective-permute-done.16.refs_2_, ...), custom_call_target="tpu_custom_call" | custom-call | flops 115350000 | tf_op jit(solution)/shard_map/lags_early/pallas_call | solution.py:331
  56.5 1.4 %collective-permute-done.14.refs_3_ = bf16[1,256,128]{2,1,0:T(8,128)(2,1)S(1)} collective-permute-done((bf16[1,256,128]{2,1,0:T(8,128)(2,1)S(1)}, bf16[1,256,128]{2,1,0:T(8,128)(2,1)S(1)}, u32[]{:S(2)}, u32[]{:S(2)}) %collective-permute-start.14) | collective-permute-done | bytes 65568 | tf_op jit(solution)/shard_map/ppermute | solution.py:369
  57.9 1.7 %lags_late.1 = bf16[32,16,2048]{2,1,0:T(8,128)(2,1)} custom-call(bf16[2,256,128]{2,1,0:T(8,128)(2,1)S(1)} %get-tuple-element.31.refs_0_, bf16[2,256,128]{2,1,0:T(8,128)(2,1)S(1)} %collective-permute-done.12.refs_1_, bf16[1,256,128]{2,1,0:T(8,128)(2,1)S(1)} %collective-permute-done.13.refs_2_, bf16[1,256,128]{2,1,0:T(8,128)(2,1)S(1)} %collective-permute-done.14.refs_3_, ...), custom_call_target="tpu_custom_call" | custom-call | flops 2307000064 | tf_op jit(solution)/shard_map/lags_late/pallas_call | solution.py:345
  (42 shorter events, 7.2 us)
Async XLA Ops:
  4.1 3.2 %collective-permute-start = (bf16[2,256,128]{2,1,0:T(8,128)(2,1)S(1)}, bf16[2,256,128]{2,1,0:T(8,128)(2,1)S(1)}, u32[]{:S(2)}, u32[]{:S(2)}) collective-permute-start(bf16[2,256,128]{2,1,0:T(8,128)(2,1)S(1)} %get-tuple-element.25), channel_id=1, source_target_pairs={{0,1},{1,0},{2,3},{3,2},{4,5},{5,4},{6,7},{7,6},{8,9},{9,8},{10,11... | collective-permute-start | bytes 393224 | tf_op jit(solution)/shard_map/ppermute | solution.py:369
  4.6 6.9 %collective-permute-start.1 = (bf16[2,256,128]{2,1,0:T(8,128)(2,1)S(1)}, bf16[2,256,128]{2,1,0:T(8,128)(2,1)S(1)}, u32[]{:S(2)}, u32[]{:S(2)}) collective-permute-start(bf16[2,256,128]{2,1,0:T(8,128)(2,1)S(1)} %get-tuple-element.26), channel_id=1, source_target_pairs={{0,2},{1,3},{2,0},{3,1},{4,6},{5,7},{6,4},{7,5},{8,10},{9,11},{10,... | collective-permute-start | bytes 393224 | tf_op jit(solution)/shard_map/ppermute | solution.py:369
  7.2 6.9 %collective-permute-start.7 = (bf16[2,256,128]{2,1,0:T(8,128)(2,1)S(1)}, bf16[2,256,128]{2,1,0:T(8,128)(2,1)S(1)}, u32[]{:S(2)}, u32[]{:S(2)}) collective-permute-start(bf16[2,256,128]{2,1,0:T(8,128)(2,1)S(1)} %get-tuple-element.27), channel_id=1, source_target_pairs={{0,2},{1,3},{2,0},{3,1},{4,6},{5,7},{6,4},{7,5},{8,10},{9,11},{10,... | collective-permute-start | bytes 393224 | tf_op jit(solution)/shard_map/ppermute | solution.py:369
  7.3 10.2 %collective-permute-start.3 = (bf16[4,256,128]{2,1,0:T(8,128)(2,1)S(1)}, bf16[4,256,128]{2,1,0:T(8,128)(2,1)S(1)}, u32[]{:S(2)}, u32[]{:S(2)}) collective-permute-start(bf16[4,256,128]{2,1,0:T(8,128)(2,1)S(1)} %joined.1.refs_0_), channel_id=1, source_target_pairs={{4,0},{5,1},{6,2},{7,3},{8,4},{9,5},{10,6},{11,7},{12,8},{13,9},{1... | collective-permute-start | bytes 786440 | tf_op jit(solution)/shard_map/ppermute | solution.py:373
  11.5 2.6 %collective-permute-start.2 = (bf16[2,256,128]{2,1,0:T(8,128)(2,1)S(1)}, bf16[2,256,128]{2,1,0:T(8,128)(2,1)S(1)}, u32[]{:S(2)}, u32[]{:S(2)}) collective-permute-start(bf16[2,256,128]{2,1,0:T(8,128)(2,1)S(1)} %collective-permute-done.1.straight), channel_id=1, source_target_pairs={{0,1},{1,0},{2,3},{3,2},{4,5},{5,4},{6,7},{7,6},{8,9},{9,8},{10,11... | collective-permute-start | bytes 393224 | tf_op jit(solution)/shard_map/ppermute | solution.py:369
  14.1 8.2 %collective-permute-start.5 = (bf16[2,256,128]{2,1,0:T(8,128)(2,1)S(1)}, bf16[2,256,128]{2,1,0:T(8,128)(2,1)S(1)}, u32[]{:S(2)}, u32[]{:S(2)}) collective-permute-start(bf16[2,256,128]{2,1,0:T(8,128)(2,1)S(1)} %far_joined.2.refs_1_), channel_id=1, source_target_pairs={{4,0},{5,1},{6,2},{7,3},{8,4},{9,5},{10,6},{11,7},{12,8},{13,9},{1... | collective-permute-start | bytes 393224 | tf_op jit(solution)/shard_map/ppermute | solution.py:373
  15.5 9.6 %collective-permute-start.9 = (bf16[2,256,128]{2,1,0:T(8,128)(2,1)S(1)}, bf16[2,256,128]{2,1,0:T(8,128)(2,1)S(1)}, u32[]{:S(2)}, u32[]{:S(2)}) collective-permute-start(bf16[2,256,128]{2,1,0:T(8,128)(2,1)S(1)} %far_joined.3.refs_1_), channel_id=1, source_target_pairs={{4,0},{5,1},{6,2},{7,3},{8,4},{9,5},{10,6},{11,7},{12,8},{13,9},{1... | collective-permute-start | bytes 393224 | tf_op jit(solution)/shard_map/ppermute | solution.py:373
  17.6 16.0 %collective-permute-start.4 = (bf16[4,256,128]{2,1,0:T(8,128)(2,1)S(1)}, bf16[4,256,128]{2,1,0:T(8,128)(2,1)S(1)}, u32[]{:S(2)}, u32[]{:S(2)}) collective-permute-start(bf16[4,256,128]{2,1,0:T(8,128)(2,1)S(1)} %collective-permute-done.3.refs_2_), channel_id=1, source_target_pairs={{4,0},{5,1},{6,2},{7,3},{8,4},{9,5},{10,6},{11,7},{20,16},{21,17},... | collective-permute-start | bytes 786440 | tf_op jit(solution)/shard_map/ppermute | solution.py:373
  25.1 8.4 %collective-permute-start.10 = (bf16[2,256,128]{2,1,0:T(8,128)(2,1)S(1)}, bf16[2,256,128]{2,1,0:T(8,128)(2,1)S(1)}, u32[]{:S(2)}, u32[]{:S(2)}) collective-permute-start(bf16[2,256,128]{2,1,0:T(8,128)(2,1)S(1)} %collective-permute-done.9.refs_3_), channel_id=1, source_target_pairs={{4,0},{5,1},{6,2},{7,3},{8,4},{9,5},{10,6},{11,7},{20,16},{21,17},... | collective-permute-start | bytes 393224 | tf_op jit(solution)/shard_map/ppermute | solution.py:373
  26.4 10.2 %collective-permute-start.6 = (bf16[2,256,128]{2,1,0:T(8,128)(2,1)S(1)}, bf16[2,256,128]{2,1,0:T(8,128)(2,1)S(1)}, u32[]{:S(2)}, u32[]{:S(2)}) collective-permute-start(bf16[2,256,128]{2,1,0:T(8,128)(2,1)S(1)} %collective-permute-done.5.refs_3_), channel_id=1, source_target_pairs={{4,0},{5,1},{6,2},{7,3},{8,4},{9,5},{10,6},{11,7},{20,16},{21,17},... | collective-permute-start | bytes 393224 | tf_op jit(solution)/shard_map/ppermute | solution.py:373
  33.6 11.1 %collective-permute-start.21 = (bf16[4,256,128]{2,1,0:T(8,128)(2,1)S(1)}, bf16[4,256,128]{2,1,0:T(8,128)(2,1)S(1)}, u32[]{:S(2)}, u32[]{:S(2)}) collective-permute-start(bf16[4,256,128]{2,1,0:T(8,128)(2,1)S(1)} %team_joined.2.refs_4_.refs_2_), channel_id=1, source_target_pairs={{4,0},{5,1},{6,2},{7,3},{20,16},{21,17},{22,18},{23,19}} | collective-permute-start | bytes 786440 | tf_op jit(solution)/shard_map/ppermute | solution.py:373
  36.6 12.2 %collective-permute-start.11 = (bf16[4,256,128]{2,1,0:T(8,128)(2,1)S(1)}, bf16[4,256,128]{2,1,0:T(8,128)(2,1)S(1)}, u32[]{:S(2)}, u32[]{:S(2)}) collective-permute-start(bf16[4,256,128]{2,1,0:T(8,128)(2,1)S(1)} %team_joined.3.refs_2_.refs_4_), channel_id=1, source_target_pairs={{4,0},{5,1},{6,2},{7,3},{20,16},{21,17},{22,18},{23,19}} | collective-permute-start | bytes 786440 | tf_op jit(solution)/shard_map/ppermute | solution.py:373
  39.7 8.6 %collective-permute-start.19 = (bf16[2,256,128]{2,1,0:T(8,128)(2,1)S(1)}, bf16[2,256,128]{2,1,0:T(8,128)(2,1)S(1)}, u32[]{:S(2)}, u32[]{:S(2)}) collective-permute-start(bf16[2,256,128]{2,1,0:T(8,128)(2,1)S(1)} %get-tuple-element.36), channel_id=1, source_target_pairs={{0,2},{1,3},{2,0},{3,1},{4,6},{5,7},{6,4},{7,5},{8,10},{9,11},{10,... | collective-permute-start | bytes 393224 | tf_op jit(solution)/shard_map/ppermute | solution.py:369
  41.5 7.3 %collective-permute-start.16 = (bf16[2,256,128]{2,1,0:T(8,128)(2,1)S(1)}, bf16[2,256,128]{2,1,0:T(8,128)(2,1)S(1)}, u32[]{:S(2)}, u32[]{:S(2)}) collective-permute-start(bf16[2,256,128]{2,1,0:T(8,128)(2,1)S(1)} %get-tuple-element.34), channel_id=1, source_target_pairs={{0,2},{1,3},{2,0},{3,1},{4,6},{5,7},{6,4},{7,5},{8,10},{9,11},{10,... | collective-permute-start | bytes 393224 | tf_op jit(solution)/shard_map/ppermute | solution.py:369
  46.4 5.0 %collective-permute-start.23 = (bf16[2,256,128]{2,1,0:T(8,128)(2,1)S(1)}, bf16[2,256,128]{2,1,0:T(8,128)(2,1)S(1)}, u32[]{:S(2)}, u32[]{:S(2)}) collective-permute-start(bf16[2,256,128]{2,1,0:T(8,128)(2,1)S(1)} %get-tuple-element.39), channel_id=1, source_target_pairs={{0,2},{1,3},{2,0},{3,1},{4,6},{5,7},{6,4},{7,5},{8,10},{9,11},{10,... | collective-permute-start | bytes 393224 | tf_op jit(solution)/shard_map/ppermute | solution.py:369
  48.2 3.2 %collective-permute-start.18 = (bf16[2,256,128]{2,1,0:T(8,128)(2,1)S(1)}, bf16[2,256,128]{2,1,0:T(8,128)(2,1)S(1)}, u32[]{:S(2)}, u32[]{:S(2)}) collective-permute-start(bf16[2,256,128]{2,1,0:T(8,128)(2,1)S(1)} %get-tuple-element.35.refs_4_), channel_id=1, source_target_pairs={{0,1},{1,0},{2,3},{3,2},{4,5},{5,4},{6,7},{7,6},{8,9},{9,8},{10,11... | collective-permute-start | bytes 393224 | tf_op jit(solution)/shard_map/ppermute | solution.py:369
  48.2 3.7 %collective-permute-start.15 = (bf16[2,256,128]{2,1,0:T(8,128)(2,1)S(1)}, bf16[2,256,128]{2,1,0:T(8,128)(2,1)S(1)}, u32[]{:S(2)}, u32[]{:S(2)}) collective-permute-start(bf16[2,256,128]{2,1,0:T(8,128)(2,1)S(1)} %get-tuple-element.29.refs_0_), channel_id=1, source_target_pairs={{0,1},{1,0},{2,3},{3,2},{4,5},{5,4},{6,7},{7,6},{8,9},{9,8},{10,11... | collective-permute-start | bytes 393224 | tf_op jit(solution)/shard_map/ppermute | solution.py:369
  48.8 3.3 %collective-permute-start.20 = (bf16[2,256,128]{2,1,0:T(8,128)(2,1)S(1)}, bf16[2,256,128]{2,1,0:T(8,128)(2,1)S(1)}, u32[]{:S(2)}, u32[]{:S(2)}) collective-permute-start(bf16[2,256,128]{2,1,0:T(8,128)(2,1)S(1)} %collective-permute-done.19.refs_6_), channel_id=1, source_target_pairs={{0,1},{1,0},{2,3},{3,2},{4,5},{5,4},{6,7},{7,6},{8,9},{9,8},{10,11... | collective-permute-start | bytes 393224 | tf_op jit(solution)/shard_map/ppermute | solution.py:369
  48.8 5.0 %collective-permute-start.17 = (bf16[2,256,128]{2,1,0:T(8,128)(2,1)S(1)}, bf16[2,256,128]{2,1,0:T(8,128)(2,1)S(1)}, u32[]{:S(2)}, u32[]{:S(2)}) collective-permute-start(bf16[2,256,128]{2,1,0:T(8,128)(2,1)S(1)} %collective-permute-done.16.refs_2_), channel_id=1, source_target_pairs={{0,1},{1,0},{2,3},{3,2},{4,5},{5,4},{6,7},{7,6},{8,9},{9,8},{10,11... | collective-permute-start | bytes 393224 | tf_op jit(solution)/shard_map/ppermute | solution.py:369
  51.4 2.5 %collective-permute-start.22 = (bf16[2,256,128]{2,1,0:T(8,128)(2,1)S(1)}, bf16[2,256,128]{2,1,0:T(8,128)(2,1)S(1)}, u32[]{:S(2)}, u32[]{:S(2)}) collective-permute-start(bf16[2,256,128]{2,1,0:T(8,128)(2,1)S(1)} %get-tuple-element.38.refs_8_), channel_id=1, source_target_pairs={{0,1},{1,0},{2,3},{3,2},{4,5},{5,4},{6,7},{7,6},{8,9},{9,8},{10,11... | collective-permute-start | bytes 393224 | tf_op jit(solution)/shard_map/ppermute | solution.py:369
  51.4 2.5 %collective-permute-start.24 = (bf16[2,256,128]{2,1,0:T(8,128)(2,1)S(1)}, bf16[2,256,128]{2,1,0:T(8,128)(2,1)S(1)}, u32[]{:S(2)}, u32[]{:S(2)}) collective-permute-start(bf16[2,256,128]{2,1,0:T(8,128)(2,1)S(1)} %collective-permute-done.23.refs_10_), channel_id=1, source_target_pairs={{0,1},{1,0},{2,3},{3,2},{4,5},{5,4},{6,7},{7,6},{8,9},{9,8},{10,11... | collective-permute-start | bytes 393224 | tf_op jit(solution)/shard_map/ppermute | solution.py:369
  51.9 5.9 %collective-permute-start.12 = (bf16[2,256,128]{2,1,0:T(8,128)(2,1)S(1)}, bf16[2,256,128]{2,1,0:T(8,128)(2,1)S(1)}, u32[]{:S(2)}, u32[]{:S(2)}) collective-permute-start(bf16[2,256,128]{2,1,0:T(8,128)(2,1)S(1)} %get-tuple-element.31.refs_0_), channel_id=1, source_target_pairs={{0,1},{1,0},{2,3},{3,2},{4,5},{5,4},{6,7},{7,6},{8,9},{9,8},{10,11... | collective-permute-start | bytes 393224 | tf_op jit(solution)/shard_map/ppermute | solution.py:369
  52.0 4.5 %collective-permute-start.13 = (bf16[1,256,128]{2,1,0:T(8,128)(2,1)S(1)}, bf16[1,256,128]{2,1,0:T(8,128)(2,1)S(1)}, u32[]{:S(2)}, u32[]{:S(2)}) collective-permute-start(bf16[1,256,128]{2,1,0:T(8,128)(2,1)S(1)} %get-tuple-element.32), channel_id=1, source_target_pairs={{0,2},{1,3},{2,0},{3,1},{4,6},{5,7},{6,4},{7,5},{8,10},{9,11},{10,... | collective-permute-start | bytes 196616 | tf_op jit(solution)/shard_map/ppermute | solution.py:369
  53.8 4.1 %collective-permute-start.14 = (bf16[1,256,128]{2,1,0:T(8,128)(2,1)S(1)}, bf16[1,256,128]{2,1,0:T(8,128)(2,1)S(1)}, u32[]{:S(2)}, u32[]{:S(2)}) collective-permute-start(bf16[1,256,128]{2,1,0:T(8,128)(2,1)S(1)} %get-tuple-element.33), channel_id=1, source_target_pairs={{0,3},{1,2},{2,1},{3,0},{4,7},{5,6},{6,5},{7,4},{8,11},{9,10},{10,... | collective-permute-start | bytes 196616 | tf_op jit(solution)/shard_map/ppermute | solution.py:369
  (3 other events, 41.3 us)
